TPU v7x, 256 devices: a whole 4x4x8 slice. The times are simulated.
256 devices in a mesh: row: 32 (over y, z_lo, core), col: 8 (over z_hi, x).
Axes of the slice: x: 4, y: 4, z: 8 (z_hi: 2, z_lo: 4; z = z_hi * 4 + z_lo), core: 2. Of those that a mesh axis runs over, the one named last changes fastest.
Arguments:
- rhs: bfloat16 [2097152, 128], P(('row', 'col')), may hold values from -6 to 6
- leaf_basis: bfloat16 [16384, 64, 256], P(('row', 'col')), may hold values from -0.375 to 0.375
- transfer: bfloat16 [4, 32, 8, 64, 64, 256], P(None, 'row', 'col'), may hold values from -0.375 to 0.375
- ranks: int32 [4, 32, 8, 64], P(None, 'row', 'col'), may hold values from 32 to 64, as said below
- out_basis: bfloat16 [32, 64, 128, 128], P('row'), may hold values from -0.1875 to 0.1875
Outputs:
- result: bfloat16 [262144, 128], P(('row', 'col'))
Inputs may be any that keep to these rules, and one draw needn't show every extreme that they name: `ranks`: at every level some block has live rank exactly 64.
All inputs are finite; a program needn't handle non-finite values.
Results may differ from a plain program's by a relative error of at most 0.0014.
Values sent between devices are 32-bit elements; how exact they have to be, the bound alone decides.
No kernel may reach another device: no remote copies, remote signals or barrier semaphores. Data moves between devices by JAX's collectives and lax.ppermute only.
A program may use at most 128 MiB of HBM per device.

v0:
```python
import jax
import jax.numpy as jnp
from jax import lax
from jax.sharding import PartitionSpec as P


def from_partner(block, axis, bit):
    count = lax.axis_size(axis)
    route = []
    for low in range(count):
        high = low | 1 << bit
        if high != low and high < count:
            route += [(low, high), (high, low)]
    return lax.ppermute(block, axis, route)


def complex_stack(block):
    middle = block.shape[-1] // 2
    flipped = jnp.concatenate([-block[..., middle:], block[..., :middle]], -1)
    return jnp.concatenate([block, flipped], -2)


def mix_level(coeff, matrices, live_ranks, level, position):
    leaves = coeff.shape[0]
    rank_cap = coeff.shape[1]
    columns = coeff.shape[2]
    half_count = leaves // 2
    upper_bit = position >> level & 1
    kept_half = lax.dynamic_slice_in_dim(coeff, upper_bit * half_count, half_count, 0)
    sent_half = lax.dynamic_slice_in_dim(coeff, (1 - upper_bit) * half_count, half_count, 0)
    partner_half = from_partner(sent_half, "row", level)
    stacked = jnp.concatenate([complex_stack(kept_half), complex_stack(partner_half)], 1)
    weights = matrices.astype(jnp.float32).reshape(half_count, 2, rank_cap, 4 * rank_cap)
    mixed = jnp.einsum("jskm,jmn->jskn", weights, stacked, precision=lax.Precision.HIGHEST)
    mixed = mixed.reshape(leaves, rank_cap, columns)
    live_rows = jnp.arange(rank_cap, dtype=jnp.int32)[None, :] < live_ranks[:, None]
    return jnp.where(live_rows[..., None], mixed, jnp.float32(0.0))


def shards(rhs, leaf_basis, transfer, ranks, out_basis):
    leaves = leaf_basis.shape[0]
    points = leaf_basis.shape[2] // 2
    columns = rhs.shape[1]
    sources = rhs.reshape(leaves, points, columns)
    coeff = jnp.einsum(
        "gkm,gmn->gkn", leaf_basis, complex_stack(sources), preferred_element_type=jnp.float32
    )
    position = lax.axis_index("row")
    for level in range(transfer.shape[0]):
        coeff = mix_level(coeff, transfer[level, 0, 0], ranks[level, 0, 0], level, position)
    owned = leaves // lax.axis_size("col")
    targets = out_basis[0]
    total = lax.psum_scatter(coeff, "col", scatter_dimension=0, tiled=True)
    basis = lax.dynamic_slice_in_dim(targets, lax.axis_index("col") * owned, owned, 0).astype(
        jnp.float32
    )
    product = jnp.einsum(
        "glm,gmn->gln", basis, complex_stack(total), precision=lax.Precision.HIGHEST
    )
    result = product.reshape(owned * points, columns)
    return result.astype(jnp.bfloat16)


def solution(mesh):
    in_specs = (
        P(("row", "col"), None),
        P(("row", "col"), None, None),
        P(None, "row", "col", None, None, None),
        P(None, "row", "col", None),
        P("row", None, None, None),
    )
    out_specs = P(("row", "col"), None)
    return jax.shard_map(shards, mesh=mesh, in_specs=in_specs, out_specs=out_specs, check_vma=False)
```

profile of v0, /device:TPU:8, one launch (start us, length us, event | category | flops | bytes accessed | tf_op | source)
XLA Modules:
  0.0 260.4 jit_solution(10908517239477554836)
XLA Ops:
  6.5 5.2 %slice_negate_fusion = (bf16[64,128,64]{2,1,0:T(8,128)(2,1)}, bf16[64,128,64]{2,1,0:T(8,128)(2,1)}) fusion(bf16[64,128,128]{2,1,0:T(8,128)(2,1)} %bitcast.62), kind=kLoop, calls=%fused_computation.54 | loop fusion | flops 524288 | bytes 4194304 | tf_op jit(solution)/shard_map/neg | solution.py:19
  11.7 3.9 %fusion = f32[64,128,64]{1,2,0:T(8,128)S(1)} fusion(bf16[64,64,256]{2,1,0:T(8,128)(2,1)S(1)} %copy-done, bf16[64,128,64]{2,1,0:T(8,128)(2,1)} %get-tuple-element.24, bf16[64,128,64]{2,1,0:T(8,128)(2,1)} %get-tuple-element.23, bf16[64,128,128]{2,1,0:T(8,128)(2,1)} %bitcast.63), kind=kOutput, calls=%fused_computation | convolution fusion | flops 281018368 | bytes 8388608 | tf_op jit(solution)/shard_map/gkm,gmn->gkn/dot_general | solution.py:45
  16.7 5.6 %fusion.64 = (bf16[1,1,1,64,64,256]{5,4,3,2,1,0:T(8,128)(2,1)S(1)}, bf16[1,1,1,64,64,256]{5,4,3,2,1,0:T(8,128)(2,1)}, bf16[1,1,1,64,64,256]{5,4,3,2,1,0:T(8,128)(2,1)}, bf16[1,1,1,64,64,256]{5,4,3,2,1,0:T(8,128)(2,1)}) fusion(bf16[4,1,1,64,64,256]{5,4,3,2,1,0:T(8,128)(2,1)} %param.7), kind=kLoop, calls=%fused_computation.102 | loop fusion | bytes 16777216 | tf_op jit(solution)/shard_map/slice | solution.py:50
  22.4 1.3 slice_negate_fusion.4
  23.7 4.6 %fusion.6 = f32[32,128,2,64]{1,3,2,0:T(8,128)S(1)} fusion(bf16[32,2,64,256]{3,2,1,0:T(8,128)(2,1)S(1)} %bitcast.67, f32[32,64,64]{2,1,0:T(8,128)} %get-tuple-element.34, f32[32,64,64]{2,1,0:T(8,128)S(1)} %get-tuple-element.33, f32[32,64,128]{2,1,0:T(8,128)S(1)} %collective-permute-done, f32[32,64,64]{2,1,0:T(8,128)S(1)} %get-tuple-element.32, ...), kind=kOutput, calls=%fused_computation.7 | convolution fusion | flops 1615855616 | bytes 8388608 | tf_op jit(solution)/shard_map/jskm,jmn->jskn/dot_general | solution.py:34
  28.3 0.9 bitcast_select_fusion.3
  29.2 1.7 constant_dynamic-slice_fusion.8
  30.8 1.9 collective-permute-start.1
  33.2 23.2 %collective-permute-done.1 = f32[32,64,128]{2,1,0:T(8,128)S(1)} collective-permute-done((f32[32,64,128]{2,1,0:T(8,128)}, f32[32,64,128]{2,1,0:T(8,128)S(1)}, u32[]{:S(2)}, u32[]{:S(2)}) %collective-permute-start.1) | collective-permute-done | bytes 1048608 | tf_op jit(solution)/shard_map/ppermute | solution.py:14
  56.4 1.5 slice_negate_fusion.3
  57.9 4.5 %fusion.17 = f32[32,128,2,64]{1,3,2,0:T(8,128)S(1)} fusion(bf16[32,2,64,256]{3,2,1,0:T(8,128)(2,1)S(1)} %bitcast.66, f32[32,64,64]{2,1,0:T(8,128)} %get-tuple-element.30, f32[32,64,64]{2,1,0:T(8,128)S(1)} %get-tuple-element.29, f32[32,64,128]{2,1,0:T(8,128)S(1)} %collective-permute-done.1, f32[32,64,64]{2,1,0:T(8,128)S(1)} %get-tuple-element.20, ...), kind=kOutput, calls=%fused_computation.19 | convolution fusion | flops 1615855616 | bytes 8388608 | tf_op jit(solution)/shard_map/jskm,jmn->jskn/dot_general | solution.py:34
  63.3 1.6 constant_dynamic-slice_fusion.6
  64.9 3.3 %collective-permute-start.2 = (f32[32,64,128]{2,1,0:T(8,128)}, f32[32,64,128]{2,1,0:T(8,128)S(1)}, u32[]{:S(2)}, u32[]{:S(2)}) collective-permute-start(f32[32,64,128]{2,1,0:T(8,128)} %get-tuple-element.14), channel_id=1, source_target_pairs={{0,32},{32,0},{8,40},{40,8},{16,48},{48,16},{24,56},{56,24},{64,96... | collective-permute-start | bytes 3145736 | tf_op jit(solution)/shard_map/ppermute | solution.py:14
  68.7 45.0 %collective-permute-done.2 = f32[32,64,128]{2,1,0:T(8,128)S(1)} collective-permute-done((f32[32,64,128]{2,1,0:T(8,128)}, f32[32,64,128]{2,1,0:T(8,128)S(1)}, u32[]{:S(2)}, u32[]{:S(2)}) %collective-permute-start.2) | collective-permute-done | bytes 1048608 | tf_op jit(solution)/shard_map/ppermute | solution.py:14
  113.7 1.4 slice_negate_fusion.2
  115.1 4.5 %fusion.28 = f32[32,128,2,64]{1,3,2,0:T(8,128)S(1)} fusion(bf16[32,2,64,256]{3,2,1,0:T(8,128)(2,1)S(1)} %bitcast.65, f32[32,64,64]{2,1,0:T(8,128)} %get-tuple-element.28, f32[32,64,64]{2,1,0:T(8,128)S(1)} %get-tuple-element.27, f32[32,64,128]{2,1,0:T(8,128)S(1)} %collective-permute-done.2, f32[32,64,64]{2,1,0:T(8,128)S(1)} %get-tuple-element.16, ...), kind=kOutput, calls=%fused_computation.31 | convolution fusion | flops 1615855616 | bytes 8388608 | tf_op jit(solution)/shard_map/jskm,jmn->jskn/dot_general | solution.py:34
  120.7 1.3 collective-permute-start.3
  122.4 22.6 %collective-permute-done.3 = f32[32,64,128]{2,1,0:T(8,128)S(1)} collective-permute-done((f32[32,64,128]{2,1,0:T(8,128)S(1)}, f32[32,64,128]{2,1,0:T(8,128)S(1)}, u32[]{:S(2)}, u32[]{:S(2)}) %collective-permute-start.3) | collective-permute-done | bytes 1048608 | tf_op jit(solution)/shard_map/ppermute | solution.py:14
  145.1 1.4 slice_negate_fusion.1
  146.5 4.4 %fusion.39 = f32[32,128,2,64]{1,3,2,0:T(8,128)S(1)} fusion(bf16[32,2,64,256]{3,2,1,0:T(8,128)(2,1)S(1)} %bitcast.64, f32[32,64,64]{2,1,0:T(8,128)} %get-tuple-element.26, f32[32,64,64]{2,1,0:T(8,128)S(1)} %get-tuple-element.25, f32[32,64,128]{2,1,0:T(8,128)S(1)} %collective-permute-done.3, f32[32,64,64]{2,1,0:T(8,128)S(1)} %get-tuple-element.12, ...), kind=kOutput, calls=%fused_computation.43 | convolution fusion | flops 1615855616 | bytes 8388608 | tf_op jit(solution)/shard_map/jskm,jmn->jskn/dot_general | solution.py:34
  150.9 1.9 bitcast_select_fusion
  152.7 97.4 %reduce-scatter.2.cloned.1.call-done = f32[8,64,128]{2,1,0:T(8,128)} async-done(((f32[64,64,128]{2,1,0:T(8,128)}), f32[8,64,128]{2,1,0:T(8,128)}) %reduce-scatter.2.cloned.1.call-update) | async-done | bytes 262160 | tf_op jit(solution)/shard_map/reduce_scatter | solution.py:53
  250.2 1.2 slice_negate_fusion.6
  251.3 2.2 convolution_convert_fusion
  (33 shorter events, 4.5 us)
Async XLA Ops:
  6.5 5.2 %copy-start = (bf16[64,64,256]{2,1,0:T(8,128)(2,1)S(1)}, bf16[64,64,256]{2,1,0:T(8,128)(2,1)}, u32[]{:S(2)}) copy-start(bf16[64,64,256]{2,1,0:T(8,128)(2,1)} %param.6) | copy-start | bytes 6291460
  6.5 243.6 %reduce-scatter.2.cloned.1.call-start = ((), (), s32[]{:S(2)}) async-start(), calls=%async_computation.1 | async-start | bytes 2359296 | tf_op jit(solution)/shard_map/reduce_scatter | solution.py:53
  15.6 0.7 copy-start.7
  15.8 6.6 %collective-permute-start = (f32[32,64,128]{2,1,0:T(8,128)S(1)}, f32[32,64,128]{2,1,0:T(8,128)S(1)}, u32[]{:S(2)}, u32[]{:S(2)}) collective-permute-start(f32[32,64,128]{2,1,0:T(8,128)S(1)} %get-tuple-element.22), channel_id=1, source_target_pairs={{0,8},{8,0},{16,24},{24,16},{32,40},{40,32},{48,56},{56,48},{64,72... | collective-permute-start | bytes 3145736 | tf_op jit(solution)/shard_map/ppermute | solution.py:14
  30.8 25.6 %collective-permute-start.1 = (f32[32,64,128]{2,1,0:T(8,128)}, f32[32,64,128]{2,1,0:T(8,128)S(1)}, u32[]{:S(2)}, u32[]{:S(2)}) collective-permute-start(f32[32,64,128]{2,1,0:T(8,128)} %get-tuple-element.18), channel_id=1, source_target_pairs={{0,16},{16,0},{8,24},{24,8},{32,48},{48,32},{40,56},{56,40},{64,80... | collective-permute-start | bytes 3145736 | tf_op jit(solution)/shard_map/ppermute | solution.py:14
  33.2 24.7 %copy-start.4 = (bf16[1,1,1,64,64,256]{5,4,3,2,1,0:T(8,128)(2,1)S(1)}, bf16[1,1,1,64,64,256]{5,4,3,2,1,0:T(8,128)(2,1)}, u32[]{:S(2)}) copy-start(bf16[1,1,1,64,64,256]{5,4,3,2,1,0:T(8,128)(2,1)} %get-tuple-element.6) | copy-start | bytes 6291460
  33.2 24.6 %copy-start.6 = (f32[32,64,128]{2,1,0:T(8,128)S(1)}, f32[32,64,128]{2,1,0:T(8,128)}, u32[]{:S(2)}) copy-start(f32[32,64,128]{2,1,0:T(8,128)} %get-tuple-element.17) | copy-start | bytes 3145732
  64.9 48.8 %collective-permute-start.2 = (f32[32,64,128]{2,1,0:T(8,128)}, f32[32,64,128]{2,1,0:T(8,128)S(1)}, u32[]{:S(2)}, u32[]{:S(2)}) collective-permute-start(f32[32,64,128]{2,1,0:T(8,128)} %get-tuple-element.14), channel_id=1, source_target_pairs={{0,32},{32,0},{8,40},{40,8},{16,48},{48,16},{24,56},{56,24},{64,96... | collective-permute-start | bytes 3145736 | tf_op jit(solution)/shard_map/ppermute | solution.py:14
  68.7 46.4 %copy-start.3 = (bf16[1,1,1,64,64,256]{5,4,3,2,1,0:T(8,128)(2,1)S(1)}, bf16[1,1,1,64,64,256]{5,4,3,2,1,0:T(8,128)(2,1)}, u32[]{:S(2)}) copy-start(bf16[1,1,1,64,64,256]{5,4,3,2,1,0:T(8,128)(2,1)} %get-tuple-element.8) | copy-start | bytes 6291460
  68.7 46.4 %copy-start.5 = (f32[32,64,128]{2,1,0:T(8,128)S(1)}, f32[32,64,128]{2,1,0:T(8,128)}, u32[]{:S(2)}) copy-start(f32[32,64,128]{2,1,0:T(8,128)} %get-tuple-element.13) | copy-start | bytes 3145732
  120.7 24.4 %collective-permute-start.3 = (f32[32,64,128]{2,1,0:T(8,128)S(1)}, f32[32,64,128]{2,1,0:T(8,128)S(1)}, u32[]{:S(2)}, u32[]{:S(2)}) collective-permute-start(f32[32,64,128]{2,1,0:T(8,128)S(1)} %get-tuple-element.10), channel_id=1, source_target_pairs={{0,64},{64,0},{8,72},{72,8},{16,80},{80,16},{24,88},{88,24},{32,96... | collective-permute-start | bytes 3145736 | tf_op jit(solution)/shard_map/ppermute | solution.py:14
  122.4 24.0 %copy-start.2 = (bf16[1,1,1,64,64,256]{5,4,3,2,1,0:T(8,128)(2,1)S(1)}, bf16[1,1,1,64,64,256]{5,4,3,2,1,0:T(8,128)(2,1)}, u32[]{:S(2)}) copy-start(bf16[1,1,1,64,64,256]{5,4,3,2,1,0:T(8,128)(2,1)} %get-tuple-element.7) | copy-start | bytes 6291460
  152.7 100.8 %copy-start.1 = (bf16[64,64,256]{2,1,0:T(8,128)(2,1)S(1)}, bf16[64,64,256]{2,1,0:T(8,128)(2,1)}, u32[]{:S(2)}) copy-start(bf16[64,64,256]{2,1,0:T(8,128)(2,1)} %param.6) | copy-start | bytes 6291460
Sparse Core Ops, SparseCore 0:
  152.9 97.2 reduce-scatter.1
where the time goes:
time: 261 us; the launch traced here: 260 us
  waiting for transfers between devices  188 us (72%)
  matrix products  24.1 us (9%)
  other arithmetic  18.2 us (7%)
  between operations  13.6 us (5%)
  local copies, waits for them, and re-layouts  9.72 us (4%)
  starting transfers between devices  6.56 us (3%)
    reduce_scatter x1, waiting for transfers between devices, shards(): total = lax.psum_scatter(coeff, 'col', scatter_dimension=0, tiled=True)  97.4 us
    ppermute x4, waiting for transfers between devices, from_partner(): return lax.ppermute(block, axis, route)  90.8 us
    dot_general x4, matrix products, mix_level(): jnp.einsum('jskm,jmn->jskn', weights, stacked, precision=lax.Precision.HI...  18.1 us
    neg x10, other arithmetic, complex_stack(): flipped = jnp.concatenate([-block[..., middle:], block[..., :middle]], -1)  13.4 us
    ppermute x4, starting transfers between devices, from_partner(): return lax.ppermute(block, axis, route)  6.56 us
    slice x1, local copies, waits for them, and re-layouts, shards(): transfer[level, 0, 0]  5.65 us
  transfers between devices with their start and end apart: 5, of which 4 were waited for; matrix products, arithmetic and copies ran while one was open for 3% of the time, Pallas kernels for 0%

commit v1 on v0

v1 whole, which is shorter than its diff:
```python
import functools

import jax
import jax.numpy as jnp
from jax import lax
from jax.experimental import pallas as pl
from jax.experimental.pallas import tpu as pltpu
from jax.sharding import PartitionSpec as P

SLOTS = 4


def swap(block, axis, mask):
    count = lax.axis_size(axis)
    return lax.ppermute(block, axis, [(at, at ^ mask) for at in range(count)])


def turn(block):
    middle = block.shape[-1] // 2
    return jnp.concatenate([-block[:, middle:], block[:, :middle]], -1)


def split(block):
    high = block.astype(jnp.bfloat16)
    low = (block - high.astype(jnp.float32)).astype(jnp.bfloat16)
    return high, low


def stack_split(blocks):
    highs, lows = [], []
    for block in blocks:
        high, low = split(block)
        highs += [high, turn(high)]
        lows += [low, turn(low)]
    return jnp.concatenate([jnp.concatenate(highs, 0), jnp.concatenate(lows, 0)], 1)


def leaf_kernel(scalars, rhs_ref, basis_ref, sent_ref, kept_ref, *, bit_at):
    half = sent_ref.shape[0]
    bit = scalars[bit_at]
    for out_ref, start in ((sent_ref, (1 - bit) * half), (kept_ref, bit * half)):
        for at in range(half):
            source = rhs_ref[start + at, 0]
            stacked = jnp.concatenate([source, turn(source)], 0)
            out_ref[at] = jnp.dot(
                basis_ref[start + at, 0], stacked, preferred_element_type=jnp.float32
            )


def level_kernel(scalars, ranks, own_ref, partner_ref, matrices_ref, *refs, level, slot, bit_at, leaves):
    sent_ref, kept_ref = refs[-2:]
    added = refs[:-2]
    half = sent_ref.shape[0]
    rank_cap, columns = sent_ref.shape[1:]
    low_count = matrices_ref.shape[3]
    chunk = scalars[slot]
    bit = scalars[bit_at]
    rows = lax.broadcasted_iota(jnp.int32, (rank_cap, columns), 0)
    for which, (out_ref, start) in enumerate(((sent_ref, (1 - bit) * half), (kept_ref, bit * half))):
        for pair in range(half // 2):
            j = start // 2 + pair
            stacked = stack_split([own_ref[j], partner_ref[j]])
            places, parts = [], []
            for s in range(2):
                local = start + 2 * pair + s
                high, low = local // low_count, local % low_count
                places.append(high * (SLOTS * low_count) + chunk * low_count + low)
                parts.append(matrices_ref[0, high, 0, low])
            both = jnp.dot(jnp.concatenate(parts, 0), stacked, preferred_element_type=jnp.float32)
            both = both[:, :columns] + both[:, columns:]
            for s in range(2):
                live = ranks[level * leaves + places[s]]
                mixed = jnp.where(rows < live, both[s * rank_cap : (s + 1) * rank_cap], 0.0)
                if added:
                    mixed = mixed + added[which][2 * pair + s]
                out_ref[2 * pair + s] = mixed


def target_kernel(scalars, basis_ref, first_ref, second_ref, third_ref, out_ref):
    points = basis_ref.shape[2]
    columns = out_ref.shape[1]
    for at in range(first_ref.shape[0]):
        total = first_ref[at] + second_ref[at] + third_ref[at]
        both = jnp.dot(basis_ref[0, at], stack_split([total]), preferred_element_type=jnp.float32)
        out_ref[at * points : (at + 1) * points, :] = (
            both[:, :columns] + both[:, columns:]
        ).astype(out_ref.dtype)


def whole(shape):
    return pl.BlockSpec(shape, lambda step, *_: (0,) * len(shape))


def call(body, prefetch, in_specs, outs, flops, moved):
    return pl.pallas_call(
        body,
        grid_spec=pltpu.PrefetchScalarGridSpec(
            num_scalar_prefetch=prefetch,
            grid=(1,),
            in_specs=in_specs,
            out_specs=[whole(out.shape) for out in outs],
        ),
        out_shape=outs,
        cost_estimate=pl.CostEstimate(flops=flops, bytes_accessed=moved, transcendentals=0),
        compiler_params=pltpu.CompilerParams(vmem_limit_bytes=16 * 1024 * 1024),
    )


def shards(rhs, leaf_basis, transfer, ranks, out_basis):
    leaves, rank_cap, wide = leaf_basis.shape
    points = wide // 2
    columns = rhs.shape[1]
    levels = transfer.shape[0]
    chunk_leaves = leaves // SLOTS
    half = chunk_leaves // 2
    position = lax.axis_index("row")
    column = lax.axis_index("col")
    column_count = lax.axis_size("col")
    owned = leaves // column_count
    scalars = jnp.stack(
        [(column >> 1) ^ (SLOTS - 1 - slot) for slot in range(SLOTS)]
        + [position >> level & 1 for level in range(levels)]
        + [column & 1, column]
    ).astype(jnp.int32)
    flat_ranks = ranks.reshape(levels * leaves)
    sources = rhs.reshape(chunk_leaves, SLOTS, points, columns)
    bases = leaf_basis.reshape(chunk_leaves, SLOTS, rank_cap, wide)
    half_out = jax.ShapeDtypeStruct((half, rank_cap, columns), jnp.float32)
    half_spec = whole(half_out.shape)

    def leaf(slot):
        at_slot = lambda step, scalars: (0, scalars[slot], 0, 0)
        return call(
            functools.partial(leaf_kernel, bit_at=SLOTS),
            1,
            [
                pl.BlockSpec((chunk_leaves, 1, points, columns), at_slot),
                pl.BlockSpec((chunk_leaves, 1, rank_cap, wide), at_slot),
            ],
            [half_out, half_out],
            2 * chunk_leaves * rank_cap * wide * columns,
            3 << 19,
        )(scalars, sources, bases)

    def mix(level, slot, kept, partner, added=()):
        low_count = 2 << level
        high_count = chunk_leaves // low_count
        matrices = transfer.reshape(levels, high_count, SLOTS, low_count, rank_cap, 4 * rank_cap)
        return call(
            functools.partial(
                level_kernel, level=level, slot=slot, bit_at=SLOTS + level + 1, leaves=leaves
            ),
            2,
            [
                half_spec,
                half_spec,
                pl.BlockSpec(
                    (1, high_count, 1, low_count, rank_cap, 4 * rank_cap),
                    lambda step, scalars, ranks: (level, 0, scalars[slot], 0, 0, 0),
                ),
            ]
            + [half_spec] * len(added),
            [half_out, half_out],
            4 * chunk_leaves * rank_cap * 4 * rank_cap * columns,
            3 << 19,
        )(scalars, flat_ranks, kept, partner, matrices, *added)

    def through(slot, added=()):
        sent, kept = leaf(slot)
        for level in range(levels):
            partner = swap(sent, "row", 1 << level)
            sent, kept = mix(level, slot, kept, partner, added if level == levels - 1 else ())
        return sent, kept

    summed = []
    for first in (0, 2):
        sent, kept = through(first)
        added = (swap(kept, "col", 3), swap(sent, "col", 3))
        sent, kept = through(first + 1, added)
        summed.append((kept, swap(sent, "col", 1)))
    far = swap(summed[0][0] + summed[0][1], "col", 4)

    result = call(
        target_kernel,
        1,
        [pl.BlockSpec((1, owned, points, 2 * rank_cap), lambda step, scalars: (0, scalars[SLOTS + levels + 1], 0, 0))]
        + [half_spec] * 3,
        [jax.ShapeDtypeStruct((owned * points, columns), jnp.bfloat16)],
        4 * owned * points * 2 * rank_cap * columns,
        3 << 19,
    )(scalars, out_basis, summed[1][0], summed[1][1], far)
    return result[0]


def solution(mesh):
    in_specs = (
        P(("row", "col"), None),
        P(("row", "col"), None, None),
        P(None, "row", "col", None, None, None),
        P(None, "row", "col", None),
        P("row", None, None, None),
    )
    out_specs = P(("row", "col"), None)
    return jax.shard_map(shards, mesh=mesh, in_specs=in_specs, out_specs=out_specs, check_vma=False)
```

time: 261 us -> 119 us (0.46)
  waiting for transfers between devices: 188 us -> 48.9 us
  starting transfers between devices: 6.56 us -> 32.6 us
  Pallas kernels: 0 us -> 24.2 us
  matrix products: 24.1 us -> 0 us
  other arithmetic: 18.2 us -> 0.7 us
  between operations: 13.6 us -> 0.25 us
    reduce_scatter x1 -> x0, waiting for transfers between devices: 97.4 us -> none  [shards(): total = lax.psum_scatter(coeff, 'col', scatter_dimension=0, tiled=True)]
    ppermute x4 -> x23, waiting for transfers between devices: 90.8 us -> 48.9 us  [swap(): return lax.ppermute(block, axis, [(at, at ^ mask) for at in range(count)])]
    ppermute x4 -> x23, starting transfers between devices: 6.56 us -> 32.6 us  [swap(): return lax.ppermute(block, axis, [(at, at ^ mask) for at in range(count)])]
    pallas_call x0 -> x21, Pallas kernels: none -> 24.2 us  [the longest x16 18.1 us: mix(): call(functools.partial(level_kernel, level=level, slot=slot, bit_at=SLOTS...]
    dot_general x6 -> x0, matrix products: 24.1 us -> none  [the longest x4 18.1 us: mix_level(): jnp.einsum('jskm,jmn->jskn', weights, stacked, precision=lax.Precision.HI...]
    neg x10 -> x0, other arithmetic: 13.4 us -> none  [complex_stack(): flipped = jnp.concatenate([-block[..., middle:], block[..., :middle]], -1)]
    unnamed x16 -> x21, local copies, waits for them, and re-layouts: 0.4 us -> 10.5 us
    slice x1 -> x0, local copies, waits for them, and re-layouts: 5.65 us -> none  [shards(): transfer[level, 0, 0]]
  transfers between devices with their start and end apart: 5 -> 23, of which waited for: 4 -> 9; matrix products, arithmetic and copies ran while one was open for 3% -> 1% of each run, Pallas kernels for 0% -> 18%
where the time goes in v1:
time: 119 us; the launch traced here: 117 us
  waiting for transfers between devices  48.9 us (41%)
  starting transfers between devices  32.6 us (27%)
  Pallas kernels  24.2 us (20%)
  local copies, waits for them, and re-layouts  10.7 us (9%)
    ppermute x23, waiting for transfers between devices, swap(): return lax.ppermute(block, axis, [(at, at ^ mask) for at in range(count)])  48.9 us
    ppermute x23, starting transfers between devices, swap(): return lax.ppermute(block, axis, [(at, at ^ mask) for at in range(count)])  32.6 us
    pallas_call x16, Pallas kernels, mix(): call(functools.partial(level_kernel, level=level, slot=slot, bit_at=SLOTS...  18.1 us
    unnamed x21, local copies, waits for them, and re-layouts  10.5 us
    pallas_call x4, Pallas kernels, leaf(): call(functools.partial(leaf_kernel, bit_at=SLOTS), 1, [pl.BlockSpec((chun...  4.52 us
  transfers between devices with their start and end apart: 23, of which 9 were waited for; matrix products, arithmetic and copies ran while one was open for 1% of the time, Pallas kernels for 18%

profile of v1, /device:TPU:8, one launch (start us, length us, event | category | flops | bytes accessed | tf_op | source)
XLA Modules:
  0.0 117.4 jit_solution(3233660787070548539)
XLA Ops:
  0.1 1.6 %copy-done.2 = bf16[8192,128]{1,0:T(8,128)(2,1)S(1)} copy-done((bf16[8192,128]{1,0:T(8,128)(2,1)S(1)}, bf16[8192,128]{1,0:T(8,128)(2,1)}, u32[]{:S(2)}) %copy-start.2) | copy-done | bytes 2097176
  1.7 1.6 %copy-done.4 = bf16[64,64,256]{2,1,0:T(8,128)(2,1)S(1)} copy-done((bf16[64,64,256]{2,1,0:T(8,128)(2,1)S(1)}, bf16[64,64,256]{2,1,0:T(8,128)(2,1)}, u32[]{:S(2)}) %copy-start.4) | copy-done | bytes 2097176
  8.8 3.4 %copy-done = bf16[4,1,1,64,64,256]{5,4,3,2,1,0:T(8,128)(2,1)S(1)} copy-done((bf16[4,1,1,64,64,256]{5,4,3,2,1,0:T(8,128)(2,1)S(1)}, bf16[4,1,1,64,64,256]{5,4,3,2,1,0:T(8,128)(2,1)}, u32[]{:S(2)}) %copy-start) | copy-done | bytes 8388632
  13.3 2.0 %collective-permute-start.16 = (f32[8,64,128]{2,1,0:T(8,128)S(1)}, f32[8,64,128]{2,1,0:T(8,128)S(1)}, u32[]{:S(2)}, u32[]{:S(2)}) collective-permute-start(f32[8,64,128]{2,1,0:T(8,128)S(1)} %get-tuple-element.76), channel_id=1, source_target_pairs={{0,16},{8,24},{16,0},{24,8},{32,48},{40,56},{48,32},{56,40},{64,80... | collective-permute-start | bytes 786440 | tf_op jit(solution)/shard_map/ppermute | solution.py:15
  16.7 3.4 %copy-done.1 = bf16[4,1,1,64,64,256]{5,4,3,2,1,0:T(8,128)(2,1)S(1)} copy-done((bf16[4,1,1,64,64,256]{5,4,3,2,1,0:T(8,128)(2,1)S(1)}, bf16[4,1,1,64,64,256]{5,4,3,2,1,0:T(8,128)(2,1)}, u32[]{:S(2)}) %copy-start.1) | copy-done | bytes 8388632
  21.2 1.4 %collective-permute-start.5 = (f32[8,64,128]{2,1,0:T(8,128)S(1)}, f32[8,64,128]{2,1,0:T(8,128)S(1)}, u32[]{:S(2)}, u32[]{:S(2)}) collective-permute-start(f32[8,64,128]{2,1,0:T(8,128)S(1)} %get-tuple-element.56), channel_id=1, source_target_pairs={{0,16},{8,24},{16,0},{24,8},{32,48},{40,56},{48,32},{56,40},{64,80... | collective-permute-start | bytes 786440 | tf_op jit(solution)/shard_map/ppermute | solution.py:15
  25.7 3.4 %collective-permute-start.17 = (f32[8,64,128]{2,1,0:T(8,128)S(1)}, f32[8,64,128]{2,1,0:T(8,128)S(1)}, u32[]{:S(2)}, u32[]{:S(2)}) collective-permute-start(f32[8,64,128]{2,1,0:T(8,128)S(1)} %get-tuple-element.78), channel_id=1, source_target_pairs={{0,32},{8,40},{16,48},{24,56},{32,0},{40,8},{48,16},{56,24},{64,96... | collective-permute-start | bytes 786440 | tf_op jit(solution)/shard_map/ppermute | solution.py:15
  30.3 1.4 %collective-permute-start.1 = (f32[8,64,128]{2,1,0:T(8,128)S(1)}, f32[8,64,128]{2,1,0:T(8,128)S(1)}, u32[]{:S(2)}, u32[]{:S(2)}) collective-permute-start(f32[8,64,128]{2,1,0:T(8,128)S(1)} %get-tuple-element.48), channel_id=1, source_target_pairs={{0,16},{8,24},{16,0},{24,8},{32,48},{40,56},{48,32},{56,40},{64,80... | collective-permute-start | bytes 786440 | tf_op jit(solution)/shard_map/ppermute | solution.py:15
  31.6 7.3 %collective-permute-done.5.partner_ref = f32[8,64,128]{2,1,0:T(8,128)S(1)} collective-permute-done((f32[8,64,128]{2,1,0:T(8,128)S(1)}, f32[8,64,128]{2,1,0:T(8,128)S(1)}, u32[]{:S(2)}, u32[]{:S(2)}) %collective-permute-start.5) | collective-permute-done | bytes 262176 | tf_op jit(solution)/shard_map/ppermute | solution.py:15
  40.1 4.4 %collective-permute-done.12.partner_ref = f32[8,64,128]{2,1,0:T(8,128)S(1)} collective-permute-done((f32[8,64,128]{2,1,0:T(8,128)S(1)}, f32[8,64,128]{2,1,0:T(8,128)S(1)}, u32[]{:S(2)}, u32[]{:S(2)}) %collective-permute-start.12) | collective-permute-done | bytes 262176 | tf_op jit(solution)/shard_map/ppermute | solution.py:15
  45.7 4.9 %collective-permute-start.13 = (f32[8,64,128]{2,1,0:T(8,128)S(1)}, f32[8,64,128]{2,1,0:T(8,128)S(1)}, u32[]{:S(2)}, u32[]{:S(2)}) collective-permute-start(f32[8,64,128]{2,1,0:T(8,128)S(1)} %get-tuple-element.70), channel_id=1, source_target_pairs={{0,32},{8,40},{16,48},{24,56},{32,0},{40,8},{48,16},{56,24},{64,96... | collective-permute-start | bytes 786440 | tf_op jit(solution)/shard_map/ppermute | solution.py:15
  51.8 1.4 %collective-permute-start.18 = (f32[8,64,128]{2,1,0:T(8,128)S(1)}, f32[8,64,128]{2,1,0:T(8,128)S(1)}, u32[]{:S(2)}, u32[]{:S(2)}) collective-permute-start(f32[8,64,128]{2,1,0:T(8,128)S(1)} %get-tuple-element.80), channel_id=1, source_target_pairs={{0,64},{8,72},{16,80},{24,88},{32,96},{40,104},{48,112},{56,120},{... | collective-permute-start | bytes 786440 | tf_op jit(solution)/shard_map/ppermute | solution.py:15
  56.4 1.2 %collective-permute-start.7 = (f32[8,64,128]{2,1,0:T(8,128)S(1)}, f32[8,64,128]{2,1,0:T(8,128)S(1)}, u32[]{:S(2)}, u32[]{:S(2)}) collective-permute-start(f32[8,64,128]{2,1,0:T(8,128)S(1)} %get-tuple-element.60), channel_id=1, source_target_pairs={{0,64},{8,72},{16,80},{24,88},{32,96},{40,104},{48,112},{56,120},{... | collective-permute-start | bytes 786440 | tf_op jit(solution)/shard_map/ppermute | solution.py:15
  57.6 14.4 %collective-permute-done.13.partner_ref = f32[8,64,128]{2,1,0:T(8,128)S(1)} collective-permute-done((f32[8,64,128]{2,1,0:T(8,128)S(1)}, f32[8,64,128]{2,1,0:T(8,128)S(1)}, u32[]{:S(2)}, u32[]{:S(2)}) %collective-permute-start.13) | collective-permute-done | bytes 262176 | tf_op jit(solution)/shard_map/ppermute | solution.py:15
  74.9 2.8 %collective-permute-start.19 = (f32[8,64,128]{2,1,0:T(8,128)S(1)}, f32[8,64,128]{2,1,0:T(8,128)S(1)}, u32[]{:S(2)}, u32[]{:S(2)}) collective-permute-start(f32[8,64,128]{2,1,0:T(8,128)S(1)} %get-tuple-element.81), channel_id=1, source_target_pairs={{0,3},{1,2},{2,1},{3,0},{4,7},{5,6},{6,5},{7,4},{8,11},{9,10},{10,... | collective-permute-start | bytes 786440 | tf_op jit(solution)/shard_map/ppermute | solution.py:15
  78.2 1.1 shard_map.58
  79.4 1.6 %collective-permute-start.3 = (f32[8,64,128]{2,1,0:T(8,128)S(1)}, f32[8,64,128]{2,1,0:T(8,128)S(1)}, u32[]{:S(2)}, u32[]{:S(2)}) collective-permute-start(f32[8,64,128]{2,1,0:T(8,128)S(1)} %get-tuple-element.52), channel_id=1, source_target_pairs={{0,64},{8,72},{16,80},{24,88},{32,96},{40,104},{48,112},{56,120},{... | collective-permute-start | bytes 786440 | tf_op jit(solution)/shard_map/ppermute | solution.py:15
  82.1 2.8 %collective-permute-start.8 = (f32[8,64,128]{2,1,0:T(8,128)S(1)}, f32[8,64,128]{2,1,0:T(8,128)S(1)}, u32[]{:S(2)}, u32[]{:S(2)}) collective-permute-start(f32[8,64,128]{2,1,0:T(8,128)S(1)} %get-tuple-element.61), channel_id=1, source_target_pairs={{0,3},{1,2},{2,1},{3,0},{4,7},{5,6},{6,5},{7,4},{8,11},{9,10},{10,... | collective-permute-start | bytes 786440 | tf_op jit(solution)/shard_map/ppermute | solution.py:15
  85.4 5.6 %collective-permute-done.20.refs_1_ = f32[8,64,128]{2,1,0:T(8,128)S(1)} collective-permute-done((f32[8,64,128]{2,1,0:T(8,128)S(1)}, f32[8,64,128]{2,1,0:T(8,128)S(1)}, u32[]{:S(2)}, u32[]{:S(2)}) %collective-permute-start.20) | collective-permute-done | bytes 262176 | tf_op jit(solution)/shard_map/ppermute | solution.py:15
  92.5 4.1 %collective-permute-done.8.refs_0_ = f32[8,64,128]{2,1,0:T(8,128)S(1)} collective-permute-done((f32[8,64,128]{2,1,0:T(8,128)S(1)}, f32[8,64,128]{2,1,0:T(8,128)S(1)}, u32[]{:S(2)}, u32[]{:S(2)}) %collective-permute-start.8) | collective-permute-done | bytes 262176 | tf_op jit(solution)/shard_map/ppermute | solution.py:15
  96.6 2.8 %collective-permute-done.9.refs_1_ = f32[8,64,128]{2,1,0:T(8,128)S(1)} collective-permute-done((f32[8,64,128]{2,1,0:T(8,128)S(1)}, f32[8,64,128]{2,1,0:T(8,128)S(1)}, u32[]{:S(2)}, u32[]{:S(2)}) %collective-permute-start.9) | collective-permute-done | bytes 262176 | tf_op jit(solution)/shard_map/ppermute | solution.py:15
  100.7 5.2 %collective-permute-start.22 = (f32[8,64,128]{2,1,0:T(8,128)S(1)}, f32[8,64,128]{2,1,0:T(8,128)S(1)}, u32[]{:S(2)}, u32[]{:S(2)}) collective-permute-start(f32[8,64,128]{2,1,0:T(8,128)S(1)} %add.3), channel_id=1, source_target_pairs={{0,4},{1,5},{2,6},{3,7},{4,0},{5,1},{6,2},{7,3},{8,12},{9,13},{10,... | collective-permute-start | bytes 786440 | tf_op jit(solution)/shard_map/ppermute | solution.py:15
  107.0 8.8 %collective-permute-done.22.third_ref = f32[8,64,128]{2,1,0:T(8,128)S(1)} collective-permute-done((f32[8,64,128]{2,1,0:T(8,128)S(1)}, f32[8,64,128]{2,1,0:T(8,128)S(1)}, u32[]{:S(2)}, u32[]{:S(2)}) %collective-permute-start.22) | collective-permute-done | bytes 262176 | tf_op jit(solution)/shard_map/ppermute | solution.py:15
  115.8 1.6 %shard_map.75 = bf16[1024,128]{1,0:T(8,128)(2,1)} custom-call(s32[10]{0:T(128)S(1)} %stack.43.scalars, bf16[1,64,128,128]{3,2,1,0:T(8,128)(2,1)S(1)} %copy-done.6, f32[8,64,128]{2,1,0:T(8,128)S(1)} %get-tuple-element.63.first_ref, f32[8,64,128]{2,1,0:T(8,128)S(1)} %collective-permute-done.10.second_ref, f32[8,64,128]{2,1,0:T(8,128)S(1)} %collective-permute-done.22.third_ref), custom_call_target="tpu_custom_call" | custom-call | flops 67108864 | bytes 1572864 | tf_op jit(solution)/shard_map/pallas_call | solution.py:183
  (69 shorter events, 29.0 us)
Async XLA Ops:
  4.4 4.3 %collective-permute-start.15 = (f32[8,64,128]{2,1,0:T(8,128)S(1)}, f32[8,64,128]{2,1,0:T(8,128)S(1)}, u32[]{:S(2)}, u32[]{:S(2)}) collective-permute-start(f32[8,64,128]{2,1,0:T(8,128)S(1)} %get-tuple-element.74), channel_id=1, source_target_pairs={{0,8},{8,0},{16,24},{24,16},{32,40},{40,32},{48,56},{56,48},{64,72... | collective-permute-start | bytes 786440 | tf_op jit(solution)/shard_map/ppermute | solution.py:15
  5.7 11.1 %collective-permute-start.4 = (f32[8,64,128]{2,1,0:T(8,128)S(1)}, f32[8,64,128]{2,1,0:T(8,128)S(1)}, u32[]{:S(2)}, u32[]{:S(2)}) collective-permute-start(f32[8,64,128]{2,1,0:T(8,128)S(1)} %get-tuple-element.54), channel_id=1, source_target_pairs={{0,8},{8,0},{16,24},{24,16},{32,40},{40,32},{48,56},{56,48},{64,72... | collective-permute-start | bytes 786440 | tf_op jit(solution)/shard_map/ppermute | solution.py:15
  7.4 15.2 %collective-permute-start.11 = (f32[8,64,128]{2,1,0:T(8,128)S(1)}, f32[8,64,128]{2,1,0:T(8,128)S(1)}, u32[]{:S(2)}, u32[]{:S(2)}) collective-permute-start(f32[8,64,128]{2,1,0:T(8,128)S(1)} %get-tuple-element.66), channel_id=1, source_target_pairs={{0,8},{8,0},{16,24},{24,16},{32,40},{40,32},{48,56},{56,48},{64,72... | collective-permute-start | bytes 786440 | tf_op jit(solution)/shard_map/ppermute | solution.py:15
  13.3 11.3 %collective-permute-start.16 = (f32[8,64,128]{2,1,0:T(8,128)S(1)}, f32[8,64,128]{2,1,0:T(8,128)S(1)}, u32[]{:S(2)}, u32[]{:S(2)}) collective-permute-start(f32[8,64,128]{2,1,0:T(8,128)S(1)} %get-tuple-element.76), channel_id=1, source_target_pairs={{0,16},{8,24},{16,0},{24,8},{32,48},{40,56},{48,32},{56,40},{64,80... | collective-permute-start | bytes 786440 | tf_op jit(solution)/shard_map/ppermute | solution.py:15
  16.4 12.7 %collective-permute-start = (f32[8,64,128]{2,1,0:T(8,128)S(1)}, f32[8,64,128]{2,1,0:T(8,128)S(1)}, u32[]{:S(2)}, u32[]{:S(2)}) collective-permute-start(f32[8,64,128]{2,1,0:T(8,128)S(1)} %get-tuple-element.46), channel_id=1, source_target_pairs={{0,8},{8,0},{16,24},{24,16},{32,40},{40,32},{48,56},{56,48},{64,72... | collective-permute-start | bytes 786440 | tf_op jit(solution)/shard_map/ppermute | solution.py:15
  21.2 17.6 %collective-permute-start.5 = (f32[8,64,128]{2,1,0:T(8,128)S(1)}, f32[8,64,128]{2,1,0:T(8,128)S(1)}, u32[]{:S(2)}, u32[]{:S(2)}) collective-permute-start(f32[8,64,128]{2,1,0:T(8,128)S(1)} %get-tuple-element.56), channel_id=1, source_target_pairs={{0,16},{8,24},{16,0},{24,8},{32,48},{40,56},{48,32},{56,40},{64,80... | collective-permute-start | bytes 786440 | tf_op jit(solution)/shard_map/ppermute | solution.py:15
  23.7 20.8 %collective-permute-start.12 = (f32[8,64,128]{2,1,0:T(8,128)S(1)}, f32[8,64,128]{2,1,0:T(8,128)S(1)}, u32[]{:S(2)}, u32[]{:S(2)}) collective-permute-start(f32[8,64,128]{2,1,0:T(8,128)S(1)} %get-tuple-element.68), channel_id=1, source_target_pairs={{0,16},{8,24},{16,0},{24,8},{32,48},{40,56},{48,32},{56,40},{64,80... | collective-permute-start | bytes 786440 | tf_op jit(solution)/shard_map/ppermute | solution.py:15
  25.7 24.9 %collective-permute-start.17 = (f32[8,64,128]{2,1,0:T(8,128)S(1)}, f32[8,64,128]{2,1,0:T(8,128)S(1)}, u32[]{:S(2)}, u32[]{:S(2)}) collective-permute-start(f32[8,64,128]{2,1,0:T(8,128)S(1)} %get-tuple-element.78), channel_id=1, source_target_pairs={{0,32},{8,40},{16,48},{24,56},{32,0},{40,8},{48,16},{56,24},{64,96... | collective-permute-start | bytes 786440 | tf_op jit(solution)/shard_map/ppermute | solution.py:15
  30.3 23.3 %collective-permute-start.1 = (f32[8,64,128]{2,1,0:T(8,128)S(1)}, f32[8,64,128]{2,1,0:T(8,128)S(1)}, u32[]{:S(2)}, u32[]{:S(2)}) collective-permute-start(f32[8,64,128]{2,1,0:T(8,128)S(1)} %get-tuple-element.48), channel_id=1, source_target_pairs={{0,16},{8,24},{16,0},{24,8},{32,48},{40,56},{48,32},{56,40},{64,80... | collective-permute-start | bytes 786440 | tf_op jit(solution)/shard_map/ppermute | solution.py:15
  40.0 15.2 %collective-permute-start.6 = (f32[8,64,128]{2,1,0:T(8,128)S(1)}, f32[8,64,128]{2,1,0:T(8,128)S(1)}, u32[]{:S(2)}, u32[]{:S(2)}) collective-permute-start(f32[8,64,128]{2,1,0:T(8,128)S(1)} %get-tuple-element.58), channel_id=1, source_target_pairs={{0,32},{8,40},{16,48},{24,56},{32,0},{40,8},{48,16},{56,24},{64,96... | collective-permute-start | bytes 786440 | tf_op jit(solution)/shard_map/ppermute | solution.py:15
  45.7 26.4 %collective-permute-start.13 = (f32[8,64,128]{2,1,0:T(8,128)S(1)}, f32[8,64,128]{2,1,0:T(8,128)S(1)}, u32[]{:S(2)}, u32[]{:S(2)}) collective-permute-start(f32[8,64,128]{2,1,0:T(8,128)S(1)} %get-tuple-element.70), channel_id=1, source_target_pairs={{0,32},{8,40},{16,48},{24,56},{32,0},{40,8},{48,16},{56,24},{64,96... | collective-permute-start | bytes 786440 | tf_op jit(solution)/shard_map/ppermute | solution.py:15
  51.8 22.0 %collective-permute-start.18 = (f32[8,64,128]{2,1,0:T(8,128)S(1)}, f32[8,64,128]{2,1,0:T(8,128)S(1)}, u32[]{:S(2)}, u32[]{:S(2)}) collective-permute-start(f32[8,64,128]{2,1,0:T(8,128)S(1)} %get-tuple-element.80), channel_id=1, source_target_pairs={{0,64},{8,72},{16,80},{24,88},{32,96},{40,104},{48,112},{56,120},{... | collective-permute-start | bytes 786440 | tf_op jit(solution)/shard_map/ppermute | solution.py:15
  54.7 23.5 %collective-permute-start.2 = (f32[8,64,128]{2,1,0:T(8,128)S(1)}, f32[8,64,128]{2,1,0:T(8,128)S(1)}, u32[]{:S(2)}, u32[]{:S(2)}) collective-permute-start(f32[8,64,128]{2,1,0:T(8,128)S(1)} %get-tuple-element.50), channel_id=1, source_target_pairs={{0,32},{8,40},{16,48},{24,56},{32,0},{40,8},{48,16},{56,24},{64,96... | collective-permute-start | bytes 786440 | tf_op jit(solution)/shard_map/ppermute | solution.py:15
  56.4 24.6 %collective-permute-start.7 = (f32[8,64,128]{2,1,0:T(8,128)S(1)}, f32[8,64,128]{2,1,0:T(8,128)S(1)}, u32[]{:S(2)}, u32[]{:S(2)}) collective-permute-start(f32[8,64,128]{2,1,0:T(8,128)S(1)} %get-tuple-element.60), channel_id=1, source_target_pairs={{0,64},{8,72},{16,80},{24,88},{32,96},{40,104},{48,112},{56,120},{... | collective-permute-start | bytes 786440 | tf_op jit(solution)/shard_map/ppermute | solution.py:15
  73.2 11.8 %collective-permute-start.14 = (f32[8,64,128]{2,1,0:T(8,128)S(1)}, f32[8,64,128]{2,1,0:T(8,128)S(1)}, u32[]{:S(2)}, u32[]{:S(2)}) collective-permute-start(f32[8,64,128]{2,1,0:T(8,128)S(1)} %get-tuple-element.72), channel_id=1, source_target_pairs={{0,64},{8,72},{16,80},{24,88},{32,96},{40,104},{48,112},{56,120},{... | collective-permute-start | bytes 786440 | tf_op jit(solution)/shard_map/ppermute | solution.py:15
  74.9 10.5 %collective-permute-start.19 = (f32[8,64,128]{2,1,0:T(8,128)S(1)}, f32[8,64,128]{2,1,0:T(8,128)S(1)}, u32[]{:S(2)}, u32[]{:S(2)}) collective-permute-start(f32[8,64,128]{2,1,0:T(8,128)S(1)} %get-tuple-element.81), channel_id=1, source_target_pairs={{0,3},{1,2},{2,1},{3,0},{4,7},{5,6},{6,5},{7,4},{8,11},{9,10},{10,... | collective-permute-start | bytes 786440 | tf_op jit(solution)/shard_map/ppermute | solution.py:15
  77.7 13.4 %collective-permute-start.20 = (f32[8,64,128]{2,1,0:T(8,128)S(1)}, f32[8,64,128]{2,1,0:T(8,128)S(1)}, u32[]{:S(2)}, u32[]{:S(2)}) collective-permute-start(f32[8,64,128]{2,1,0:T(8,128)S(1)} %get-tuple-element.82), channel_id=1, source_target_pairs={{0,3},{1,2},{2,1},{3,0},{4,7},{5,6},{6,5},{7,4},{8,11},{9,10},{10,... | collective-permute-start | bytes 786440 | tf_op jit(solution)/shard_map/ppermute | solution.py:15
  79.4 13.1 %collective-permute-start.3 = (f32[8,64,128]{2,1,0:T(8,128)S(1)}, f32[8,64,128]{2,1,0:T(8,128)S(1)}, u32[]{:S(2)}, u32[]{:S(2)}) collective-permute-start(f32[8,64,128]{2,1,0:T(8,128)S(1)} %get-tuple-element.52), channel_id=1, source_target_pairs={{0,64},{8,72},{16,80},{24,88},{32,96},{40,104},{48,112},{56,120},{... | collective-permute-start | bytes 786440 | tf_op jit(solution)/shard_map/ppermute | solution.py:15
  82.1 14.5 %collective-permute-start.8 = (f32[8,64,128]{2,1,0:T(8,128)S(1)}, f32[8,64,128]{2,1,0:T(8,128)S(1)}, u32[]{:S(2)}, u32[]{:S(2)}) collective-permute-start(f32[8,64,128]{2,1,0:T(8,128)S(1)} %get-tuple-element.61), channel_id=1, source_target_pairs={{0,3},{1,2},{2,1},{3,0},{4,7},{5,6},{6,5},{7,4},{8,11},{9,10},{10,... | collective-permute-start | bytes 786440 | tf_op jit(solution)/shard_map/ppermute | solution.py:15
  84.9 14.5 %collective-permute-start.9 = (f32[8,64,128]{2,1,0:T(8,128)S(1)}, f32[8,64,128]{2,1,0:T(8,128)S(1)}, u32[]{:S(2)}, u32[]{:S(2)}) collective-permute-start(f32[8,64,128]{2,1,0:T(8,128)S(1)} %get-tuple-element.62), channel_id=1, source_target_pairs={{0,3},{1,2},{2,1},{3,0},{4,7},{5,6},{6,5},{7,4},{8,11},{9,10},{10,... | collective-permute-start | bytes 786440 | tf_op jit(solution)/shard_map/ppermute | solution.py:15
  92.2 8.5 %collective-permute-start.21 = (f32[8,64,128]{2,1,0:T(8,128)S(1)}, f32[8,64,128]{2,1,0:T(8,128)S(1)}, u32[]{:S(2)}, u32[]{:S(2)}) collective-permute-start(f32[8,64,128]{2,1,0:T(8,128)S(1)} %get-tuple-element.84), channel_id=1, source_target_pairs={{0,1},{1,0},{2,3},{3,2},{4,5},{5,4},{6,7},{7,6},{8,9},{9,8},{10,11... | collective-permute-start | bytes 786440 | tf_op jit(solution)/shard_map/ppermute | solution.py:15
  99.4 16.3 %copy-start.6 = (bf16[1,64,128,128]{3,2,1,0:T(8,128)(2,1)S(1)}, bf16[1,64,128,128]{3,2,1,0:T(8,128)(2,1)}, u32[]{:S(2)}) copy-start(bf16[1,64,128,128]{3,2,1,0:T(8,128)(2,1)} %basis_ref.1) | copy-start | bytes 6291460
  100.5 6.5 %collective-permute-start.10 = (f32[8,64,128]{2,1,0:T(8,128)S(1)}, f32[8,64,128]{2,1,0:T(8,128)S(1)}, u32[]{:S(2)}, u32[]{:S(2)}) collective-permute-start(f32[8,64,128]{2,1,0:T(8,128)S(1)} %get-tuple-element.64), channel_id=1, source_target_pairs={{0,1},{1,0},{2,3},{3,2},{4,5},{5,4},{6,7},{7,6},{8,9},{9,8},{10,11... | collective-permute-start | bytes 786440 | tf_op jit(solution)/shard_map/ppermute | solution.py:15
  100.7 15.1 %collective-permute-start.22 = (f32[8,64,128]{2,1,0:T(8,128)S(1)}, f32[8,64,128]{2,1,0:T(8,128)S(1)}, u32[]{:S(2)}, u32[]{:S(2)}) collective-permute-start(f32[8,64,128]{2,1,0:T(8,128)S(1)} %add.3), channel_id=1, source_target_pairs={{0,4},{1,5},{2,6},{3,7},{4,0},{5,1},{6,2},{7,3},{8,12},{9,13},{10,... | collective-permute-start | bytes 786440 | tf_op jit(solution)/shard_map/ppermute | solution.py:15
  (9 other events, 29.6 us)

commit v2 on v0

v2 whole, which is shorter than its diff:
```python
import functools

import jax
import jax.numpy as jnp
from jax import lax
from jax.experimental import pallas as pl
from jax.experimental.pallas import tpu as pltpu
from jax.sharding import PartitionSpec as P

SLOTS = 4

ORDER = [
    ("leaf", 0), ("leaf", 1), ("mix", 0, 0), ("leaf", 2), ("leaf", 3), ("mix", 1, 0),
    ("mix", 0, 1), ("mix", 1, 1), ("mix", 0, 2), ("mix", 2, 0), ("mix", 1, 2), ("mix", 3, 0),
    ("mix", 0, 3), ("mix", 2, 1), ("mix", 1, 3), ("mix", 3, 1), ("mix", 2, 2), ("mix", 3, 2),
    ("mix", 2, 3), ("far",), ("mix", 3, 3), ("end",),
]


def swap(block, axis, mask):
    count = lax.axis_size(axis)
    return lax.ppermute(block, axis, [(at, at ^ mask) for at in range(count)])


def turn(block):
    middle = block.shape[-1] // 2
    return jnp.concatenate([-block[:, middle:], block[:, :middle]], -1)


def split(block):
    high = block.astype(jnp.bfloat16)
    low = (block - high.astype(jnp.float32)).astype(jnp.bfloat16)
    return high, low


def stack_split(blocks):
    highs, lows = [], []
    for block in blocks:
        high, low = split(block)
        highs += [high, turn(high)]
        lows += [low, turn(low)]
    return jnp.concatenate([jnp.concatenate(highs, 0), jnp.concatenate(lows, 0)], 1)


def halves(bit, half):
    return (1 - bit) * half, bit * half


def leaf_body(scalars, ranks, mine, outs, *, bit_at):
    rhs_ref, basis_ref = mine
    half = outs[0].shape[0]
    for out_ref, start in zip(outs, halves(scalars[bit_at], half)):
        for at in range(half):
            source = rhs_ref[start + at]
            stacked = jnp.concatenate([source, turn(source)], 0)
            out_ref[at] = jnp.dot(basis_ref[start + at], stacked, preferred_element_type=jnp.float32)


def mix_body(scalars, ranks, mine, outs, *, level, slot, bit_at):
    matrices_ref, own_ref, partner_ref = mine[:3]
    added = mine[3:]
    half, rank_cap, columns = outs[0].shape
    low_count = 2 << level
    chunk = scalars[slot]
    rows = lax.broadcasted_iota(jnp.int32, (rank_cap, columns), 0)
    for which, (out_ref, start) in enumerate(zip(outs, halves(scalars[bit_at], half))):
        for pair in range(half // 2):
            j = start // 2 + pair
            stacked = stack_split([own_ref[j], partner_ref[j]])
            first = start + 2 * pair
            left = jnp.concatenate([matrices_ref[first], matrices_ref[first + 1]], 0)
            both = jnp.dot(left, stacked, preferred_element_type=jnp.float32)
            both = both[:, :columns] + both[:, columns:]
            for s in range(2):
                local = first + s
                place = (local // low_count) * (SLOTS * low_count) + chunk * low_count + local % low_count
                live = ranks[level, 0, 0, place]
                mixed = jnp.where(rows < live, both[s * rank_cap : (s + 1) * rank_cap], 0.0)
                if added:
                    mixed = mixed + added[which][2 * pair + s]
                out_ref[2 * pair + s] = mixed


def far_body(scalars, ranks, mine, outs):
    for at in range(outs[0].shape[0]):
        outs[0][at] = mine[0][at] + mine[1][at]


def end_body(scalars, ranks, mine, outs):
    basis_ref, first_ref, second_ref, third_ref = mine
    out_ref = outs[0]
    points = basis_ref.shape[1]
    columns = out_ref.shape[1]
    for at in range(first_ref.shape[0]):
        total = first_ref[at] + second_ref[at] + third_ref[at]
        both = jnp.dot(basis_ref[at], stack_split([total]), preferred_element_type=jnp.float32)
        both = both[:, :columns] + both[:, columns:]
        out_ref[at * points : (at + 1) * points, :] = both.astype(out_ref.dtype)


def kernel(*refs, body, sizes, first_copies, next_copies):
    scalars, ranks, token = refs[:3]
    at = 3
    groups = []
    for size in sizes:
        groups.append(refs[at : at + size])
        at += size
    mine, first_from, next_from, outs, next_to, first_to, sems = groups
    loads = list(first_copies(scalars, first_from, first_to, sems[0])) if first_copies else []
    for load in loads:
        load.start()
    coming = list(next_copies(scalars, next_from, next_to, sems[-1])) if next_copies else []
    for load in coming:
        load.start()
    for load in loads:
        load.wait()
    body(scalars, ranks, first_to + mine, outs)
    for load in coming:
        load.wait()


def shards(rhs, leaf_basis, transfer, ranks, out_basis):
    leaves, rank_cap, wide = leaf_basis.shape
    points = wide // 2
    columns = rhs.shape[1]
    levels = transfer.shape[0]
    chunk_leaves = leaves // SLOTS
    half = chunk_leaves // 2
    position = lax.axis_index("row")
    column = lax.axis_index("col")
    column_count = lax.axis_size("col")
    owned = leaves // column_count
    scalars = jnp.stack(
        [(column >> 1) ^ (SLOTS - 1 - slot) for slot in range(SLOTS)]
        + [position >> level & 1 for level in range(levels)]
        + [column & 1, column]
    ).astype(jnp.int32)
    far_memory = lambda array: pltpu.with_memory_space_constraint(array, pltpu.HBM)
    sources = far_memory(rhs.reshape(chunk_leaves, SLOTS, points, columns))
    bases = far_memory(leaf_basis.reshape(chunk_leaves, SLOTS, rank_cap, wide))
    matrices = []
    for level in range(levels):
        low_count = 2 << level
        shape = (levels, chunk_leaves // low_count, SLOTS, low_count, rank_cap, 4 * rank_cap)
        matrices.append(far_memory(transfer.reshape(shape)))
    targets = far_memory(out_basis)
    half_out = ((half, rank_cap, columns), jnp.float32)

    def load_of(step):
        if step[0] == "leaf":
            slot = step[1]

            def copies(scalars, arrays, buffers, sems):
                for at, (array, buffer) in enumerate(zip(arrays, buffers)):
                    yield pltpu.make_async_copy(array.at[:, scalars[slot]], buffer, sems.at[at])

            return [sources, bases], [((chunk_leaves, points, columns), rhs.dtype), ((chunk_leaves, rank_cap, wide), leaf_basis.dtype)], copies, 2
        if step[0] == "mix":
            level, slot = step[1:]
            low_count = 2 << level
            count = chunk_leaves // low_count

            def copies(scalars, arrays, buffers, sems):
                for at in range(count):
                    yield pltpu.make_async_copy(
                        arrays[0].at[level, at, scalars[slot]],
                        buffers[0].at[pl.ds(at * low_count, low_count)],
                        sems.at[at],
                    )

            return [matrices[level]], [((chunk_leaves, rank_cap, 4 * rank_cap), transfer.dtype)], copies, count
        if step[0] == "end":

            def copies(scalars, arrays, buffers, sems):
                yield pltpu.make_async_copy(
                    arrays[0].at[0, pl.ds(scalars[SLOTS + levels + 1] * owned, owned)], buffers[0], sems.at[0]
                )

            return [targets], [((owned, points, 2 * rank_cap), out_basis.dtype)], copies, 1
        return [], [], None, 0

    def run(at, body, loaded, arrays, outs, token, flops):
        first = load_of(ORDER[at]) if at == 0 else ([], [], None, 0)
        after = load_of(ORDER[at + 1]) if at + 1 < len(ORDER) else ([], [], None, 0)
        in_vmem = list(loaded) + [pltpu.with_memory_space_constraint(array, pltpu.VMEM) for array in arrays]
        outs = list(outs)
        last = at + 1 == len(ORDER)
        sems = [count for count in (first[3], after[3]) if count]
        token = [scalars] if token is None else [token]
        sizes = (len(in_vmem), len(first[0]), len(after[0]), len(outs), len(after[1]), len(first[1]), len(sems))
        vmem = pl.BlockSpec(memory_space=pltpu.VMEM)
        smem = pl.BlockSpec(memory_space=pltpu.SMEM)
        anywhere = pl.BlockSpec(memory_space=pl.ANY)
        moved = 4 * sum(array.size for array in arrays) + (3 << 19)
        results = pl.pallas_call(
            functools.partial(kernel, body=body, sizes=sizes, first_copies=first[2], next_copies=after[2]),
            in_specs=[smem, smem, anywhere] + [vmem] * len(in_vmem) + [anywhere] * (len(first[0]) + len(after[0])),
            out_specs=[vmem] * (len(outs) + len(after[1])),
            out_shape=[
                jax.ShapeDtypeStruct(shape, kind) if last else pltpu.VMEM(shape, kind) for shape, kind in outs + after[1]
            ],
            scratch_shapes=[pltpu.VMEM(shape, kind) for shape, kind in first[1]]
            + [pltpu.SemaphoreType.DMA((count,)) for count in sems],
            cost_estimate=pl.CostEstimate(flops=flops, bytes_accessed=moved, transcendentals=0),
            compiler_params=pltpu.CompilerParams(vmem_limit_bytes=16 * 1024 * 1024),
        )(scalars, ranks, *token, *in_vmem, *first[0], *after[0])
        return results[: len(outs)], results[len(outs) :]

    loaded, token = [], None
    sent, kept, added, near = {}, {}, {}, {}
    far = result = None
    for at, step in enumerate(ORDER):
        if step[0] == "leaf":
            slot = step[1]
            body = functools.partial(leaf_body, bit_at=SLOTS)
            flops = 2 * chunk_leaves * rank_cap * wide * columns
            (sent[slot], kept[slot]), loaded = run(at, body, loaded, [], [half_out] * 2, token, flops)
            token = kept[slot]
        elif step[0] == "mix":
            level, slot = step[1:]
            partner = swap(sent[slot], "row", 1 << level)
            body = functools.partial(mix_body, level=level, slot=slot, bit_at=SLOTS + level + 1)
            arrays = [kept[slot], partner] + (added.get(slot, []) if level == levels - 1 else [])
            flops = 4 * chunk_leaves * rank_cap * 4 * rank_cap * columns
            (sent[slot], kept[slot]), loaded = run(at, body, loaded, arrays, [half_out] * 2, token, flops)
            token = kept[slot]
            if level == levels - 1:
                if slot % 2 == 0:
                    added[slot + 1] = [swap(kept[slot], "col", 3), swap(sent[slot], "col", 3)]
                else:
                    near[slot] = swap(sent[slot], "col", 1)
        elif step[0] == "far":
            (total,), loaded = run(at, far_body, loaded, [kept[1], near[1]], [half_out], token, 1 << 16)
            far = swap(total, "col", 4)
            token = total
        else:
            arrays = [kept[3], near[3], far]
            out = ((owned * points, columns), jnp.bfloat16)
            flops = 4 * owned * points * 2 * rank_cap * columns
            (result,), _ = run(at, end_body, loaded, arrays, [out], token, flops)
    return result


def solution(mesh):
    in_specs = (
        P(("row", "col"), None),
        P(("row", "col"), None, None),
        P(None, "row", "col", None, None, None),
        P(None, "row", "col", None),
        P("row", None, None, None),
    )
    out_specs = P(("row", "col"), None)
    return jax.shard_map(shards, mesh=mesh, in_specs=in_specs, out_specs=out_specs, check_vma=False)
```

time: 261 us -> 122 us (0.47)
  waiting for transfers between devices: 188 us -> 49.3 us
  Pallas kernels: 0 us -> 44.6 us
  matrix products: 24.1 us -> 0 us
  starting transfers between devices: 6.56 us -> 26.5 us
  other arithmetic: 18.2 us -> 0 us
  between operations: 13.6 us -> 0.26 us
  local copies, waits for them, and re-layouts: 9.72 us -> 0.77 us
    reduce_scatter x1 -> x0, waiting for transfers between devices: 97.4 us -> none  [shards(): total = lax.psum_scatter(coeff, 'col', scatter_dimension=0, tiled=True)]
    pallas_call x0 -> x22, Pallas kernels: none -> 44.6 us  [run(): pl.pallas_call(functools.partial(kernel, body=body, sizes=sizes, first_co...]
    ppermute x4 -> x23, waiting for transfers between devices: 90.8 us -> 49.3 us  [swap(): return lax.ppermute(block, axis, [(at, at ^ mask) for at in range(count)])]
    dot_general x6 -> x0, matrix products: 24.1 us -> none  [the longest x4 18.1 us: mix_level(): jnp.einsum('jskm,jmn->jskn', weights, stacked, precision=lax.Precision.HI...]
    ppermute x4 -> x23, starting transfers between devices: 6.56 us -> 26.5 us  [swap(): return lax.ppermute(block, axis, [(at, at ^ mask) for at in range(count)])]
    neg x10 -> x0, other arithmetic: 13.4 us -> none  [complex_stack(): flipped = jnp.concatenate([-block[..., middle:], block[..., :middle]], -1)]
    slice x1 -> x0, local copies, waits for them, and re-layouts: 5.65 us -> none  [shards(): transfer[level, 0, 0]]
    select_n x4 -> x0, other arithmetic: 4.46 us -> none  [mix_level(): return jnp.where(live_rows[..., None], mixed, jnp.float32(0.0))]
  transfers between devices with their start and end apart: 5 -> 23, of which waited for: 4 -> 14; matrix products, arithmetic and copies ran while one was open for 3% -> 0% of each run, Pallas kernels for 0% -> 28%
where the time goes in v2:
time: 122 us; the launch traced here: 121 us
  waiting for transfers between devices  49.3 us (40%)
  Pallas kernels  44.6 us (37%)
  starting transfers between devices  26.5 us (22%)
    ppermute x23, waiting for transfers between devices, swap(): return lax.ppermute(block, axis, [(at, at ^ mask) for at in range(count)])  49.3 us
    pallas_call x22, Pallas kernels, run(): pl.pallas_call(functools.partial(kernel, body=body, sizes=sizes, first_co...  44.6 us
    ppermute x23, starting transfers between devices, swap(): return lax.ppermute(block, axis, [(at, at ^ mask) for at in range(count)])  26.5 us
  transfers between devices with their start and end apart: 23, of which 14 were waited for; matrix products, arithmetic and copies ran while one was open for 0% of the time, Pallas kernels for 28%

profile of v2, /device:TPU:8, one launch (start us, length us, event | category | flops | bytes accessed | tf_op | source)
XLA Modules:
  0.0 121.4 jit_solution(11802037287833935776)
XLA Ops:
  0.8 2.5 %shard_map.55 = (f32[8,64,128]{2,1,0:T(8,128)S(1)}, f32[8,64,128]{2,1,0:T(8,128)S(1)}, bf16[16,128,128]{2,1,0:T(8,128)(2,1)S(1)}, bf16[16,64,256]{2,1,0:T(8,128)(2,1)S(1)}) custom-call(s32[10]{0:T(128)S(1)} %stack.43.refs_0_.refs_2_, s32[4,1,1,64]{3,2,1,0:T(1,128)S(1)} %copy-done, s32[10]{0:T(128)S(1)} %stack.43.refs_0_.refs_2_, ...), custom_call_target="tpu_custom_call" | custom-call | flops 67108864 | bytes 1572864 | tf_op jit(solution)/shard_map/pallas_call | solution.py:195
  5.5 2.2 %shard_map.57 = (f32[8,64,128]{2,1,0:T(8,128)S(1)}, f32[8,64,128]{2,1,0:T(8,128)S(1)}, bf16[16,128,128]{2,1,0:T(8,128)(2,1)S(1)}, bf16[16,64,256]{2,1,0:T(8,128)(2,1)S(1)}) custom-call(s32[10]{0:T(128)S(1)} %stack.43.refs_0_.refs_2_, s32[4,1,1,64]{3,2,1,0:T(1,128)S(1)} %copy-done, f32[8,64,128]{2,1,0:T(8,128)S(1)} %get-tuple-element.72.refs_2_.refs_4_, ...), custom_call_target="tpu_custom_call" | custom-call | flops 134217728 | bytes 2097152 | tf_op jit(solution)/shard_map/pallas_call | solution.py:195
  9.9 2.1 %shard_map.58 = (f32[8,64,128]{2,1,0:T(8,128)S(1)}, f32[8,64,128]{2,1,0:T(8,128)S(1)}, bf16[16,128,128]{2,1,0:T(8,128)(2,1)S(1)}, bf16[16,64,256]{2,1,0:T(8,128)(2,1)S(1)}) custom-call(s32[10]{0:T(128)S(1)} %stack.43.refs_0_.refs_2_, s32[4,1,1,64]{3,2,1,0:T(1,128)S(1)} %copy-done, f32[8,64,128]{2,1,0:T(8,128)S(1)} %get-tuple-element.75.refs_2_.refs_4_, ...), custom_call_target="tpu_custom_call" | custom-call | flops 67108864 | bytes 1572864 | tf_op jit(solution)/shard_map/pallas_call | solution.py:195
  14.0 2.7 %collective-permute-done.1.refs_5_ = f32[8,64,128]{2,1,0:T(8,128)S(1)} collective-permute-done((f32[8,64,128]{2,1,0:T(8,128)S(1)}, f32[8,64,128]{2,1,0:T(8,128)S(1)}, u32[]{:S(2)}, u32[]{:S(2)}) %collective-permute-start.1) | collective-permute-done | bytes 262176 | tf_op jit(solution)/shard_map/ppermute | solution.py:22
  16.7 2.1 %shard_map.60 = (f32[8,64,128]{2,1,0:T(8,128)S(1)}, f32[8,64,128]{2,1,0:T(8,128)S(1)}, bf16[16,64,256]{2,1,0:T(8,128)(2,1)S(1)}) custom-call(s32[10]{0:T(128)S(1)} %stack.43.refs_0_.refs_2_, s32[4,1,1,64]{3,2,1,0:T(1,128)S(1)} %copy-done, f32[8,64,128]{2,1,0:T(8,128)S(1)} %get-tuple-element.81.refs_2_.refs_4_, ...), custom_call_target="tpu_custom_call" | custom-call | flops 134217728 | bytes 2097152 | tf_op jit(solution)/shard_map/pallas_call | solution.py:195
  18.8 2.1 %shard_map.61 = (f32[8,64,128]{2,1,0:T(8,128)S(1)}, f32[8,64,128]{2,1,0:T(8,128)S(1)}, bf16[16,64,256]{2,1,0:T(8,128)(2,1)S(1)}) custom-call(s32[10]{0:T(128)S(1)} %stack.43.refs_0_.refs_2_, s32[4,1,1,64]{3,2,1,0:T(1,128)S(1)} %copy-done, f32[8,64,128]{2,1,0:T(8,128)S(1)} %get-tuple-element.84.refs_2_.refs_4_, ...), custom_call_target="tpu_custom_call" | custom-call | flops 134217728 | bytes 2097152 | tf_op jit(solution)/shard_map/pallas_call | solution.py:195
  22.8 3.3 %collective-permute-start.5 = (f32[8,64,128]{2,1,0:T(8,128)S(1)}, f32[8,64,128]{2,1,0:T(8,128)S(1)}, u32[]{:S(2)}, u32[]{:S(2)}) collective-permute-start(f32[8,64,128]{2,1,0:T(8,128)S(1)} %get-tuple-element.95), channel_id=1, source_target_pairs={{0,32},{8,40},{16,48},{24,56},{32,0},{40,8},{48,16},{56,24},{64,96... | collective-permute-start | bytes 786440 | tf_op jit(solution)/shard_map/ppermute | solution.py:22
  26.1 7.4 %collective-permute-done.3.refs_5_ = f32[8,64,128]{2,1,0:T(8,128)S(1)} collective-permute-done((f32[8,64,128]{2,1,0:T(8,128)S(1)}, f32[8,64,128]{2,1,0:T(8,128)S(1)}, u32[]{:S(2)}, u32[]{:S(2)}) %collective-permute-start.3) | collective-permute-done | bytes 262176 | tf_op jit(solution)/shard_map/ppermute | solution.py:22
  33.5 2.1 %shard_map.62 = (f32[8,64,128]{2,1,0:T(8,128)S(1)}, f32[8,64,128]{2,1,0:T(8,128)S(1)}, bf16[16,64,256]{2,1,0:T(8,128)(2,1)S(1)}) custom-call(s32[10]{0:T(128)S(1)} %stack.43.refs_0_.refs_2_, s32[4,1,1,64]{3,2,1,0:T(1,128)S(1)} %copy-done, f32[8,64,128]{2,1,0:T(8,128)S(1)} %get-tuple-element.87.refs_2_.refs_4_, ...), custom_call_target="tpu_custom_call" | custom-call | flops 134217728 | bytes 2097152 | tf_op jit(solution)/shard_map/pallas_call | solution.py:195
  38.8 2.1 %shard_map.64 = (f32[8,64,128]{2,1,0:T(8,128)S(1)}, f32[8,64,128]{2,1,0:T(8,128)S(1)}, bf16[16,64,256]{2,1,0:T(8,128)(2,1)S(1)}) custom-call(s32[10]{0:T(128)S(1)} %stack.43.refs_0_.refs_2_, s32[4,1,1,64]{3,2,1,0:T(1,128)S(1)} %copy-done, f32[8,64,128]{2,1,0:T(8,128)S(1)} %get-tuple-element.93.refs_2_.refs_4_, ...), custom_call_target="tpu_custom_call" | custom-call | flops 134217728 | bytes 2097152 | tf_op jit(solution)/shard_map/pallas_call | solution.py:195
  46.4 2.7 %collective-permute-done.7.refs_5_ = f32[8,64,128]{2,1,0:T(8,128)S(1)} collective-permute-done((f32[8,64,128]{2,1,0:T(8,128)S(1)}, f32[8,64,128]{2,1,0:T(8,128)S(1)}, u32[]{:S(2)}, u32[]{:S(2)}) %collective-permute-start.7) | collective-permute-done | bytes 262176 | tf_op jit(solution)/shard_map/ppermute | solution.py:22
  49.1 2.1 %shard_map.66 = (f32[8,64,128]{2,1,0:T(8,128)S(1)}, f32[8,64,128]{2,1,0:T(8,128)S(1)}, bf16[16,64,256]{2,1,0:T(8,128)(2,1)S(1)}) custom-call(s32[10]{0:T(128)S(1)} %stack.43.refs_0_.refs_2_, s32[4,1,1,64]{3,2,1,0:T(1,128)S(1)} %copy-done, f32[8,64,128]{2,1,0:T(8,128)S(1)} %get-tuple-element.99.refs_2_.refs_4_, ...), custom_call_target="tpu_custom_call" | custom-call | flops 134217728 | bytes 2097152 | tf_op jit(solution)/shard_map/pallas_call | solution.py:195
  51.3 2.1 %shard_map.67 = (f32[8,64,128]{2,1,0:T(8,128)S(1)}, f32[8,64,128]{2,1,0:T(8,128)S(1)}, bf16[16,64,256]{2,1,0:T(8,128)(2,1)S(1)}) custom-call(s32[10]{0:T(128)S(1)} %stack.43.refs_0_.refs_2_, s32[4,1,1,64]{3,2,1,0:T(1,128)S(1)} %copy-done, f32[8,64,128]{2,1,0:T(8,128)S(1)} %get-tuple-element.102.refs_2_, bf16[16,64,256]{2,1,0:T(8,128)(2,1)S(1)} %get-tuple-element.103.refs_3_, ...), custom_call_target="tpu_custom_call" | custom-call | flops 134217728 | bytes 2097152 | tf_op jit(solution)/shard_map/pallas_call | solution.py:195
  53.6 3.7 %collective-permute-done.9.refs_5_ = f32[8,64,128]{2,1,0:T(8,128)S(1)} collective-permute-done((f32[8,64,128]{2,1,0:T(8,128)S(1)}, f32[8,64,128]{2,1,0:T(8,128)S(1)}, u32[]{:S(2)}, u32[]{:S(2)}) %collective-permute-start.9) | collective-permute-done | bytes 262176 | tf_op jit(solution)/shard_map/ppermute | solution.py:22
  57.4 2.1 %shard_map.68 = (f32[8,64,128]{2,1,0:T(8,128)S(1)}, f32[8,64,128]{2,1,0:T(8,128)S(1)}, bf16[16,64,256]{2,1,0:T(8,128)(2,1)S(1)}) custom-call(s32[10]{0:T(128)S(1)} %stack.43.refs_0_.refs_2_, s32[4,1,1,64]{3,2,1,0:T(1,128)S(1)} %copy-done, f32[8,64,128]{2,1,0:T(8,128)S(1)} %get-tuple-element.105.refs_2_.refs_4_, ...), custom_call_target="tpu_custom_call" | custom-call | flops 134217728 | bytes 2097152 | tf_op jit(solution)/shard_map/pallas_call | solution.py:195
  60.6 2.8 %collective-permute-start.13 = (f32[8,64,128]{2,1,0:T(8,128)S(1)}, f32[8,64,128]{2,1,0:T(8,128)S(1)}, u32[]{:S(2)}, u32[]{:S(2)}) collective-permute-start(f32[8,64,128]{2,1,0:T(8,128)S(1)} %get-tuple-element.114), channel_id=1, source_target_pairs={{0,3},{1,2},{2,1},{3,0},{4,7},{5,6},{6,5},{7,4},{8,11},{9,10},{10,... | collective-permute-start | bytes 786440 | tf_op jit(solution)/shard_map/ppermute | solution.py:22
  67.5 3.6 %collective-permute-done.13.refs_7_ = f32[8,64,128]{2,1,0:T(8,128)S(1)} collective-permute-done((f32[8,64,128]{2,1,0:T(8,128)S(1)}, f32[8,64,128]{2,1,0:T(8,128)S(1)}, u32[]{:S(2)}, u32[]{:S(2)}) %collective-permute-start.13) | collective-permute-done | bytes 262176 | tf_op jit(solution)/shard_map/ppermute | solution.py:22
  71.1 4.0 %collective-permute-done.12.refs_6_ = f32[8,64,128]{2,1,0:T(8,128)S(1)} collective-permute-done((f32[8,64,128]{2,1,0:T(8,128)S(1)}, f32[8,64,128]{2,1,0:T(8,128)S(1)}, u32[]{:S(2)}, u32[]{:S(2)}) %collective-permute-start.12) | collective-permute-done | bytes 262176 | tf_op jit(solution)/shard_map/ppermute | solution.py:22
  80.3 7.2 %collective-permute-done.15.refs_5_ = f32[8,64,128]{2,1,0:T(8,128)S(1)} collective-permute-done((f32[8,64,128]{2,1,0:T(8,128)S(1)}, f32[8,64,128]{2,1,0:T(8,128)S(1)}, u32[]{:S(2)}, u32[]{:S(2)}) %collective-permute-start.15) | collective-permute-done | bytes 262176 | tf_op jit(solution)/shard_map/ppermute | solution.py:22
  89.6 4.0 %collective-permute-done.16.refs_5_ = f32[8,64,128]{2,1,0:T(8,128)S(1)} collective-permute-done((f32[8,64,128]{2,1,0:T(8,128)S(1)}, f32[8,64,128]{2,1,0:T(8,128)S(1)}, u32[]{:S(2)}, u32[]{:S(2)}) %collective-permute-start.16) | collective-permute-done | bytes 262176 | tf_op jit(solution)/shard_map/ppermute | solution.py:22
  95.8 2.8 %collective-permute-start.20 = (f32[8,64,128]{2,1,0:T(8,128)S(1)}, f32[8,64,128]{2,1,0:T(8,128)S(1)}, u32[]{:S(2)}, u32[]{:S(2)}) collective-permute-start(f32[8,64,128]{2,1,0:T(8,128)S(1)} %get-tuple-element.129), channel_id=1, source_target_pairs={{0,3},{1,2},{2,1},{3,0},{4,7},{5,6},{6,5},{7,4},{8,11},{9,10},{10,... | collective-permute-start | bytes 786440 | tf_op jit(solution)/shard_map/ppermute | solution.py:22
  100.7 5.7 %collective-permute-start.22 = (f32[8,64,128]{2,1,0:T(8,128)S(1)}, f32[8,64,128]{2,1,0:T(8,128)S(1)}, u32[]{:S(2)}, u32[]{:S(2)}) collective-permute-start(f32[8,64,128]{2,1,0:T(8,128)S(1)} %get-tuple-element.126.refs_2_), channel_id=1, source_target_pairs={{0,4},{1,5},{2,6},{3,7},{4,0},{5,1},{6,2},{7,3},{8,12},{9,13},{10,... | collective-permute-start | bytes 786440 | tf_op jit(solution)/shard_map/ppermute | solution.py:22
  106.4 4.2 %collective-permute-done.19.refs_6_ = f32[8,64,128]{2,1,0:T(8,128)S(1)} collective-permute-done((f32[8,64,128]{2,1,0:T(8,128)S(1)}, f32[8,64,128]{2,1,0:T(8,128)S(1)}, u32[]{:S(2)}, u32[]{:S(2)}) %collective-permute-start.19) | collective-permute-done | bytes 262176 | tf_op jit(solution)/shard_map/ppermute | solution.py:22
  112.7 5.0 %collective-permute-done.22.refs_6_ = f32[8,64,128]{2,1,0:T(8,128)S(1)} collective-permute-done((f32[8,64,128]{2,1,0:T(8,128)S(1)}, f32[8,64,128]{2,1,0:T(8,128)S(1)}, u32[]{:S(2)}, u32[]{:S(2)}) %collective-permute-start.22) | collective-permute-done | bytes 262176 | tf_op jit(solution)/shard_map/ppermute | solution.py:22
  (47 shorter events, 40.3 us)
Async XLA Ops:
  0.1 0.7 copy-start
  3.3 2.1 %collective-permute-start = (f32[8,64,128]{2,1,0:T(8,128)S(1)}, f32[8,64,128]{2,1,0:T(8,128)S(1)}, u32[]{:S(2)}, u32[]{:S(2)}) collective-permute-start(f32[8,64,128]{2,1,0:T(8,128)S(1)} %get-tuple-element.74), channel_id=1, source_target_pairs={{0,8},{8,0},{16,24},{24,16},{32,40},{40,32},{48,56},{56,48},{64,72... | collective-permute-start | bytes 786440 | tf_op jit(solution)/shard_map/ppermute | solution.py:22
  7.7 9.0 %collective-permute-start.1 = (f32[8,64,128]{2,1,0:T(8,128)S(1)}, f32[8,64,128]{2,1,0:T(8,128)S(1)}, u32[]{:S(2)}, u32[]{:S(2)}) collective-permute-start(f32[8,64,128]{2,1,0:T(8,128)S(1)} %get-tuple-element.83), channel_id=1, source_target_pairs={{0,16},{8,24},{16,0},{24,8},{32,48},{40,56},{48,32},{56,40},{64,80... | collective-permute-start | bytes 786440 | tf_op jit(solution)/shard_map/ppermute | solution.py:22
  9.7 9.1 %collective-permute-start.2 = (f32[8,64,128]{2,1,0:T(8,128)S(1)}, f32[8,64,128]{2,1,0:T(8,128)S(1)}, u32[]{:S(2)}, u32[]{:S(2)}) collective-permute-start(f32[8,64,128]{2,1,0:T(8,128)S(1)} %get-tuple-element.86), channel_id=1, source_target_pairs={{0,8},{8,0},{16,24},{24,16},{32,40},{40,32},{48,56},{56,48},{64,72... | collective-permute-start | bytes 786440 | tf_op jit(solution)/shard_map/ppermute | solution.py:22
  21.0 12.5 %collective-permute-start.3 = (f32[8,64,128]{2,1,0:T(8,128)S(1)}, f32[8,64,128]{2,1,0:T(8,128)S(1)}, u32[]{:S(2)}, u32[]{:S(2)}) collective-permute-start(f32[8,64,128]{2,1,0:T(8,128)S(1)} %get-tuple-element.89), channel_id=1, source_target_pairs={{0,16},{8,24},{16,0},{24,8},{32,48},{40,56},{48,32},{56,40},{64,80... | collective-permute-start | bytes 786440 | tf_op jit(solution)/shard_map/ppermute | solution.py:22
  22.8 12.9 %collective-permute-start.4 = (f32[8,64,128]{2,1,0:T(8,128)S(1)}, f32[8,64,128]{2,1,0:T(8,128)S(1)}, u32[]{:S(2)}, u32[]{:S(2)}) collective-permute-start(f32[8,64,128]{2,1,0:T(8,128)S(1)} %get-tuple-element.92), channel_id=1, source_target_pairs={{0,8},{8,0},{16,24},{24,16},{32,40},{40,32},{48,56},{56,48},{64,72... | collective-permute-start | bytes 786440 | tf_op jit(solution)/shard_map/ppermute | solution.py:22
  22.8 15.9 %collective-permute-start.5 = (f32[8,64,128]{2,1,0:T(8,128)S(1)}, f32[8,64,128]{2,1,0:T(8,128)S(1)}, u32[]{:S(2)}, u32[]{:S(2)}) collective-permute-start(f32[8,64,128]{2,1,0:T(8,128)S(1)} %get-tuple-element.95), channel_id=1, source_target_pairs={{0,32},{8,40},{16,48},{24,56},{32,0},{40,8},{48,16},{56,24},{64,96... | collective-permute-start | bytes 786440 | tf_op jit(solution)/shard_map/ppermute | solution.py:22
  37.8 6.6 %collective-permute-start.6 = (f32[8,64,128]{2,1,0:T(8,128)S(1)}, f32[8,64,128]{2,1,0:T(8,128)S(1)}, u32[]{:S(2)}, u32[]{:S(2)}) collective-permute-start(f32[8,64,128]{2,1,0:T(8,128)S(1)} %get-tuple-element.98), channel_id=1, source_target_pairs={{0,16},{8,24},{16,0},{24,8},{32,48},{40,56},{48,32},{56,40},{64,80... | collective-permute-start | bytes 786440 | tf_op jit(solution)/shard_map/ppermute | solution.py:22
  40.9 8.2 %collective-permute-start.7 = (f32[8,64,128]{2,1,0:T(8,128)S(1)}, f32[8,64,128]{2,1,0:T(8,128)S(1)}, u32[]{:S(2)}, u32[]{:S(2)}) collective-permute-start(f32[8,64,128]{2,1,0:T(8,128)S(1)} %get-tuple-element.101), channel_id=1, source_target_pairs={{0,64},{8,72},{16,80},{24,88},{32,96},{40,104},{48,112},{56,120},{... | collective-permute-start | bytes 786440 | tf_op jit(solution)/shard_map/ppermute | solution.py:22
  42.0 9.2 %collective-permute-start.8 = (f32[8,64,128]{2,1,0:T(8,128)S(1)}, f32[8,64,128]{2,1,0:T(8,128)S(1)}, u32[]{:S(2)}, u32[]{:S(2)}) collective-permute-start(f32[8,64,128]{2,1,0:T(8,128)S(1)} %get-tuple-element.104), channel_id=1, source_target_pairs={{0,8},{8,0},{16,24},{24,16},{32,40},{40,32},{48,56},{56,48},{64,72... | collective-permute-start | bytes 786440 | tf_op jit(solution)/shard_map/ppermute | solution.py:22
  42.0 15.3 %collective-permute-start.9 = (f32[8,64,128]{2,1,0:T(8,128)S(1)}, f32[8,64,128]{2,1,0:T(8,128)S(1)}, u32[]{:S(2)}, u32[]{:S(2)}) collective-permute-start(f32[8,64,128]{2,1,0:T(8,128)S(1)} %get-tuple-element.107), channel_id=1, source_target_pairs={{0,32},{8,40},{16,48},{24,56},{32,0},{40,8},{48,16},{56,24},{64,96... | collective-permute-start | bytes 786440 | tf_op jit(solution)/shard_map/ppermute | solution.py:22
  53.4 10.5 %collective-permute-start.10 = (f32[8,64,128]{2,1,0:T(8,128)S(1)}, f32[8,64,128]{2,1,0:T(8,128)S(1)}, u32[]{:S(2)}, u32[]{:S(2)}) collective-permute-start(f32[8,64,128]{2,1,0:T(8,128)S(1)} %get-tuple-element.110), channel_id=1, source_target_pairs={{0,16},{8,24},{16,0},{24,8},{32,48},{40,56},{48,32},{56,40},{64,80... | collective-permute-start | bytes 786440 | tf_op jit(solution)/shard_map/ppermute | solution.py:22
  59.5 7.9 %collective-permute-start.11 = (f32[8,64,128]{2,1,0:T(8,128)S(1)}, f32[8,64,128]{2,1,0:T(8,128)S(1)}, u32[]{:S(2)}, u32[]{:S(2)}) collective-permute-start(f32[8,64,128]{2,1,0:T(8,128)S(1)} %get-tuple-element.113), channel_id=1, source_target_pairs={{0,64},{8,72},{16,80},{24,88},{32,96},{40,104},{48,112},{56,120},{... | collective-permute-start | bytes 786440 | tf_op jit(solution)/shard_map/ppermute | solution.py:22
  60.6 10.5 %collective-permute-start.13 = (f32[8,64,128]{2,1,0:T(8,128)S(1)}, f32[8,64,128]{2,1,0:T(8,128)S(1)}, u32[]{:S(2)}, u32[]{:S(2)}) collective-permute-start(f32[8,64,128]{2,1,0:T(8,128)S(1)} %get-tuple-element.114), channel_id=1, source_target_pairs={{0,3},{1,2},{2,1},{3,0},{4,7},{5,6},{6,5},{7,4},{8,11},{9,10},{10,... | collective-permute-start | bytes 786440 | tf_op jit(solution)/shard_map/ppermute | solution.py:22
  63.4 11.7 %collective-permute-start.12 = (f32[8,64,128]{2,1,0:T(8,128)S(1)}, f32[8,64,128]{2,1,0:T(8,128)S(1)}, u32[]{:S(2)}, u32[]{:S(2)}) collective-permute-start(f32[8,64,128]{2,1,0:T(8,128)S(1)} %get-tuple-element.102.refs_2_), channel_id=1, source_target_pairs={{0,3},{1,2},{2,1},{3,0},{4,7},{5,6},{6,5},{7,4},{8,11},{9,10},{10,... | collective-permute-start | bytes 786440 | tf_op jit(solution)/shard_map/ppermute | solution.py:22
  63.8 13.3 %collective-permute-start.14 = (f32[8,64,128]{2,1,0:T(8,128)S(1)}, f32[8,64,128]{2,1,0:T(8,128)S(1)}, u32[]{:S(2)}, u32[]{:S(2)}) collective-permute-start(f32[8,64,128]{2,1,0:T(8,128)S(1)} %get-tuple-element.117), channel_id=1, source_target_pairs={{0,32},{8,40},{16,48},{24,56},{32,0},{40,8},{48,16},{56,24},{64,96... | collective-permute-start | bytes 786440 | tf_op jit(solution)/shard_map/ppermute | solution.py:22
  79.2 8.3 %collective-permute-start.15 = (f32[8,64,128]{2,1,0:T(8,128)S(1)}, f32[8,64,128]{2,1,0:T(8,128)S(1)}, u32[]{:S(2)}, u32[]{:S(2)}) collective-permute-start(f32[8,64,128]{2,1,0:T(8,128)S(1)} %get-tuple-element.120), channel_id=1, source_target_pairs={{0,64},{8,72},{16,80},{24,88},{32,96},{40,104},{48,112},{56,120},{... | collective-permute-start | bytes 786440 | tf_op jit(solution)/shard_map/ppermute | solution.py:22
  80.3 13.3 %collective-permute-start.16 = (f32[8,64,128]{2,1,0:T(8,128)S(1)}, f32[8,64,128]{2,1,0:T(8,128)S(1)}, u32[]{:S(2)}, u32[]{:S(2)}) collective-permute-start(f32[8,64,128]{2,1,0:T(8,128)S(1)} %get-tuple-element.123), channel_id=1, source_target_pairs={{0,32},{8,40},{16,48},{24,56},{32,0},{40,8},{48,16},{56,24},{64,96... | collective-permute-start | bytes 786440 | tf_op jit(solution)/shard_map/ppermute | solution.py:22
  80.3 18.8 %collective-permute-start.17 = (f32[8,64,128]{2,1,0:T(8,128)S(1)}, f32[8,64,128]{2,1,0:T(8,128)S(1)}, u32[]{:S(2)}, u32[]{:S(2)}) collective-permute-start(f32[8,64,128]{2,1,0:T(8,128)S(1)} %get-tuple-element.125), channel_id=1, source_target_pairs={{0,1},{1,0},{2,3},{3,2},{4,5},{5,4},{6,7},{7,6},{8,9},{9,8},{10,11... | collective-permute-start | bytes 786440 | tf_op jit(solution)/shard_map/ppermute | solution.py:22
  94.7 11.7 %collective-permute-start.18 = (f32[8,64,128]{2,1,0:T(8,128)S(1)}, f32[8,64,128]{2,1,0:T(8,128)S(1)}, u32[]{:S(2)}, u32[]{:S(2)}) collective-permute-start(f32[8,64,128]{2,1,0:T(8,128)S(1)} %get-tuple-element.128), channel_id=1, source_target_pairs={{0,64},{8,72},{16,80},{24,88},{32,96},{40,104},{48,112},{56,120},{... | collective-permute-start | bytes 786440 | tf_op jit(solution)/shard_map/ppermute | solution.py:22
  95.8 10.6 %collective-permute-start.20 = (f32[8,64,128]{2,1,0:T(8,128)S(1)}, f32[8,64,128]{2,1,0:T(8,128)S(1)}, u32[]{:S(2)}, u32[]{:S(2)}) collective-permute-start(f32[8,64,128]{2,1,0:T(8,128)S(1)} %get-tuple-element.129), channel_id=1, source_target_pairs={{0,3},{1,2},{2,1},{3,0},{4,7},{5,6},{6,5},{7,4},{8,11},{9,10},{10,... | collective-permute-start | bytes 786440 | tf_op jit(solution)/shard_map/ppermute | solution.py:22
  98.6 12.0 %collective-permute-start.19 = (f32[8,64,128]{2,1,0:T(8,128)S(1)}, f32[8,64,128]{2,1,0:T(8,128)S(1)}, u32[]{:S(2)}, u32[]{:S(2)}) collective-permute-start(f32[8,64,128]{2,1,0:T(8,128)S(1)} %get-tuple-element.121.refs_2_), channel_id=1, source_target_pairs={{0,3},{1,2},{2,1},{3,0},{4,7},{5,6},{6,5},{7,4},{8,11},{9,10},{10,... | collective-permute-start | bytes 786440 | tf_op jit(solution)/shard_map/ppermute | solution.py:22
  100.7 17.0 %collective-permute-start.22 = (f32[8,64,128]{2,1,0:T(8,128)S(1)}, f32[8,64,128]{2,1,0:T(8,128)S(1)}, u32[]{:S(2)}, u32[]{:S(2)}) collective-permute-start(f32[8,64,128]{2,1,0:T(8,128)S(1)} %get-tuple-element.126.refs_2_), channel_id=1, source_target_pairs={{0,4},{1,5},{2,6},{3,7},{4,0},{5,1},{6,2},{7,3},{8,12},{9,13},{10,... | collective-permute-start | bytes 786440 | tf_op jit(solution)/shard_map/ppermute | solution.py:22
  112.6 7.1 %collective-permute-start.21 = (f32[8,64,128]{2,1,0:T(8,128)S(1)}, f32[8,64,128]{2,1,0:T(8,128)S(1)}, u32[]{:S(2)}, u32[]{:S(2)}) collective-permute-start(f32[8,64,128]{2,1,0:T(8,128)S(1)} %get-tuple-element.132), channel_id=1, source_target_pairs={{0,1},{1,0},{2,3},{3,2},{4,5},{5,4},{6,7},{7,6},{8,9},{9,8},{10,11... | collective-permute-start | bytes 786440 | tf_op jit(solution)/shard_map/ppermute | solution.py:22

commit v3 on v0

v3 whole, which is shorter than its diff:
```python
import functools

import jax
import jax.numpy as jnp
from jax import lax
from jax.experimental import pallas as pl
from jax.experimental.pallas import tpu as pltpu
from jax.sharding import PartitionSpec as P

SLOTS = 4

ORDER = [
    ("first",), ("rest",), ("mix", 0, 0), ("load",), ("mix", 0, 1), ("mix", 1, 0),
    ("mix", 1, 1), ("mix", 0, 2), ("mix", 2, 0), ("mix", 1, 2), ("mix", 3, 0),
    ("mix", 0, 3), ("mix", 2, 1), ("mix", 1, 3), ("mix", 3, 1), ("mix", 2, 2), ("mix", 3, 2),
    ("mix", 2, 3), ("far",), ("mix", 3, 3), ("end",),
]


def swap(block, axis, mask):
    count = lax.axis_size(axis)
    return lax.ppermute(block, axis, [(at, at ^ mask) for at in range(count)])


def turn(block):
    middle = block.shape[-1] // 2
    return jnp.concatenate([-block[:, middle:], block[:, :middle]], -1)


def split(block):
    high = block.astype(jnp.bfloat16)
    low = (block - high.astype(jnp.float32)).astype(jnp.bfloat16)
    return high, low


def stack_split(blocks):
    highs, lows = [], []
    for block in blocks:
        high, low = split(block)
        highs += [high, turn(high)]
        lows += [low, turn(low)]
    return jnp.concatenate([jnp.concatenate(highs, 0), jnp.concatenate(lows, 0)], 1)


def halves(bit, half):
    return (1 - bit) * half, bit * half


def slot_chunk(slot):
    return (lax.axis_index("col") >> 1) ^ (SLOTS - 1 - slot)


def leaf_product(source, basis):
    stacked = jnp.concatenate([source, turn(source)], 0)
    return jnp.dot(basis, stacked, preferred_element_type=jnp.float32)


def first_body(mine, outs, *, half):
    rhs_ref, basis_ref = mine
    sent_ref, kept_ref, rhs_to, basis_to, sems = outs
    chunk = slot_chunk(0)
    starts = halves(level_bit(0), half)
    loads = []
    for which, start in enumerate(starts):
        for array, to in ((rhs_ref, rhs_to), (basis_ref, basis_to)):
            load = pltpu.make_async_copy(array.at[pl.ds(start, half), chunk], to.at[which], sems.at[len(loads)])
            load.start()
            loads.append(load)
    for which, out_ref in enumerate((sent_ref, kept_ref)):
        loads[2 * which].wait()
        loads[2 * which + 1].wait()
        for at in range(half):
            out_ref[at] = leaf_product(rhs_to[which, at], basis_to[which, at])


def rest_body(mine, outs, *, half):
    rhs_ref, basis_ref, matrices_ref, ranks_ref = mine
    count = 2 * (SLOTS - 1)
    to_refs, live_ref, matrices_to = outs[:count], outs[count], outs[count + 1]
    rhs_to, basis_to, ranks_to, sems = outs[count + 2 :]
    starts = halves(level_bit(0), half)
    ranks_load = pltpu.make_async_copy(ranks_ref, ranks_to, sems.at[0])
    ranks_load.start()
    loads = []
    for slot in range(1, SLOTS):
        chunk = slot_chunk(slot)
        for at, (array, to) in enumerate(((rhs_ref, rhs_to), (basis_ref, basis_to))):
            load = pltpu.make_async_copy(array.at[:, chunk], to.at[slot - 1], sems.at[2 * slot + at])
            load.start()
            loads.append(load)
    matrices_load = pltpu.make_async_copy(matrices_ref.at[0], matrices_to, sems.at[1])
    matrices_load.start()
    ranks_load.wait()
    levels, leaves, columns = live_ref.shape
    diagonal = lax.broadcasted_iota(jnp.int32, (leaves, leaves), 0) == lax.broadcasted_iota(jnp.int32, (leaves, leaves), 1)
    for level in range(levels):
        spread = jnp.broadcast_to(ranks_to[level, 0], (leaves, leaves)).astype(jnp.float32)
        column = jnp.sum(jnp.where(diagonal, spread, 0.0), axis=1, keepdims=True)
        live_ref[level] = jnp.broadcast_to(column, (leaves, columns)).astype(jnp.int32)
    for slot in range(1, SLOTS):
        loads[2 * slot - 2].wait()
        loads[2 * slot - 1].wait()
        for which, start in enumerate(starts):
            for at in range(half):
                product = leaf_product(rhs_to[slot - 1, start + at], basis_to[slot - 1, start + at])
                to_refs[2 * slot - 2 + which][at] = product
    matrices_load.wait()


def load_body(mine, outs):
    matrices_ref, targets_ref = mine
    tos, targets_to, sems = outs[:-2], outs[-2], outs[-1]
    owned = targets_to.shape[0]
    start = lax.axis_index("col") * owned
    loads = [
        pltpu.make_async_copy(matrices_ref.at[level + 1], to, sems.at[level]) for level, to in enumerate(tos)
    ]
    loads.append(pltpu.make_async_copy(targets_ref.at[0, pl.ds(start, owned)], targets_to, sems.at[len(tos)]))
    for load in loads:
        load.start()
    for load in loads:
        load.wait()


def mix_body(mine, outs, *, level, slot, bit):
    live_ref, matrices_ref, own_ref, partner_ref = mine[:4]
    added = mine[4:]
    half, rank_cap, columns = outs[0].shape
    low_count = 2 << level
    chunk = slot_chunk(slot)
    rows = lax.broadcasted_iota(jnp.int32, (rank_cap, columns), 0)
    for which, (out_ref, start) in enumerate(zip(outs, halves(bit(), half))):
        for pair in range(half // 2):
            j = start // 2 + pair
            stacked = stack_split([own_ref[j], partner_ref[j]])
            first = start + 2 * pair
            place = (first // low_count) * (SLOTS * low_count) + chunk * low_count + first % low_count
            left = jnp.concatenate([matrices_ref[place], matrices_ref[place + 1]], 0)
            both = jnp.dot(left, stacked, preferred_element_type=jnp.float32)
            both = both[:, :columns] + both[:, columns:]
            for s in range(2):
                live = live_ref[level, pl.ds(place + s, 1), :]
                mixed = jnp.where(rows < live, both[s * rank_cap : (s + 1) * rank_cap], 0.0)
                if added:
                    mixed = mixed + added[which][2 * pair + s]
                out_ref[2 * pair + s] = mixed


def far_body(mine, outs):
    for at in range(outs[0].shape[0]):
        outs[0][at] = mine[0][at] + mine[1][at]


def end_body(mine, outs):
    basis_ref, first_ref, second_ref, third_ref = mine
    out_ref = outs[0]
    points = basis_ref.shape[1]
    columns = out_ref.shape[1]
    owned = first_ref.shape[0]
    for at in range(owned):
        total = first_ref[at] + second_ref[at] + third_ref[at]
        both = jnp.dot(basis_ref[at], stack_split([total]), preferred_element_type=jnp.float32)
        both = both[:, :columns] + both[:, columns:]
        out_ref[at * points : (at + 1) * points, :] = both.astype(out_ref.dtype)


def kernel(*refs, body, ins):
    body(refs[1 : 1 + ins], refs[1 + ins :])


def level_bit(level):
    return lax.axis_index("row") >> level & 1


def owner_bit():
    return lax.axis_index("col") & 1


def shards(rhs, leaf_basis, transfer, ranks, out_basis):
    leaves, rank_cap, wide = leaf_basis.shape
    points = wide // 2
    columns = rhs.shape[1]
    levels = transfer.shape[0]
    chunk_leaves = leaves // SLOTS
    half = chunk_leaves // 2
    owned = leaves // lax.axis_size("col")
    in_vmem = lambda array: pltpu.with_memory_space_constraint(array, pltpu.VMEM)
    in_hbm = lambda array: pltpu.with_memory_space_constraint(array, pltpu.HBM)
    sources = in_hbm(rhs.reshape(chunk_leaves, SLOTS, points, columns))
    bases = in_hbm(leaf_basis.reshape(chunk_leaves, SLOTS, rank_cap, wide))
    transfers = in_hbm(transfer.reshape(levels, leaves, rank_cap, 4 * rank_cap))
    half_out = ((half, rank_cap, columns), jnp.float32)
    level_out = ((leaves, rank_cap, 4 * rank_cap), transfer.dtype)

    def run(name, body, arrays, outs, token, scratch=(), from_hbm=False, last=False):
        vmem = pl.BlockSpec(memory_space=pltpu.VMEM)
        anywhere = pl.BlockSpec(memory_space=pl.ANY)
        if not from_hbm:
            arrays = [in_vmem(array) for array in arrays]
        return pl.pallas_call(
            functools.partial(kernel, body=body, ins=len(arrays)),
            in_specs=[anywhere] + [anywhere if from_hbm else vmem] * len(arrays),
            out_specs=[vmem] * len(outs),
            out_shape=[jax.ShapeDtypeStruct(*out) if last else pltpu.VMEM(*out) for out in outs],
            scratch_shapes=scratch,
            cost_estimate=pl.CostEstimate(flops=1 << 33, bytes_accessed=1 << 20, transcendentals=0),
            compiler_params=pltpu.CompilerParams(vmem_limit_bytes=16 * 1024 * 1024),
            name=name,
        )(token, *arrays)

    token = transfers
    sent, kept, added, near = {}, {}, {}, {}
    live = far = targets = result = None
    matrices = []
    for step in ORDER:
        name = "_".join(str(part) for part in step)
        if step[0] == "first":
            scratch = [
                pltpu.VMEM((2, half, points, columns), rhs.dtype),
                pltpu.VMEM((2, half, rank_cap, wide), leaf_basis.dtype),
                pltpu.SemaphoreType.DMA((4,)),
            ]
            body = functools.partial(first_body, half=half)
            sent[0], kept[0] = run(name, body, [sources, bases], [half_out] * 2, token, scratch, True)
            token = kept[0]
        elif step[0] == "rest":
            scratch = [
                pltpu.VMEM((SLOTS - 1, chunk_leaves, points, columns), rhs.dtype),
                pltpu.VMEM((SLOTS - 1, chunk_leaves, rank_cap, wide), leaf_basis.dtype),
                pltpu.VMEM(ranks.shape, ranks.dtype),
                pltpu.SemaphoreType.DMA((2 * SLOTS,)),
            ]
            outs = [half_out] * (2 * SLOTS - 2) + [((levels, leaves, columns), jnp.int32), level_out]
            body = functools.partial(rest_body, half=half)
            made = run(name, body, [sources, bases, transfers, in_hbm(ranks)], outs, token, scratch, True)
            for slot in range(1, SLOTS):
                sent[slot], kept[slot] = made[2 * slot - 2 : 2 * slot]
            live, first_matrices = made[-2:]
            matrices = [first_matrices]
            token = live
        elif step[0] == "load":
            outs = [level_out] * (levels - 1) + [((owned, points, 2 * rank_cap), out_basis.dtype)]
            scratch = [pltpu.SemaphoreType.DMA((levels,))]
            made = run(name, load_body, [transfers, in_hbm(out_basis)], outs, token, scratch, True)
            matrices += made[:-1]
            token = targets = made[-1]
        elif step[0] == "mix":
            level, slot = step[1:]
            last = level == levels - 1
            partner = swap(sent[slot], "row", 1 << level)
            bit = owner_bit if last else functools.partial(level_bit, level + 1)
            body = functools.partial(mix_body, level=level, slot=slot, bit=bit)
            arrays = [live, matrices[level], kept[slot], partner] + (added.get(slot, []) if last else [])
            sent[slot], kept[slot] = run(name, body, arrays, [half_out] * 2, token)
            token = kept[slot]
            if last and slot % 2 == 0:
                added[slot + 1] = [swap(kept[slot], "col", 3), swap(sent[slot], "col", 3)]
            elif last:
                near[slot] = swap(sent[slot], "col", 1)
        elif step[0] == "far":
            (total,) = run(name, far_body, [kept[1], near[1]], [half_out], token)
            far = swap(total, "col", 4)
            token = total
        else:
            out = ((owned * points, columns), jnp.bfloat16)
            (result,) = run(name, end_body, [targets, kept[3], near[3], far], [out], token, last=True)
    return result


def solution(mesh):
    in_specs = (
        P(("row", "col"), None),
        P(("row", "col"), None, None),
        P(None, "row", "col", None, None, None),
        P(None, "row", "col", None),
        P("row", None, None, None),
    )
    out_specs = P(("row", "col"), None)
    return jax.shard_map(shards, mesh=mesh, in_specs=in_specs, out_specs=out_specs, check_vma=False)
```

time: 261 us -> 94.3 us (0.36)
  waiting for transfers between devices: 188 us -> 47.9 us
  matrix products: 24.1 us -> 0 us
  starting transfers between devices: 6.56 us -> 28.1 us
  other arithmetic: 18.2 us -> 0 us
  Pallas kernels: 0 us -> 17.7 us
  between operations: 13.6 us -> 0.26 us
  local copies, waits for them, and re-layouts: 9.72 us -> 0 us
    reduce_scatter x1 -> x0, waiting for transfers between devices: 97.4 us -> none  [shards(): total = lax.psum_scatter(coeff, 'col', scatter_dimension=0, tiled=True)]
    ppermute x4 -> x23, waiting for transfers between devices: 90.8 us -> 47.9 us  [swap(): return lax.ppermute(block, axis, [(at, at ^ mask) for at in range(count)])]
    dot_general x6 -> x0, matrix products: 24.1 us -> none  [the longest x4 18.1 us: mix_level(): jnp.einsum('jskm,jmn->jskn', weights, stacked, precision=lax.Precision.HI...]
    ppermute x4 -> x23, starting transfers between devices: 6.56 us -> 28.1 us  [swap(): return lax.ppermute(block, axis, [(at, at ^ mask) for at in range(count)])]
    pallas_call x0 -> x21, Pallas kernels: none -> 17.7 us  [run(): pl.pallas_call(functools.partial(kernel, body=body, ins=len(arrays)), in_...]
    neg x10 -> x0, other arithmetic: 13.4 us -> none  [complex_stack(): flipped = jnp.concatenate([-block[..., middle:], block[..., :middle]], -1)]
    slice x1 -> x0, local copies, waits for them, and re-layouts: 5.65 us -> none  [shards(): transfer[level, 0, 0]]
    select_n x4 -> x0, other arithmetic: 4.46 us -> none  [mix_level(): return jnp.where(live_rows[..., None], mixed, jnp.float32(0.0))]
  transfers between devices with their start and end apart: 5 -> 23, of which waited for: 4 -> 10; matrix products, arithmetic and copies ran while one was open for 3% -> 0% of each run, Pallas kernels for 0% -> 15%
where the time goes in v3:
time: 94.3 us; the launch traced here: 93.9 us
  waiting for transfers between devices  47.9 us (51%)
  starting transfers between devices  28.1 us (30%)
  Pallas kernels  17.7 us (19%)
    ppermute x23, waiting for transfers between devices, swap(): return lax.ppermute(block, axis, [(at, at ^ mask) for at in range(count)])  47.9 us
    ppermute x23, starting transfers between devices, swap(): return lax.ppermute(block, axis, [(at, at ^ mask) for at in range(count)])  28.1 us
    pallas_call x21, Pallas kernels, run(): pl.pallas_call(functools.partial(kernel, body=body, ins=len(arrays)), in_...  17.7 us
  transfers between devices with their start and end apart: 23, of which 10 were waited for; matrix products, arithmetic and copies ran while one was open for 0% of the time, Pallas kernels for 15%

profile of v3, /device:TPU:8, one launch (start us, length us, event | category | flops | bytes accessed | tf_op | source)
XLA Modules:
  0.0 93.9 jit_solution(10117094480280593952)
XLA Ops:
  0.0 1.8 %first.1 = (f32[8,64,128]{2,1,0:T(8,128)S(1)}, f32[8,64,128]{2,1,0:T(8,128)S(1)}) custom-call(bf16[4,64,64,256]{3,2,1,0:T(8,128)(2,1)} %bitcast.3, bf16[16,4,128,128]{3,2,1,0:T(8,128)(2,1)} %bitcast.6, bf16[16,4,64,256]{3,2,1,0:T(8,128)(2,1)} %bitcast.8), custom_call_target="tpu_custom_call" | custom-call | flops 8589934592 | bytes 1048576 | tf_op jit(solution)/shard_map/first/pallas_call | solution.py:200
  1.9 3.0 %rest.1 = (f32[8,64,128]{2,1,0:T(8,128)S(1)}, f32[8,64,128]{2,1,0:T(8,128)S(1)}, f32[8,64,128]{2,1,0:T(8,128)S(1)}, f32[8,64,128]{2,1,0:T(8,128)S(1)}, f32[8,64,...) custom-call(f32[8,64,128]{2,1,0:T(8,128)S(1)} %get-tuple-element.51., ...), custom_call_target="tpu_custom_call" | custom-call | flops 8589934592 | bytes 1048576 | tf_op jit(solution)/shard_map/rest/pallas_call | solution.py:200
  6.5 2.0 %collective-permute-start.2 = (f32[8,64,128]{2,1,0:T(8,128)S(1)}, f32[8,64,128]{2,1,0:T(8,128)S(1)}, u32[]{:S(2)}, u32[]{:S(2)}) collective-permute-start(f32[8,64,128]{2,1,0:T(8,128)S(1)} %get-tuple-element.61), channel_id=1, source_target_pairs={{0,16},{8,24},{16,0},{24,8},{32,48},{40,56},{48,32},{56,40},{64,80... | collective-permute-start | bytes 786440 | tf_op jit(solution)/shard_map/ppermute | solution.py:22
  8.5 2.9 %load.1 = (bf16[64,64,256]{2,1,0:T(8,128)(2,1)S(1)}, bf16[64,64,256]{2,1,0:T(8,128)(2,1)S(1)}, bf16[64,64,256]{2,1,0:T(8,128)(2,1)S(1)}, bf16[8,128,128]{2,1,0:T(8,128)(2,1)S(1)}) custom-call(f32[8,64,128]{2,1,0:T(8,128)S(1)} %get-tuple-element.55.refs_0_.refs_3_, bf16[4,64,64,256]{3,2,1,0:T(8,128)(2,1)} %bitcast.5, bf16[1,64,128,128]{3,2,1,0:T(8,128)(2,1)} %refs_2_.1), custom_call_target="tpu_custom_call" | custom-call | flops 8589934592 | bytes 1048576 | tf_op jit(solution)/shard_map/load/pallas_call | solution.py:200
  12.2 3.4 %collective-permute-done.2.refs_4_ = f32[8,64,128]{2,1,0:T(8,128)S(1)} collective-permute-done((f32[8,64,128]{2,1,0:T(8,128)S(1)}, f32[8,64,128]{2,1,0:T(8,128)S(1)}, u32[]{:S(2)}, u32[]{:S(2)}) %collective-permute-start.2) | collective-permute-done | bytes 262176 | tf_op jit(solution)/shard_map/ppermute | solution.py:22
  16.2 3.4 %collective-permute-start.5 = (f32[8,64,128]{2,1,0:T(8,128)S(1)}, f32[8,64,128]{2,1,0:T(8,128)S(1)}, u32[]{:S(2)}, u32[]{:S(2)}) collective-permute-start(f32[8,64,128]{2,1,0:T(8,128)S(1)} %get-tuple-element.69), channel_id=1, source_target_pairs={{0,32},{8,40},{16,48},{24,56},{32,0},{40,8},{48,16},{56,24},{64,96... | collective-permute-start | bytes 786440 | tf_op jit(solution)/shard_map/ppermute | solution.py:22
  19.5 5.3 %collective-permute-done.3.refs_4_ = f32[8,64,128]{2,1,0:T(8,128)S(1)} collective-permute-done((f32[8,64,128]{2,1,0:T(8,128)S(1)}, f32[8,64,128]{2,1,0:T(8,128)S(1)}, u32[]{:S(2)}, u32[]{:S(2)}) %collective-permute-start.3) | collective-permute-done | bytes 262176 | tf_op jit(solution)/shard_map/ppermute | solution.py:22
  26.1 2.3 %collective-permute-start.9 = (f32[8,64,128]{2,1,0:T(8,128)S(1)}, f32[8,64,128]{2,1,0:T(8,128)S(1)}, u32[]{:S(2)}, u32[]{:S(2)}) collective-permute-start(f32[8,64,128]{2,1,0:T(8,128)S(1)} %get-tuple-element.79), channel_id=1, source_target_pairs={{0,32},{8,40},{16,48},{24,56},{32,0},{40,8},{48,16},{56,24},{64,96... | collective-permute-start | bytes 786440 | tf_op jit(solution)/shard_map/ppermute | solution.py:22
  28.4 3.4 %collective-permute-done.5.refs_4_ = f32[8,64,128]{2,1,0:T(8,128)S(1)} collective-permute-done((f32[8,64,128]{2,1,0:T(8,128)S(1)}, f32[8,64,128]{2,1,0:T(8,128)S(1)}, u32[]{:S(2)}, u32[]{:S(2)}) %collective-permute-start.5) | collective-permute-done | bytes 262176 | tf_op jit(solution)/shard_map/ppermute | solution.py:22
  32.4 1.7 %collective-permute-start.7 = (f32[8,64,128]{2,1,0:T(8,128)S(1)}, f32[8,64,128]{2,1,0:T(8,128)S(1)}, u32[]{:S(2)}, u32[]{:S(2)}) collective-permute-start(f32[8,64,128]{2,1,0:T(8,128)S(1)} %get-tuple-element.74), channel_id=1, source_target_pairs={{0,64},{8,72},{16,80},{24,88},{32,96},{40,104},{48,112},{56,120},{... | collective-permute-start | bytes 786440 | tf_op jit(solution)/shard_map/ppermute | solution.py:22
  34.0 5.4 %collective-permute-done.6.refs_4_ = f32[8,64,128]{2,1,0:T(8,128)S(1)} collective-permute-done((f32[8,64,128]{2,1,0:T(8,128)S(1)}, f32[8,64,128]{2,1,0:T(8,128)S(1)}, u32[]{:S(2)}, u32[]{:S(2)}) %collective-permute-start.6) | collective-permute-done | bytes 262176 | tf_op jit(solution)/shard_map/ppermute | solution.py:22
  40.7 3.0 %collective-permute-start.12 = (f32[8,64,128]{2,1,0:T(8,128)S(1)}, f32[8,64,128]{2,1,0:T(8,128)S(1)}, u32[]{:S(2)}, u32[]{:S(2)}) collective-permute-start(f32[8,64,128]{2,1,0:T(8,128)S(1)} %get-tuple-element.75.refs_0_), channel_id=1, source_target_pairs={{0,3},{1,2},{2,1},{3,0},{4,7},{5,6},{6,5},{7,4},{8,11},{9,10},{10,... | collective-permute-start | bytes 786440 | tf_op jit(solution)/shard_map/ppermute | solution.py:22
  44.3 2.4 %collective-permute-start.10 = (f32[8,64,128]{2,1,0:T(8,128)S(1)}, f32[8,64,128]{2,1,0:T(8,128)S(1)}, u32[]{:S(2)}, u32[]{:S(2)}) collective-permute-start(f32[8,64,128]{2,1,0:T(8,128)S(1)} %get-tuple-element.81), channel_id=1, source_target_pairs={{0,16},{8,24},{16,0},{24,8},{32,48},{40,56},{48,32},{56,40},{64,80... | collective-permute-start | bytes 786440 | tf_op jit(solution)/shard_map/ppermute | solution.py:22
  47.8 1.1 %collective-permute-start.11 = (f32[8,64,128]{2,1,0:T(8,128)S(1)}, f32[8,64,128]{2,1,0:T(8,128)S(1)}, u32[]{:S(2)}, u32[]{:S(2)}) collective-permute-start(f32[8,64,128]{2,1,0:T(8,128)S(1)} %get-tuple-element.83), channel_id=1, source_target_pairs={{0,64},{8,72},{16,80},{24,88},{32,96},{40,104},{48,112},{56,120},{... | collective-permute-start | bytes 786440 | tf_op jit(solution)/shard_map/ppermute | solution.py:22
  48.9 8.9 %collective-permute-done.10.refs_4_ = f32[8,64,128]{2,1,0:T(8,128)S(1)} collective-permute-done((f32[8,64,128]{2,1,0:T(8,128)S(1)}, f32[8,64,128]{2,1,0:T(8,128)S(1)}, u32[]{:S(2)}, u32[]{:S(2)}) %collective-permute-start.10) | collective-permute-done | bytes 262176 | tf_op jit(solution)/shard_map/ppermute | solution.py:22
  60.1 0.6 collective-permute-start.16
  60.7 0.6 collective-permute-start.17
  61.3 5.0 %collective-permute-done.15.refs_4_ = f32[8,64,128]{2,1,0:T(8,128)S(1)} collective-permute-done((f32[8,64,128]{2,1,0:T(8,128)S(1)}, f32[8,64,128]{2,1,0:T(8,128)S(1)}, u32[]{:S(2)}, u32[]{:S(2)}) %collective-permute-start.15) | collective-permute-done | bytes 262176 | tf_op jit(solution)/shard_map/ppermute | solution.py:22
  67.4 5.7 %collective-permute-done.16.refs_4_ = f32[8,64,128]{2,1,0:T(8,128)S(1)} collective-permute-done((f32[8,64,128]{2,1,0:T(8,128)S(1)}, f32[8,64,128]{2,1,0:T(8,128)S(1)}, u32[]{:S(2)}, u32[]{:S(2)}) %collective-permute-start.16) | collective-permute-done | bytes 262176 | tf_op jit(solution)/shard_map/ppermute | solution.py:22
  73.6 1.7 %collective-permute-start.18 = (f32[8,64,128]{2,1,0:T(8,128)S(1)}, f32[8,64,128]{2,1,0:T(8,128)S(1)}, u32[]{:S(2)}, u32[]{:S(2)}) collective-permute-start(f32[8,64,128]{2,1,0:T(8,128)S(1)} %get-tuple-element.93), channel_id=1, source_target_pairs={{0,64},{8,72},{16,80},{24,88},{32,96},{40,104},{48,112},{56,120},{... | collective-permute-start | bytes 786440 | tf_op jit(solution)/shard_map/ppermute | solution.py:22
  75.7 5.9 %collective-permute-start.22 = (f32[8,64,128]{2,1,0:T(8,128)S(1)}, f32[8,64,128]{2,1,0:T(8,128)S(1)}, u32[]{:S(2)}, u32[]{:S(2)}) collective-permute-start(f32[8,64,128]{2,1,0:T(8,128)S(1)} %far.1.refs_0_), channel_id=1, source_target_pairs={{0,4},{1,5},{2,6},{3,7},{4,0},{5,1},{6,2},{7,3},{8,12},{9,13},{10,... | collective-permute-start | bytes 786440 | tf_op jit(solution)/shard_map/ppermute | solution.py:22
  81.9 2.4 %collective-permute-done.20.refs_6_ = f32[8,64,128]{2,1,0:T(8,128)S(1)} collective-permute-done((f32[8,64,128]{2,1,0:T(8,128)S(1)}, f32[8,64,128]{2,1,0:T(8,128)S(1)}, u32[]{:S(2)}, u32[]{:S(2)}) %collective-permute-start.20) | collective-permute-done | bytes 262176 | tf_op jit(solution)/shard_map/ppermute | solution.py:22
  85.0 7.8 %collective-permute-done.22.refs_4_ = f32[8,64,128]{2,1,0:T(8,128)S(1)} collective-permute-done((f32[8,64,128]{2,1,0:T(8,128)S(1)}, f32[8,64,128]{2,1,0:T(8,128)S(1)}, u32[]{:S(2)}, u32[]{:S(2)}) %collective-permute-start.22) | collective-permute-done | bytes 262176 | tf_op jit(solution)/shard_map/ppermute | solution.py:22
  92.9 1.1 %end.1 = bf16[1024,128]{1,0:T(8,128)(2,1)} custom-call(f32[8,64,128]{2,1,0:T(8,128)S(1)} %get-tuple-element.95.refs_0_.refs_2_, bf16[8,128,128]{2,1,0:T(8,128)(2,1)S(1)} %get-tuple-element.56.refs_0_.refs_1_, f32[8,64,128]{2,1,0:T(8,128)S(1)} %get-tuple-element.95.refs_0_.refs_2_, f32[8,64,128]{2,1,0:T(8,128)S(1)} %collective-permute-done.21.refs_3_, ...), custom_call_target="tpu_custom_call" | custom-call | flops 8589934592 | bytes 1048576 | tf_op jit(solution)/shard_map/end/pallas_call | solution.py:200
  (43 shorter events, 12.9 us)
Async XLA Ops:
  1.8 4.2 %collective-permute-start = (f32[8,64,128]{2,1,0:T(8,128)S(1)}, f32[8,64,128]{2,1,0:T(8,128)S(1)}, u32[]{:S(2)}, u32[]{:S(2)}) collective-permute-start(f32[8,64,128]{2,1,0:T(8,128)S(1)} %get-tuple-element.54), channel_id=1, source_target_pairs={{0,8},{8,0},{16,24},{24,16},{32,40},{40,32},{48,56},{56,48},{64,72... | collective-permute-start | bytes 786440 | tf_op jit(solution)/shard_map/ppermute | solution.py:22
  4.9 6.6 %collective-permute-start.1 = (f32[8,64,128]{2,1,0:T(8,128)S(1)}, f32[8,64,128]{2,1,0:T(8,128)S(1)}, u32[]{:S(2)}, u32[]{:S(2)}) collective-permute-start(f32[8,64,128]{2,1,0:T(8,128)S(1)} %get-tuple-element.58), channel_id=1, source_target_pairs={{0,8},{8,0},{16,24},{24,16},{32,40},{40,32},{48,56},{56,48},{64,72... | collective-permute-start | bytes 786440 | tf_op jit(solution)/shard_map/ppermute | solution.py:22
  5.5 20.0 %collective-permute-start.4 = (f32[8,64,128]{2,1,0:T(8,128)S(1)}, f32[8,64,128]{2,1,0:T(8,128)S(1)}, u32[]{:S(2)}, u32[]{:S(2)}) collective-permute-start(f32[8,64,128]{2,1,0:T(8,128)S(1)} %get-tuple-element.66), channel_id=1, source_target_pairs={{0,8},{8,0},{16,24},{24,16},{32,40},{40,32},{48,56},{56,48},{64,72... | collective-permute-start | bytes 786440 | tf_op jit(solution)/shard_map/ppermute | solution.py:22
  5.6 38.2 %collective-permute-start.8 = (f32[8,64,128]{2,1,0:T(8,128)S(1)}, f32[8,64,128]{2,1,0:T(8,128)S(1)}, u32[]{:S(2)}, u32[]{:S(2)}) collective-permute-start(f32[8,64,128]{2,1,0:T(8,128)S(1)} %get-tuple-element.77), channel_id=1, source_target_pairs={{0,8},{8,0},{16,24},{24,16},{32,40},{40,32},{48,56},{56,48},{64,72... | collective-permute-start | bytes 786440 | tf_op jit(solution)/shard_map/ppermute | solution.py:22
  6.5 9.1 %collective-permute-start.2 = (f32[8,64,128]{2,1,0:T(8,128)S(1)}, f32[8,64,128]{2,1,0:T(8,128)S(1)}, u32[]{:S(2)}, u32[]{:S(2)}) collective-permute-start(f32[8,64,128]{2,1,0:T(8,128)S(1)} %get-tuple-element.61), channel_id=1, source_target_pairs={{0,16},{8,24},{16,0},{24,8},{32,48},{40,56},{48,32},{56,40},{64,80... | collective-permute-start | bytes 786440 | tf_op jit(solution)/shard_map/ppermute | solution.py:22
  12.0 12.8 %collective-permute-start.3 = (f32[8,64,128]{2,1,0:T(8,128)S(1)}, f32[8,64,128]{2,1,0:T(8,128)S(1)}, u32[]{:S(2)}, u32[]{:S(2)}) collective-permute-start(f32[8,64,128]{2,1,0:T(8,128)S(1)} %get-tuple-element.63), channel_id=1, source_target_pairs={{0,16},{8,24},{16,0},{24,8},{32,48},{40,56},{48,32},{56,40},{64,80... | collective-permute-start | bytes 786440 | tf_op jit(solution)/shard_map/ppermute | solution.py:22
  16.2 15.6 %collective-permute-start.5 = (f32[8,64,128]{2,1,0:T(8,128)S(1)}, f32[8,64,128]{2,1,0:T(8,128)S(1)}, u32[]{:S(2)}, u32[]{:S(2)}) collective-permute-start(f32[8,64,128]{2,1,0:T(8,128)S(1)} %get-tuple-element.69), channel_id=1, source_target_pairs={{0,32},{8,40},{16,48},{24,56},{32,0},{40,8},{48,16},{56,24},{64,96... | collective-permute-start | bytes 786440 | tf_op jit(solution)/shard_map/ppermute | solution.py:22
  26.0 13.4 %collective-permute-start.6 = (f32[8,64,128]{2,1,0:T(8,128)S(1)}, f32[8,64,128]{2,1,0:T(8,128)S(1)}, u32[]{:S(2)}, u32[]{:S(2)}) collective-permute-start(f32[8,64,128]{2,1,0:T(8,128)S(1)} %get-tuple-element.71), channel_id=1, source_target_pairs={{0,16},{8,24},{16,0},{24,8},{32,48},{40,56},{48,32},{56,40},{64,80... | collective-permute-start | bytes 786440 | tf_op jit(solution)/shard_map/ppermute | solution.py:22
  26.1 21.1 %collective-permute-start.9 = (f32[8,64,128]{2,1,0:T(8,128)S(1)}, f32[8,64,128]{2,1,0:T(8,128)S(1)}, u32[]{:S(2)}, u32[]{:S(2)}) collective-permute-start(f32[8,64,128]{2,1,0:T(8,128)S(1)} %get-tuple-element.79), channel_id=1, source_target_pairs={{0,32},{8,40},{16,48},{24,56},{32,0},{40,8},{48,16},{56,24},{64,96... | collective-permute-start | bytes 786440 | tf_op jit(solution)/shard_map/ppermute | solution.py:22
  32.4 7.8 %collective-permute-start.7 = (f32[8,64,128]{2,1,0:T(8,128)S(1)}, f32[8,64,128]{2,1,0:T(8,128)S(1)}, u32[]{:S(2)}, u32[]{:S(2)}) collective-permute-start(f32[8,64,128]{2,1,0:T(8,128)S(1)} %get-tuple-element.74), channel_id=1, source_target_pairs={{0,64},{8,72},{16,80},{24,88},{32,96},{40,104},{48,112},{56,120},{... | collective-permute-start | bytes 786440 | tf_op jit(solution)/shard_map/ppermute | solution.py:22
  40.0 18.9 %collective-permute-start.14 = (f32[8,64,128]{2,1,0:T(8,128)S(1)}, f32[8,64,128]{2,1,0:T(8,128)S(1)}, u32[]{:S(2)}, u32[]{:S(2)}) collective-permute-start(f32[8,64,128]{2,1,0:T(8,128)S(1)} %get-tuple-element.86), channel_id=1, source_target_pairs={{0,32},{8,40},{16,48},{24,56},{32,0},{40,8},{48,16},{56,24},{64,96... | collective-permute-start | bytes 786440 | tf_op jit(solution)/shard_map/ppermute | solution.py:22
  40.7 17.7 %collective-permute-start.12 = (f32[8,64,128]{2,1,0:T(8,128)S(1)}, f32[8,64,128]{2,1,0:T(8,128)S(1)}, u32[]{:S(2)}, u32[]{:S(2)}) collective-permute-start(f32[8,64,128]{2,1,0:T(8,128)S(1)} %get-tuple-element.75.refs_0_), channel_id=1, source_target_pairs={{0,3},{1,2},{2,1},{3,0},{4,7},{5,6},{6,5},{7,4},{8,11},{9,10},{10,... | collective-permute-start | bytes 786440 | tf_op jit(solution)/shard_map/ppermute | solution.py:22
  44.3 13.5 %collective-permute-start.10 = (f32[8,64,128]{2,1,0:T(8,128)S(1)}, f32[8,64,128]{2,1,0:T(8,128)S(1)}, u32[]{:S(2)}, u32[]{:S(2)}) collective-permute-start(f32[8,64,128]{2,1,0:T(8,128)S(1)} %get-tuple-element.81), channel_id=1, source_target_pairs={{0,16},{8,24},{16,0},{24,8},{32,48},{40,56},{48,32},{56,40},{64,80... | collective-permute-start | bytes 786440 | tf_op jit(solution)/shard_map/ppermute | solution.py:22
  46.7 11.6 %collective-permute-start.13 = (f32[8,64,128]{2,1,0:T(8,128)S(1)}, f32[8,64,128]{2,1,0:T(8,128)S(1)}, u32[]{:S(2)}, u32[]{:S(2)}) collective-permute-start(f32[8,64,128]{2,1,0:T(8,128)S(1)} %get-tuple-element.84), channel_id=1, source_target_pairs={{0,3},{1,2},{2,1},{3,0},{4,7},{5,6},{6,5},{7,4},{8,11},{9,10},{10,... | collective-permute-start | bytes 786440 | tf_op jit(solution)/shard_map/ppermute | solution.py:22
  47.8 10.6 %collective-permute-start.11 = (f32[8,64,128]{2,1,0:T(8,128)S(1)}, f32[8,64,128]{2,1,0:T(8,128)S(1)}, u32[]{:S(2)}, u32[]{:S(2)}) collective-permute-start(f32[8,64,128]{2,1,0:T(8,128)S(1)} %get-tuple-element.83), channel_id=1, source_target_pairs={{0,64},{8,72},{16,80},{24,88},{32,96},{40,104},{48,112},{56,120},{... | collective-permute-start | bytes 786440 | tf_op jit(solution)/shard_map/ppermute | solution.py:22
  59.5 6.8 %collective-permute-start.15 = (f32[8,64,128]{2,1,0:T(8,128)S(1)}, f32[8,64,128]{2,1,0:T(8,128)S(1)}, u32[]{:S(2)}, u32[]{:S(2)}) collective-permute-start(f32[8,64,128]{2,1,0:T(8,128)S(1)} %get-tuple-element.88), channel_id=1, source_target_pairs={{0,64},{8,72},{16,80},{24,88},{32,96},{40,104},{48,112},{56,120},{... | collective-permute-start | bytes 786440 | tf_op jit(solution)/shard_map/ppermute | solution.py:22
  60.1 13.0 %collective-permute-start.16 = (f32[8,64,128]{2,1,0:T(8,128)S(1)}, f32[8,64,128]{2,1,0:T(8,128)S(1)}, u32[]{:S(2)}, u32[]{:S(2)}) collective-permute-start(f32[8,64,128]{2,1,0:T(8,128)S(1)} %get-tuple-element.90), channel_id=1, source_target_pairs={{0,32},{8,40},{16,48},{24,56},{32,0},{40,8},{48,16},{56,24},{64,96... | collective-permute-start | bytes 786440 | tf_op jit(solution)/shard_map/ppermute | solution.py:22
  60.7 14.9 %collective-permute-start.17 = (f32[8,64,128]{2,1,0:T(8,128)S(1)}, f32[8,64,128]{2,1,0:T(8,128)S(1)}, u32[]{:S(2)}, u32[]{:S(2)}) collective-permute-start(f32[8,64,128]{2,1,0:T(8,128)S(1)} %get-tuple-element.92), channel_id=1, source_target_pairs={{0,1},{1,0},{2,3},{3,2},{4,5},{5,4},{6,7},{7,6},{8,9},{9,8},{10,11... | collective-permute-start | bytes 786440 | tf_op jit(solution)/shard_map/ppermute | solution.py:22
  66.9 17.4 %collective-permute-start.19 = (f32[8,64,128]{2,1,0:T(8,128)S(1)}, f32[8,64,128]{2,1,0:T(8,128)S(1)}, u32[]{:S(2)}, u32[]{:S(2)}) collective-permute-start(f32[8,64,128]{2,1,0:T(8,128)S(1)} %get-tuple-element.89.refs_0_), channel_id=1, source_target_pairs={{0,3},{1,2},{2,1},{3,0},{4,7},{5,6},{6,5},{7,4},{8,11},{9,10},{10,... | collective-permute-start | bytes 786440 | tf_op jit(solution)/shard_map/ppermute | solution.py:22
  73.6 8.3 %collective-permute-start.18 = (f32[8,64,128]{2,1,0:T(8,128)S(1)}, f32[8,64,128]{2,1,0:T(8,128)S(1)}, u32[]{:S(2)}, u32[]{:S(2)}) collective-permute-start(f32[8,64,128]{2,1,0:T(8,128)S(1)} %get-tuple-element.93), channel_id=1, source_target_pairs={{0,64},{8,72},{16,80},{24,88},{32,96},{40,104},{48,112},{56,120},{... | collective-permute-start | bytes 786440 | tf_op jit(solution)/shard_map/ppermute | solution.py:22
  75.3 9.1 %collective-permute-start.20 = (f32[8,64,128]{2,1,0:T(8,128)S(1)}, f32[8,64,128]{2,1,0:T(8,128)S(1)}, u32[]{:S(2)}, u32[]{:S(2)}) collective-permute-start(f32[8,64,128]{2,1,0:T(8,128)S(1)} %get-tuple-element.94), channel_id=1, source_target_pairs={{0,3},{1,2},{2,1},{3,0},{4,7},{5,6},{6,5},{7,4},{8,11},{9,10},{10,... | collective-permute-start | bytes 786440 | tf_op jit(solution)/shard_map/ppermute | solution.py:22
  75.7 17.1 %collective-permute-start.22 = (f32[8,64,128]{2,1,0:T(8,128)S(1)}, f32[8,64,128]{2,1,0:T(8,128)S(1)}, u32[]{:S(2)}, u32[]{:S(2)}) collective-permute-start(f32[8,64,128]{2,1,0:T(8,128)S(1)} %far.1.refs_0_), channel_id=1, source_target_pairs={{0,4},{1,5},{2,6},{3,7},{4,0},{5,1},{6,2},{7,3},{8,12},{9,13},{10,... | collective-permute-start | bytes 786440 | tf_op jit(solution)/shard_map/ppermute | solution.py:22
  84.9 7.9 %collective-permute-start.21 = (f32[8,64,128]{2,1,0:T(8,128)S(1)}, f32[8,64,128]{2,1,0:T(8,128)S(1)}, u32[]{:S(2)}, u32[]{:S(2)}) collective-permute-start(f32[8,64,128]{2,1,0:T(8,128)S(1)} %get-tuple-element.96), channel_id=1, source_target_pairs={{0,1},{1,0},{2,3},{3,2},{4,5},{5,4},{6,7},{7,6},{8,9},{9,8},{10,11... | collective-permute-start | bytes 786440 | tf_op jit(solution)/shard_map/ppermute | solution.py:22

commit v4 on v3

v4 whole, which is shorter than its diff:
```python
import functools

import jax
import jax.numpy as jnp
from jax import lax
from jax.experimental import pallas as pl
from jax.experimental.pallas import tpu as pltpu
from jax.sharding import PartitionSpec as P

SLOTS = 4
LEVELS = 4

ORDER = [
    ('first',),
    ('tables',),
    ('mix', 0, 0, ('sent_a', 'sent_b', 'kept')),
    ('rest',),
    ('mix', 1, 0, ('sent',)),
    ('mix', 1, 0, ('kept',)),
    ('mix', 0, 1, ('sent', 'kept')),
    ('load',),
    ('mix', 1, 1, ('sent', 'kept')),
    ('mix', 0, 2, ('sent', 'kept')),
    ('mix', 2, 0, ('sent', 'kept')),
    ('mix', 0, 3, ('sent', 'kept'), 2),
    ('mix', 1, 2, ('sent', 'kept')),
    ('mix', 3, 0, ('kept_sent',)),
    ('mix', 2, 1, ('sent', 'kept')),
    ('mix', 1, 3, ('sent_a', 'sent_b', 'kept')),
    ('mix', 2, 2, ('sent', 'kept')),
    ('mix', 3, 1, ('sent', 'kept')),
    ('mix', 2, 3, ('sent',)),
    ('mix', 3, 2, ('kept',)),
    ('far',),
    ('mix', 2, 3, ('kept',)),
    ('mix', 3, 2, ('sent',)),
    ('targets',),
    ('mix', 3, 3, ('sent',)),
    ('mix', 3, 3, ('kept',)),
    ('end',),
]


def swap(block, axis, mask):
    count = lax.axis_size(axis)
    return lax.ppermute(block, axis, [(at, at ^ mask) for at in range(count)])


def turn(block):
    middle = block.shape[-1] // 2
    return jnp.concatenate([-block[:, middle:], block[:, :middle]], -1)


def split(block):
    high = block.astype(jnp.bfloat16)
    low = (block - high.astype(jnp.float32)).astype(jnp.bfloat16)
    return high, low


def stack_split(blocks):
    highs, lows = [], []
    for block in blocks:
        high, low = split(block)
        highs += [high, turn(high)]
        lows += [low, turn(low)]
    return jnp.concatenate([jnp.concatenate(highs, 0), jnp.concatenate(lows, 0)], 1)


def halves(bit, half):
    return (1 - bit) * half, bit * half


def piece_range(piece, level, half):
    bit = owner_bit() if level == LEVELS - 1 else level_bit(level + 1)
    sent, kept = halves(bit, half)
    if piece == "kept":
        return kept, half
    if piece == "sent":
        return sent, half
    first, second = halves(level_bit(level + 2), half // 2)
    return sent + (first if piece == "sent_a" else second), half // 2


def slot_chunk(slot):
    return (lax.axis_index("col") >> 1) ^ (SLOTS - 1 - slot)


def leaf_product(source, basis):
    stacked = jnp.concatenate([source, turn(source)], 0)
    return jnp.dot(basis, stacked, preferred_element_type=jnp.float32)


def first_body(mine, outs, *, half):
    rhs_ref, basis_ref = mine
    sent_ref, kept_ref, rhs_to, basis_to, sems = outs
    chunk = slot_chunk(0)
    starts = halves(level_bit(0), half)
    loads = []
    for which, start in enumerate(starts):
        for array, to in ((rhs_ref, rhs_to), (basis_ref, basis_to)):
            load = pltpu.make_async_copy(array.at[pl.ds(start, half), chunk], to.at[which], sems.at[len(loads)])
            load.start()
            loads.append(load)
    for which, out_ref in enumerate((sent_ref, kept_ref)):
        loads[2 * which].wait()
        loads[2 * which + 1].wait()
        for at in range(half):
            out_ref[at] = leaf_product(rhs_to[which, at], basis_to[which, at])


def tables_body(mine, outs):
    matrices_ref, ranks_ref = mine
    live_ref, matrices_to, ranks_to, sems = outs
    ranks_load = pltpu.make_async_copy(ranks_ref, ranks_to, sems.at[0])
    ranks_load.start()
    matrices_load = pltpu.make_async_copy(matrices_ref.at[0], matrices_to, sems.at[1])
    matrices_load.start()
    ranks_load.wait()
    levels, leaves, columns = live_ref.shape
    diagonal = lax.broadcasted_iota(jnp.int32, (leaves, leaves), 0) == lax.broadcasted_iota(jnp.int32, (leaves, leaves), 1)
    for level in range(levels):
        spread = jnp.broadcast_to(ranks_to[level, 0], (leaves, leaves)).astype(jnp.float32)
        column = jnp.sum(jnp.where(diagonal, spread, 0.0), axis=1, keepdims=True)
        live_ref[level] = jnp.broadcast_to(column, (leaves, columns)).astype(jnp.int32)
    matrices_load.wait()


def rest_body(mine, outs, *, half):
    rhs_ref, basis_ref, matrices_ref = mine
    sent_ref, kept_ref, matrices_to, rhs_to, basis_to, sems = outs
    starts = halves(level_bit(0), half)
    loads = []
    for slot in range(1, SLOTS):
        chunk = slot_chunk(slot)
        for at, (array, to) in enumerate(((rhs_ref, rhs_to), (basis_ref, basis_to))):
            load = pltpu.make_async_copy(array.at[:, chunk], to.at[slot - 1], sems.at[2 * slot + at])
            load.start()
            loads.append(load)
    matrices_load = pltpu.make_async_copy(matrices_ref.at[1], matrices_to, sems.at[0])
    matrices_load.start()
    for slot in range(1, SLOTS):
        loads[2 * slot - 2].wait()
        loads[2 * slot - 1].wait()
        for to_ref, start in zip((sent_ref, kept_ref), starts):
            for at in range(half):
                product = leaf_product(rhs_to[slot - 1, start + at], basis_to[slot - 1, start + at])
                to_ref[(slot - 1) * half + at] = product
    matrices_load.wait()


def load_body(mine, outs):
    tos, sems = outs[:-1], outs[-1]
    loads = [
        pltpu.make_async_copy(mine[0].at[level + 2], to, sems.at[level]) for level, to in enumerate(tos)
    ]
    for load in loads:
        load.start()
    for load in loads:
        load.wait()


def targets_body(mine, outs):
    to, sem = outs
    owned = to.shape[0]
    load = pltpu.make_async_copy(mine[0].at[0, pl.ds(lax.axis_index("col") * owned, owned)], to, sem)
    load.start()
    load.wait()


def mix_body(mine, outs, *, level, slot, pieces, half, offset, in_parts):
    live_ref, matrices_ref, own_ref, partner_ref = mine[:4]
    added = mine[4:]
    rank_cap, columns = outs[0].shape[1:]
    low_count = 2 << level
    chunk = slot_chunk(slot)
    rows = lax.broadcasted_iota(jnp.int32, (rank_cap, columns), 0)
    if pieces == ("kept_sent",):
        pieces, outs = ("kept", "sent"), (outs[0].at[pl.ds(0, half)], outs[0].at[pl.ds(half, half)])
    for piece, out_ref in zip(pieces, outs):
        start, count = piece_range(piece, level, half)
        for pair in range(count // 2):
            j = start // 2 + pair
            partner = partner_ref[pair if in_parts else offset + j]
            stacked = stack_split([own_ref[offset + j], partner])
            first = start + 2 * pair
            place = (first // low_count) * (SLOTS * low_count) + chunk * low_count + first % low_count
            left = jnp.concatenate([matrices_ref[place], matrices_ref[place + 1]], 0)
            both = jnp.dot(left, stacked, preferred_element_type=jnp.float32)
            both = both[:, :columns] + both[:, columns:]
            for s in range(2):
                live = live_ref[level, pl.ds(place + s, 1), :]
                mixed = jnp.where(rows < live, both[s * rank_cap : (s + 1) * rank_cap], 0.0)
                if added and added[0].shape[0] > half:
                    mixed = mixed + added[0][(half if piece == "kept" else 0) + 2 * pair + s]
                elif added:
                    mixed = mixed + added[0][2 * pair + s]
                out_ref[2 * pair + s] = mixed


def far_body(mine, outs):
    for at in range(outs[0].shape[0]):
        outs[0][at] = mine[0][at] + mine[1][at]


def end_body(mine, outs):
    basis_ref, *summed = mine
    out_ref = outs[0]
    points = basis_ref.shape[1]
    columns = out_ref.shape[1]
    for at in range(basis_ref.shape[0]):
        total = summed[0][at]
        for other in summed[1:]:
            total = total + other[at]
        both = jnp.dot(basis_ref[at], stack_split([total]), preferred_element_type=jnp.float32)
        both = both[:, :columns] + both[:, columns:]
        out_ref[at * points : (at + 1) * points, :] = both.astype(out_ref.dtype)


def kernel(*refs, body, first, ins):
    body(refs[first : first + ins], refs[first + ins :])


def level_bit(level):
    return lax.axis_index("row") >> level & 1


def owner_bit():
    return lax.axis_index("col") & 1


def shards(rhs, leaf_basis, transfer, ranks, out_basis):
    leaves, rank_cap, wide = leaf_basis.shape
    points = wide // 2
    columns = rhs.shape[1]
    levels = transfer.shape[0]
    chunk_leaves = leaves // SLOTS
    half = chunk_leaves // 2
    owned = leaves // lax.axis_size("col")
    in_vmem = lambda array: pltpu.with_memory_space_constraint(array, pltpu.VMEM)
    in_hbm = lambda array: pltpu.with_memory_space_constraint(array, pltpu.HBM)
    sources = in_hbm(rhs.reshape(chunk_leaves, SLOTS, points, columns))
    bases = in_hbm(leaf_basis.reshape(chunk_leaves, SLOTS, rank_cap, wide))
    transfers = in_hbm(transfer.reshape(levels, leaves, rank_cap, 4 * rank_cap))
    half_out = ((half, rank_cap, columns), jnp.float32)
    level_out = ((leaves, rank_cap, 4 * rank_cap), transfer.dtype)

    def run(name, body, arrays, outs, token, scratch=(), from_hbm=False, last=False):
        token = token if isinstance(token, tuple) else (token,)
        vmem = pl.BlockSpec(memory_space=pltpu.VMEM)
        anywhere = pl.BlockSpec(memory_space=pl.ANY)
        if not from_hbm:
            arrays = [in_vmem(array) for array in arrays]
        return pl.pallas_call(
            functools.partial(kernel, body=body, first=len(token), ins=len(arrays)),
            in_specs=[anywhere] * len(token) + [anywhere if from_hbm else vmem] * len(arrays),
            out_specs=[vmem] * len(outs),
            out_shape=[jax.ShapeDtypeStruct(*out) if last else pltpu.VMEM(*out) for out in outs],
            scratch_shapes=scratch,
            cost_estimate=pl.CostEstimate(flops=1 << 33, bytes_accessed=1 << 20, transcendentals=0),
            compiler_params=pltpu.CompilerParams(vmem_limit_bytes=16 * 1024 * 1024),
            name=name,
        )(*token, *arrays)

    token = transfers
    kept, arrived, added, near, offset = {}, {}, {}, {}, {}
    live = far = targets = result = None
    matrices, coming = [], {}
    for step in ORDER:
        name = "_".join(str(part) for part in step[:3])
        if step[0] == "first":
            scratch = [
                pltpu.VMEM((2, half, points, columns), rhs.dtype),
                pltpu.VMEM((2, half, rank_cap, wide), leaf_basis.dtype),
                pltpu.SemaphoreType.DMA((4,)),
            ]
            body = functools.partial(first_body, half=half)
            sent, kept[0] = run(name, body, [sources, bases], [half_out] * 2, token, scratch, True)
            arrived[0] = {"sent": swap(sent, "row", 1)}
            offset[0] = 0
            token = kept[0]
        elif step[0] == "tables":
            scratch = [pltpu.VMEM(ranks.shape, ranks.dtype), pltpu.SemaphoreType.DMA((2,))]
            outs = [((levels, leaves, columns), jnp.int32), level_out]
            live, made = run(name, tables_body, [transfers, in_hbm(ranks)], outs, token, scratch, True)
            matrices.append(made)
            token = live
        elif step[0] == "rest":
            scratch = [
                pltpu.VMEM((SLOTS - 1, chunk_leaves, points, columns), rhs.dtype),
                pltpu.VMEM((SLOTS - 1, chunk_leaves, rank_cap, wide), leaf_basis.dtype),
                pltpu.SemaphoreType.DMA((2 * SLOTS,)),
            ]
            outs = [(((SLOTS - 1) * half, rank_cap, columns), jnp.float32)] * 2 + [level_out]
            body = functools.partial(rest_body, half=half)
            sent, token, made = run(name, body, [sources, bases, transfers], outs, token, scratch, True)
            matrices.append(made)
            sent = {"sent": swap(sent, "row", 1)}
            for slot in range(1, SLOTS):
                kept[slot], arrived[slot], offset[slot] = token, sent, (slot - 1) * half
        elif step[0] == "load":
            scratch = [pltpu.SemaphoreType.DMA((levels - 2,))]
            matrices += run(name, load_body, [transfers], [level_out] * (levels - 2), token, scratch, True)
            token = matrices[-1]
        elif step[0] == "targets":
            outs = [((owned, points, 2 * rank_cap), out_basis.dtype)]
            (targets,) = run(name, targets_body, [in_hbm(out_basis)], outs, token, [pltpu.SemaphoreType.DMA], True)
            token = targets
        elif step[0] == "mix":
            level, slot, pieces = step[1:4]
            if step[4:]:
                token = (token, arrived[step[4]]["sent"])
            last = level == levels - 1
            in_parts = "sent" not in arrived[slot]
            partner = arrived[slot]["sent_a" if pieces == ("sent",) else "sent_b"] if in_parts else arrived[slot]["sent"]
            body = functools.partial(
                mix_body, level=level, slot=slot, pieces=pieces, half=half, offset=offset[slot], in_parts=in_parts
            )
            plus = [added[slot, "sent"]] if last and slot % 2 and "sent" in pieces else []
            counts = {"kept_sent": 2 * half, "sent_a": half // 2, "sent_b": half // 2}
            outs = [((counts.get(piece, half), rank_cap, columns), jnp.float32) for piece in pieces]
            made = dict(zip(pieces, run(name, body, [live, matrices[level], kept[slot], partner] + plus, outs, token)))
            token = made[pieces[-1]]
            if last and slot % 2 == 0:
                for piece, other in (("kept", "sent"), ("sent", "kept"), ("kept_sent", "sent")):
                    if piece in made:
                        added[slot + 1, other] = swap(made[piece], "col", 3)
            elif last:
                if "sent" in made:
                    near[slot] = swap(made["sent"], "col", 1)
                if "kept" in made:
                    kept[slot] = made["kept"]
            else:
                coming.setdefault((level, slot), {}).update(
                    {piece: swap(made[piece], "row", 2 << level) for piece in pieces if piece != "kept"}
                )
                if "kept" in made:
                    kept[slot], arrived[slot], offset[slot] = made["kept"], coming[level, slot], 0
        elif step[0] == "far":
            (token,) = run(name, far_body, [kept[1], near[1]], [half_out], token)
            far = swap(token, "col", 4)
        else:
            out = ((owned * points, columns), jnp.bfloat16)
            arrays = [targets, kept[3], added[3, "kept"], near[3], far]
            (result,) = run(name, end_body, arrays, [out], token, last=True)
    return result


def solution(mesh):
    in_specs = (
        P(("row", "col"), None),
        P(("row", "col"), None, None),
        P(None, "row", "col", None, None, None),
        P(None, "row", "col", None),
        P("row", None, None, None),
    )
    out_specs = P(("row", "col"), None)
    return jax.shard_map(shards, mesh=mesh, in_specs=in_specs, out_specs=out_specs, check_vma=False)
```

time: 94.3 us -> 96.6 us (1.024)
  waiting for transfers between devices: 47.9 us -> 40.4 us
  starting transfers between devices: 28.1 us -> 34.7 us
  Pallas kernels: 17.7 us -> 20.4 us
    ppermute x23 -> x22, waiting for transfers between devices: 47.9 us -> 40.4 us  [swap(): return lax.ppermute(block, axis, [(at, at ^ mask) for at in range(count)])]
    ppermute x23 -> x22, starting transfers between devices: 28.1 us -> 34.7 us  [swap(): return lax.ppermute(block, axis, [(at, at ^ mask) for at in range(count)])]
    pallas_call x21 -> x27, Pallas kernels: 17.7 us -> 20.4 us  [run(): pl.pallas_call(functools.partial(kernel, body=body, first=len(token), ins...]
  transfers between devices with their start and end apart: 23 -> 22, of which waited for: 10 -> 8; matrix products, arithmetic and copies ran while one was open for 0% -> 0% of each run, Pallas kernels for 15% -> 18%
where the time goes in v4:
time: 96.6 us; the launch traced here: 95.8 us
  waiting for transfers between devices  40.4 us (42%)
  starting transfers between devices  34.7 us (36%)
  Pallas kernels  20.4 us (21%)
    ppermute x22, waiting for transfers between devices, swap(): return lax.ppermute(block, axis, [(at, at ^ mask) for at in range(count)])  40.4 us
    ppermute x22, starting transfers between devices, swap(): return lax.ppermute(block, axis, [(at, at ^ mask) for at in range(count)])  34.7 us
    pallas_call x27, Pallas kernels, run(): pl.pallas_call(functools.partial(kernel, body=body, first=len(token), ins...  20.4 us
  transfers between devices with their start and end apart: 22, of which 8 were waited for; matrix products, arithmetic and copies ran while one was open for 0% of the time, Pallas kernels for 18%

profile of v4, /device:TPU:8, one launch (start us, length us, event | category | flops | bytes accessed | tf_op | source)
XLA Modules:
  0.0 95.8 jit_solution(13439732643167662721)
XLA Ops:
  0.0 1.8 %first.1 = (f32[8,64,128]{2,1,0:T(8,128)S(1)}, f32[8,64,128]{2,1,0:T(8,128)S(1)}) custom-call(bf16[4,64,64,256]{3,2,1,0:T(8,128)(2,1)} %bitcast.3, bf16[16,4,128,128]{3,2,1,0:T(8,128)(2,1)} %bitcast.7, bf16[16,4,64,256]{3,2,1,0:T(8,128)(2,1)} %bitcast.9), custom_call_target="tpu_custom_call" | custom-call | flops 8589934592 | bytes 1048576 | tf_op jit(solution)/shard_map/first/pallas_call | solution.py:253
  1.9 1.6 %tables.1 = (s32[4,64,128]{2,1,0:T(8,128)S(1)}, bf16[64,64,256]{2,1,0:T(8,128)(2,1)S(1)}) custom-call(f32[8,64,128]{2,1,0:T(8,128)S(1)} %get-tuple-element.38.refs_0_.refs_3_, bf16[4,64,64,256]{3,2,1,0:T(8,128)(2,1)} %bitcast.4, s32[4,1,1,64]{3,2,1,0:T(1,128)} %refs_2_.1), custom_call_target="tpu_custom_call" | custom-call | flops 8589934592 | bytes 1048576 | tf_op jit(solution)/shard_map/tables/pallas_call | solution.py:253
  4.1 2.0 %collective-permute-start.1 = (f32[4,64,128]{2,1,0:T(8,128)S(1)}, f32[4,64,128]{2,1,0:T(8,128)S(1)}, u32[]{:S(2)}, u32[]{:S(2)}) collective-permute-start(f32[4,64,128]{2,1,0:T(8,128)S(1)} %get-tuple-element.45), channel_id=1, source_target_pairs={{0,16},{8,24},{16,0},{24,8},{32,48},{40,56},{48,32},{56,40},{64,80... | collective-permute-start | bytes 393224 | tf_op jit(solution)/shard_map/ppermute | solution.py:46
  6.3 2.9 %rest.1 = (f32[24,64,128]{2,1,0:T(8,128)S(1)}, f32[24,64,128]{2,1,0:T(8,128)S(1)}, bf16[64,64,256]{2,1,0:T(8,128)(2,1)S(1)}) custom-call(f32[8,64,128]{2,1,0:T(8,128)S(1)} %get-tuple-element.42.refs_0_.refs_3_, bf16[16,4,128,128]{3,2,1,0:T(8,128)(2,1)} %bitcast.8, bf16[16,4,64,256]{3,2,1,0:T(8,128)(2,1)} %bitcast.10, bf16[4,64,64,256]{3,2,1,0:T(8,128)(2,1)} %bitcast.5), custom_call_target="tpu_custom_call" | custom-call | flops 8589934592 | bytes 1048576 | tf_op jit(solution)/shard_map/rest/pallas_call | solution.py:253
  9.5 1.1 %collective-permute-done.1.refs_4_ = f32[4,64,128]{2,1,0:T(8,128)S(1)} collective-permute-done((f32[4,64,128]{2,1,0:T(8,128)S(1)}, f32[4,64,128]{2,1,0:T(8,128)S(1)}, u32[]{:S(2)}, u32[]{:S(2)}) %collective-permute-start.1) | collective-permute-done | bytes 131104 | tf_op jit(solution)/shard_map/ppermute | solution.py:46
  11.0 3.4 %collective-permute-start.5 = (f32[8,64,128]{2,1,0:T(8,128)S(1)}, f32[8,64,128]{2,1,0:T(8,128)S(1)}, u32[]{:S(2)}, u32[]{:S(2)}) collective-permute-start(f32[8,64,128]{2,1,0:T(8,128)S(1)} %mix_1_0.2.refs_0_), channel_id=1, source_target_pairs={{0,32},{8,40},{16,48},{24,56},{32,0},{40,8},{48,16},{56,24},{64,96... | collective-permute-start | bytes 786440 | tf_op jit(solution)/shard_map/ppermute | solution.py:46
  15.3 1.9 %collective-permute-start.4 = (f32[8,64,128]{2,1,0:T(8,128)S(1)}, f32[8,64,128]{2,1,0:T(8,128)S(1)}, u32[]{:S(2)}, u32[]{:S(2)}) collective-permute-start(f32[8,64,128]{2,1,0:T(8,128)S(1)} %get-tuple-element.50), channel_id=1, source_target_pairs={{0,16},{8,24},{16,0},{24,8},{32,48},{40,56},{48,32},{56,40},{64,80... | collective-permute-start | bytes 786440 | tf_op jit(solution)/shard_map/ppermute | solution.py:46
  17.2 2.2 %load.1 = (bf16[64,64,256]{2,1,0:T(8,128)(2,1)S(1)}, bf16[64,64,256]{2,1,0:T(8,128)(2,1)S(1)}) custom-call(f32[8,64,128]{2,1,0:T(8,128)S(1)} %get-tuple-element.48.refs_0_.refs_3_, bf16[4,64,64,256]{3,2,1,0:T(8,128)(2,1)} %bitcast.6), custom_call_target="tpu_custom_call" | custom-call | flops 8589934592 | bytes 1048576 | tf_op jit(solution)/shard_map/load/pallas_call | solution.py:253
  19.5 7.8 %collective-permute-done.4.refs_4_ = f32[8,64,128]{2,1,0:T(8,128)S(1)} collective-permute-done((f32[8,64,128]{2,1,0:T(8,128)S(1)}, f32[8,64,128]{2,1,0:T(8,128)S(1)}, u32[]{:S(2)}, u32[]{:S(2)}) %collective-permute-start.4) | collective-permute-done | bytes 262176 | tf_op jit(solution)/shard_map/ppermute | solution.py:46
  27.8 3.0 %collective-permute-start.8 = (f32[8,64,128]{2,1,0:T(8,128)S(1)}, f32[8,64,128]{2,1,0:T(8,128)S(1)}, u32[]{:S(2)}, u32[]{:S(2)}) collective-permute-start(f32[8,64,128]{2,1,0:T(8,128)S(1)} %get-tuple-element.59), channel_id=1, source_target_pairs={{0,32},{8,40},{16,48},{24,56},{32,0},{40,8},{48,16},{56,24},{64,96... | collective-permute-start | bytes 786440 | tf_op jit(solution)/shard_map/ppermute | solution.py:46
  31.3 2.6 %collective-permute-start.6 = (f32[8,64,128]{2,1,0:T(8,128)S(1)}, f32[8,64,128]{2,1,0:T(8,128)S(1)}, u32[]{:S(2)}, u32[]{:S(2)}) collective-permute-start(f32[8,64,128]{2,1,0:T(8,128)S(1)} %get-tuple-element.55), channel_id=1, source_target_pairs={{0,16},{8,24},{16,0},{24,8},{32,48},{40,56},{48,32},{56,40},{64,80... | collective-permute-start | bytes 786440 | tf_op jit(solution)/shard_map/ppermute | solution.py:46
  35.0 7.5 %collective-permute-done.6.refs_1_.refs_4_ = f32[8,64,128]{2,1,0:T(8,128)S(1)} collective-permute-done((f32[8,64,128]{2,1,0:T(8,128)S(1)}, f32[8,64,128]{2,1,0:T(8,128)S(1)}, u32[]{:S(2)}, u32[]{:S(2)}) %collective-permute-start.6) | collective-permute-done | bytes 262176 | tf_op jit(solution)/shard_map/ppermute | solution.py:46
  43.1 1.0 %collective-permute-start.9 = (f32[8,64,128]{2,1,0:T(8,128)S(1)}, f32[8,64,128]{2,1,0:T(8,128)S(1)}, u32[]{:S(2)}, u32[]{:S(2)}) collective-permute-start(f32[8,64,128]{2,1,0:T(8,128)S(1)} %get-tuple-element.61), channel_id=1, source_target_pairs={{0,16},{8,24},{16,0},{24,8},{32,48},{40,56},{48,32},{56,40},{64,80... | collective-permute-start | bytes 786440 | tf_op jit(solution)/shard_map/ppermute | solution.py:46
  45.3 3.0 %collective-permute-start.12 = (f32[16,64,128]{2,1,0:T(8,128)S(1)}, f32[16,64,128]{2,1,0:T(8,128)S(1)}, u32[]{:S(2)}, u32[]{:S(2)}) collective-permute-start(f32[16,64,128]{2,1,0:T(8,128)S(1)} %mix_3_0.1.refs_0_), channel_id=1, source_target_pairs={{0,3},{1,2},{2,1},{3,0},{4,7},{5,6},{6,5},{7,4},{8,11},{9,10},{10,... | collective-permute-start | bytes 1572872 | tf_op jit(solution)/shard_map/ppermute | solution.py:46
  49.4 3.7 %collective-permute-start.10 = (f32[8,64,128]{2,1,0:T(8,128)S(1)}, f32[8,64,128]{2,1,0:T(8,128)S(1)}, u32[]{:S(2)}, u32[]{:S(2)}) collective-permute-start(f32[8,64,128]{2,1,0:T(8,128)S(1)} %get-tuple-element.63), channel_id=1, source_target_pairs={{0,32},{8,40},{16,48},{24,56},{32,0},{40,8},{48,16},{56,24},{64,96... | collective-permute-start | bytes 786440 | tf_op jit(solution)/shard_map/ppermute | solution.py:46
  54.5 2.1 %collective-permute-start.16 = (f32[4,64,128]{2,1,0:T(8,128)S(1)}, f32[4,64,128]{2,1,0:T(8,128)S(1)}, u32[]{:S(2)}, u32[]{:S(2)}) collective-permute-start(f32[4,64,128]{2,1,0:T(8,128)S(1)} %get-tuple-element.70), channel_id=1, source_target_pairs={{0,32},{8,40},{16,48},{24,56},{32,0},{40,8},{48,16},{56,24},{64,96... | collective-permute-start | bytes 393224 | tf_op jit(solution)/shard_map/ppermute | solution.py:46
  56.6 12.0 %collective-permute-done.10.refs_4_ = f32[8,64,128]{2,1,0:T(8,128)S(1)} collective-permute-done((f32[8,64,128]{2,1,0:T(8,128)S(1)}, f32[8,64,128]{2,1,0:T(8,128)S(1)}, u32[]{:S(2)}, u32[]{:S(2)}) %collective-permute-start.10) | collective-permute-done | bytes 262176 | tf_op jit(solution)/shard_map/ppermute | solution.py:46
  71.3 1.0 %collective-permute-start.17 = (f32[8,64,128]{2,1,0:T(8,128)S(1)}, f32[8,64,128]{2,1,0:T(8,128)S(1)}, u32[]{:S(2)}, u32[]{:S(2)}) collective-permute-start(f32[8,64,128]{2,1,0:T(8,128)S(1)} %mix_2_3.2.refs_0_), channel_id=1, source_target_pairs={{0,64},{8,72},{16,80},{24,88},{32,96},{40,104},{48,112},{56,120},{... | collective-permute-start | bytes 786440 | tf_op jit(solution)/shard_map/ppermute | solution.py:46
  73.2 4.5 %collective-permute-done.14.refs_4_ = f32[8,64,128]{2,1,0:T(8,128)S(1)} collective-permute-done((f32[8,64,128]{2,1,0:T(8,128)S(1)}, f32[8,64,128]{2,1,0:T(8,128)S(1)}, u32[]{:S(2)}, u32[]{:S(2)}) %collective-permute-start.14) | collective-permute-done | bytes 262176 | tf_op jit(solution)/shard_map/ppermute | solution.py:46
  79.0 4.5 %collective-permute-start.21 = (f32[8,64,128]{2,1,0:T(8,128)S(1)}, f32[8,64,128]{2,1,0:T(8,128)S(1)}, u32[]{:S(2)}, u32[]{:S(2)}) collective-permute-start(f32[8,64,128]{2,1,0:T(8,128)S(1)} %far.1.refs_0_), channel_id=1, source_target_pairs={{0,4},{1,5},{2,6},{3,7},{4,0},{5,1},{6,2},{7,3},{8,12},{9,13},{10,... | collective-permute-start | bytes 786440 | tf_op jit(solution)/shard_map/ppermute | solution.py:46
  84.3 2.5 %collective-permute-start.19 = (f32[8,64,128]{2,1,0:T(8,128)S(1)}, f32[8,64,128]{2,1,0:T(8,128)S(1)}, u32[]{:S(2)}, u32[]{:S(2)}) collective-permute-start(f32[8,64,128]{2,1,0:T(8,128)S(1)} %mix_3_2.3.refs_0_), channel_id=1, source_target_pairs={{0,3},{1,2},{2,1},{3,0},{4,7},{5,6},{6,5},{7,4},{8,11},{9,10},{10,... | collective-permute-start | bytes 786440 | tf_op jit(solution)/shard_map/ppermute | solution.py:46
  86.8 1.0 targets.1.refs_0_.refs_1_
  88.7 6.0 %collective-permute-done.20.refs_4_ = f32[8,64,128]{2,1,0:T(8,128)S(1)} collective-permute-done((f32[8,64,128]{2,1,0:T(8,128)S(1)}, f32[8,64,128]{2,1,0:T(8,128)S(1)}, u32[]{:S(2)}, u32[]{:S(2)}) %collective-permute-start.20) | collective-permute-done | bytes 262176 | tf_op jit(solution)/shard_map/ppermute | solution.py:46
  94.7 1.1 %end.1 = bf16[1024,128]{1,0:T(8,128)(2,1)} custom-call(f32[8,64,128]{2,1,0:T(8,128)S(1)} %mix_3_3.3.refs_0_.refs_2_, bf16[8,128,128]{2,1,0:T(8,128)(2,1)S(1)} %targets.1.refs_0_.refs_1_, f32[8,64,128]{2,1,0:T(8,128)S(1)} %mix_3_3.3.refs_0_.refs_2_, f32[8,64,128]{2,1,0:T(8,128)S(1)} %collective-permute-done.19.refs_3_, ...), custom_call_target="tpu_custom_call" | custom-call | flops 8589934592 | bytes 1048576 | tf_op jit(solution)/shard_map/end/pallas_call | solution.py:253
  (47 shorter events, 15.4 us)
Async XLA Ops:
  1.8 1.7 %collective-permute-start = (f32[8,64,128]{2,1,0:T(8,128)S(1)}, f32[8,64,128]{2,1,0:T(8,128)S(1)}, u32[]{:S(2)}, u32[]{:S(2)}) collective-permute-start(f32[8,64,128]{2,1,0:T(8,128)S(1)} %get-tuple-element.41), channel_id=1, source_target_pairs={{0,8},{8,0},{16,24},{24,16},{32,40},{40,32},{48,56},{56,48},{64,72... | collective-permute-start | bytes 786440 | tf_op jit(solution)/shard_map/ppermute | solution.py:46
  4.1 6.5 %collective-permute-start.1 = (f32[4,64,128]{2,1,0:T(8,128)S(1)}, f32[4,64,128]{2,1,0:T(8,128)S(1)}, u32[]{:S(2)}, u32[]{:S(2)}) collective-permute-start(f32[4,64,128]{2,1,0:T(8,128)S(1)} %get-tuple-element.45), channel_id=1, source_target_pairs={{0,16},{8,24},{16,0},{24,8},{32,48},{40,56},{48,32},{56,40},{64,80... | collective-permute-start | bytes 393224 | tf_op jit(solution)/shard_map/ppermute | solution.py:46
  6.1 8.2 %collective-permute-start.2 = (f32[4,64,128]{2,1,0:T(8,128)S(1)}, f32[4,64,128]{2,1,0:T(8,128)S(1)}, u32[]{:S(2)}, u32[]{:S(2)}) collective-permute-start(f32[4,64,128]{2,1,0:T(8,128)S(1)} %get-tuple-element.46), channel_id=1, source_target_pairs={{0,16},{8,24},{16,0},{24,8},{32,48},{40,56},{48,32},{56,40},{64,80... | collective-permute-start | bytes 393224 | tf_op jit(solution)/shard_map/ppermute | solution.py:46
  9.2 5.5 %collective-permute-start.3 = (f32[24,64,128]{2,1,0:T(8,128)S(1)}, f32[24,64,128]{2,1,0:T(8,128)S(1)}, u32[]{:S(2)}, u32[]{:S(2)}) collective-permute-start(f32[24,64,128]{2,1,0:T(8,128)S(1)} %get-tuple-element.47), channel_id=1, source_target_pairs={{0,8},{8,0},{16,24},{24,16},{32,40},{40,32},{48,56},{56,48},{64,72... | collective-permute-start | bytes 2359304 | tf_op jit(solution)/shard_map/ppermute | solution.py:46
  11.0 22.9 %collective-permute-start.5 = (f32[8,64,128]{2,1,0:T(8,128)S(1)}, f32[8,64,128]{2,1,0:T(8,128)S(1)}, u32[]{:S(2)}, u32[]{:S(2)}) collective-permute-start(f32[8,64,128]{2,1,0:T(8,128)S(1)} %mix_1_0.2.refs_0_), channel_id=1, source_target_pairs={{0,32},{8,40},{16,48},{24,56},{32,0},{40,8},{48,16},{56,24},{64,96... | collective-permute-start | bytes 786440 | tf_op jit(solution)/shard_map/ppermute | solution.py:46
  15.3 11.9 %collective-permute-start.4 = (f32[8,64,128]{2,1,0:T(8,128)S(1)}, f32[8,64,128]{2,1,0:T(8,128)S(1)}, u32[]{:S(2)}, u32[]{:S(2)}) collective-permute-start(f32[8,64,128]{2,1,0:T(8,128)S(1)} %get-tuple-element.50), channel_id=1, source_target_pairs={{0,16},{8,24},{16,0},{24,8},{32,48},{40,56},{48,32},{56,40},{64,80... | collective-permute-start | bytes 786440 | tf_op jit(solution)/shard_map/ppermute | solution.py:46
  27.8 20.5 %collective-permute-start.8 = (f32[8,64,128]{2,1,0:T(8,128)S(1)}, f32[8,64,128]{2,1,0:T(8,128)S(1)}, u32[]{:S(2)}, u32[]{:S(2)}) collective-permute-start(f32[8,64,128]{2,1,0:T(8,128)S(1)} %get-tuple-element.59), channel_id=1, source_target_pairs={{0,32},{8,40},{16,48},{24,56},{32,0},{40,8},{48,16},{56,24},{64,96... | collective-permute-start | bytes 786440 | tf_op jit(solution)/shard_map/ppermute | solution.py:46
  31.3 11.2 %collective-permute-start.6 = (f32[8,64,128]{2,1,0:T(8,128)S(1)}, f32[8,64,128]{2,1,0:T(8,128)S(1)}, u32[]{:S(2)}, u32[]{:S(2)}) collective-permute-start(f32[8,64,128]{2,1,0:T(8,128)S(1)} %get-tuple-element.55), channel_id=1, source_target_pairs={{0,16},{8,24},{16,0},{24,8},{32,48},{40,56},{48,32},{56,40},{64,80... | collective-permute-start | bytes 786440 | tf_op jit(solution)/shard_map/ppermute | solution.py:46
  34.5 10.2 %collective-permute-start.7 = (f32[8,64,128]{2,1,0:T(8,128)S(1)}, f32[8,64,128]{2,1,0:T(8,128)S(1)}, u32[]{:S(2)}, u32[]{:S(2)}) collective-permute-start(f32[8,64,128]{2,1,0:T(8,128)S(1)} %get-tuple-element.58), channel_id=1, source_target_pairs={{0,64},{8,72},{16,80},{24,88},{32,96},{40,104},{48,112},{56,120},{... | collective-permute-start | bytes 786440 | tf_op jit(solution)/shard_map/ppermute | solution.py:46
  43.1 10.0 %collective-permute-start.9 = (f32[8,64,128]{2,1,0:T(8,128)S(1)}, f32[8,64,128]{2,1,0:T(8,128)S(1)}, u32[]{:S(2)}, u32[]{:S(2)}) collective-permute-start(f32[8,64,128]{2,1,0:T(8,128)S(1)} %get-tuple-element.61), channel_id=1, source_target_pairs={{0,16},{8,24},{16,0},{24,8},{32,48},{40,56},{48,32},{56,40},{64,80... | collective-permute-start | bytes 786440 | tf_op jit(solution)/shard_map/ppermute | solution.py:46
  45.3 24.4 %collective-permute-start.12 = (f32[16,64,128]{2,1,0:T(8,128)S(1)}, f32[16,64,128]{2,1,0:T(8,128)S(1)}, u32[]{:S(2)}, u32[]{:S(2)}) collective-permute-start(f32[16,64,128]{2,1,0:T(8,128)S(1)} %mix_3_0.1.refs_0_), channel_id=1, source_target_pairs={{0,3},{1,2},{2,1},{3,0},{4,7},{5,6},{6,5},{7,4},{8,11},{9,10},{10,... | collective-permute-start | bytes 1572872 | tf_op jit(solution)/shard_map/ppermute | solution.py:46
  48.9 20.8 %collective-permute-start.11 = (f32[8,64,128]{2,1,0:T(8,128)S(1)}, f32[8,64,128]{2,1,0:T(8,128)S(1)}, u32[]{:S(2)}, u32[]{:S(2)}) collective-permute-start(f32[8,64,128]{2,1,0:T(8,128)S(1)} %get-tuple-element.65), channel_id=1, source_target_pairs={{0,64},{8,72},{16,80},{24,88},{32,96},{40,104},{48,112},{56,120},{... | collective-permute-start | bytes 786440 | tf_op jit(solution)/shard_map/ppermute | solution.py:46
  49.4 19.2 %collective-permute-start.10 = (f32[8,64,128]{2,1,0:T(8,128)S(1)}, f32[8,64,128]{2,1,0:T(8,128)S(1)}, u32[]{:S(2)}, u32[]{:S(2)}) collective-permute-start(f32[8,64,128]{2,1,0:T(8,128)S(1)} %get-tuple-element.63), channel_id=1, source_target_pairs={{0,32},{8,40},{16,48},{24,56},{32,0},{40,8},{48,16},{56,24},{64,96... | collective-permute-start | bytes 786440 | tf_op jit(solution)/shard_map/ppermute | solution.py:46
  53.6 17.3 %collective-permute-start.13 = (f32[4,64,128]{2,1,0:T(8,128)S(1)}, f32[4,64,128]{2,1,0:T(8,128)S(1)}, u32[]{:S(2)}, u32[]{:S(2)}) collective-permute-start(f32[4,64,128]{2,1,0:T(8,128)S(1)} %get-tuple-element.67), channel_id=1, source_target_pairs={{0,32},{8,40},{16,48},{24,56},{32,0},{40,8},{48,16},{56,24},{64,96... | collective-permute-start | bytes 393224 | tf_op jit(solution)/shard_map/ppermute | solution.py:46
  54.5 29.0 %collective-permute-start.16 = (f32[4,64,128]{2,1,0:T(8,128)S(1)}, f32[4,64,128]{2,1,0:T(8,128)S(1)}, u32[]{:S(2)}, u32[]{:S(2)}) collective-permute-start(f32[4,64,128]{2,1,0:T(8,128)S(1)} %get-tuple-element.70), channel_id=1, source_target_pairs={{0,32},{8,40},{16,48},{24,56},{32,0},{40,8},{48,16},{56,24},{64,96... | collective-permute-start | bytes 393224 | tf_op jit(solution)/shard_map/ppermute | solution.py:46
  69.1 8.6 %collective-permute-start.14 = (f32[8,64,128]{2,1,0:T(8,128)S(1)}, f32[8,64,128]{2,1,0:T(8,128)S(1)}, u32[]{:S(2)}, u32[]{:S(2)}) collective-permute-start(f32[8,64,128]{2,1,0:T(8,128)S(1)} %get-tuple-element.68), channel_id=1, source_target_pairs={{0,64},{8,72},{16,80},{24,88},{32,96},{40,104},{48,112},{56,120},{... | collective-permute-start | bytes 786440 | tf_op jit(solution)/shard_map/ppermute | solution.py:46
  71.3 16.5 %collective-permute-start.17 = (f32[8,64,128]{2,1,0:T(8,128)S(1)}, f32[8,64,128]{2,1,0:T(8,128)S(1)}, u32[]{:S(2)}, u32[]{:S(2)}) collective-permute-start(f32[8,64,128]{2,1,0:T(8,128)S(1)} %mix_2_3.2.refs_0_), channel_id=1, source_target_pairs={{0,64},{8,72},{16,80},{24,88},{32,96},{40,104},{48,112},{56,120},{... | collective-permute-start | bytes 786440 | tf_op jit(solution)/shard_map/ppermute | solution.py:46
  72.3 6.7 %collective-permute-start.15 = (f32[8,64,128]{2,1,0:T(8,128)S(1)}, f32[8,64,128]{2,1,0:T(8,128)S(1)}, u32[]{:S(2)}, u32[]{:S(2)}) collective-permute-start(f32[8,64,128]{2,1,0:T(8,128)S(1)} %get-tuple-element.69), channel_id=1, source_target_pairs={{0,1},{1,0},{2,3},{3,2},{4,5},{5,4},{6,7},{7,6},{8,9},{9,8},{10,11... | collective-permute-start | bytes 786440 | tf_op jit(solution)/shard_map/ppermute | solution.py:46
  78.1 9.7 %collective-permute-start.18 = (f32[8,64,128]{2,1,0:T(8,128)S(1)}, f32[8,64,128]{2,1,0:T(8,128)S(1)}, u32[]{:S(2)}, u32[]{:S(2)}) collective-permute-start(f32[8,64,128]{2,1,0:T(8,128)S(1)} %mix_3_2.2.refs_0_), channel_id=1, source_target_pairs={{0,3},{1,2},{2,1},{3,0},{4,7},{5,6},{6,5},{7,4},{8,11},{9,10},{10,... | collective-permute-start | bytes 786440 | tf_op jit(solution)/shard_map/ppermute | solution.py:46
  79.0 15.6 %collective-permute-start.21 = (f32[8,64,128]{2,1,0:T(8,128)S(1)}, f32[8,64,128]{2,1,0:T(8,128)S(1)}, u32[]{:S(2)}, u32[]{:S(2)}) collective-permute-start(f32[8,64,128]{2,1,0:T(8,128)S(1)} %far.1.refs_0_), channel_id=1, source_target_pairs={{0,4},{1,5},{2,6},{3,7},{4,0},{5,1},{6,2},{7,3},{8,12},{9,13},{10,... | collective-permute-start | bytes 786440 | tf_op jit(solution)/shard_map/ppermute | solution.py:46
  84.3 10.4 %collective-permute-start.19 = (f32[8,64,128]{2,1,0:T(8,128)S(1)}, f32[8,64,128]{2,1,0:T(8,128)S(1)}, u32[]{:S(2)}, u32[]{:S(2)}) collective-permute-start(f32[8,64,128]{2,1,0:T(8,128)S(1)} %mix_3_2.3.refs_0_), channel_id=1, source_target_pairs={{0,3},{1,2},{2,1},{3,0},{4,7},{5,6},{6,5},{7,4},{8,11},{9,10},{10,... | collective-permute-start | bytes 786440 | tf_op jit(solution)/shard_map/ppermute | solution.py:46
  88.2 6.5 %collective-permute-start.20 = (f32[8,64,128]{2,1,0:T(8,128)S(1)}, f32[8,64,128]{2,1,0:T(8,128)S(1)}, u32[]{:S(2)}, u32[]{:S(2)}) collective-permute-start(f32[8,64,128]{2,1,0:T(8,128)S(1)} %mix_3_3.2.refs_0_), channel_id=1, source_target_pairs={{0,1},{1,0},{2,3},{3,2},{4,5},{5,4},{6,7},{7,6},{8,9},{9,8},{10,11... | collective-permute-start | bytes 786440 | tf_op jit(solution)/shard_map/ppermute | solution.py:46

commit v5 on v4

--- a/solution.py
+++ b/solution.py
@@ -13,30 +13,29 @@
 ORDER = [
     ('first',),
     ('tables',),
-    ('mix', 0, 0, ('sent_a', 'sent_b', 'kept')),
+    ('mix', 0, 0, ('sent', 'kept')),
     ('rest',),
-    ('mix', 1, 0, ('sent',)),
-    ('mix', 1, 0, ('kept',)),
+    ('load',),
     ('mix', 0, 1, ('sent', 'kept')),
-    ('load',),
+    ('mix', 1, 0, ('sent', 'kept')),
     ('mix', 1, 1, ('sent', 'kept')),
     ('mix', 0, 2, ('sent', 'kept')),
     ('mix', 2, 0, ('sent', 'kept')),
-    ('mix', 0, 3, ('sent', 'kept'), 2),
-    ('mix', 1, 2, ('sent', 'kept')),
+    ('mix', 1, 2, ('sent_a', 'sent_b', 'kept')),
+    ('mix', 0, 3, ('sent', 'kept')),
+    ('mix', 2, 1, ('sent', 'kept')),
     ('mix', 3, 0, ('kept_sent',)),
-    ('mix', 2, 1, ('sent', 'kept')),
-    ('mix', 1, 3, ('sent_a', 'sent_b', 'kept')),
-    ('mix', 2, 2, ('sent', 'kept')),
     ('mix', 3, 1, ('sent', 'kept')),
-    ('mix', 2, 3, ('sent',)),
+    ('mix', 2, 2, ('sent',)),
+    ('mix', 1, 3, ('sent', 'kept')),
+    ('mix', 2, 2, ('kept',)),
     ('mix', 3, 2, ('kept',)),
+    ('mix', 2, 3, ('sent', 'kept')),
     ('far',),
-    ('mix', 2, 3, ('kept',)),
     ('mix', 3, 2, ('sent',)),
-    ('targets',),
     ('mix', 3, 3, ('sent',)),
     ('mix', 3, 3, ('kept',)),
+    ('targets',),
     ('end',),
 ]
 
@@ -199,7 +198,10 @@
 
 def far_body(mine, outs):
     for at in range(outs[0].shape[0]):
-        outs[0][at] = mine[0][at] + mine[1][at]
+        total = mine[0][at]
+        for other in mine[1:]:
+            total = total + other[at]
+        outs[0][at] = total
 
 
 def end_body(mine, outs):
@@ -265,6 +267,7 @@
     kept, arrived, added, near, offset = {}, {}, {}, {}, {}
     live = far = targets = result = None
     matrices, coming = [], {}
+    late = lambda slot: [added[slot, "kept"]] if (slot, "kept") in added else []
     for step in ORDER:
         name = "_".join(str(part) for part in step[:3])
         if step[0] == "first":
@@ -336,11 +339,11 @@
                 if "kept" in made:
                     kept[slot], arrived[slot], offset[slot] = made["kept"], coming[level, slot], 0
         elif step[0] == "far":
-            (token,) = run(name, far_body, [kept[1], near[1]], [half_out], token)
+            (token,) = run(name, far_body, [kept[1], near[1]] + late(1), [half_out], token)
             far = swap(token, "col", 4)
         else:
             out = ((owned * points, columns), jnp.bfloat16)
-            arrays = [targets, kept[3], added[3, "kept"], near[3], far]
+            arrays = [targets, kept[3], near[3], far] + late(3)
             (result,) = run(name, end_body, arrays, [out], token, last=True)
     return result
 

time: 96.6 us -> 89.5 us (0.927)
  waiting for transfers between devices: 40.4 us -> 31.4 us
  starting transfers between devices: 34.7 us -> 35.9 us
    ppermute x22 -> x21, waiting for transfers between devices: 40.4 us -> 31.4 us  [swap(): return lax.ppermute(block, axis, [(at, at ^ mask) for at in range(count)])]
    ppermute x22 -> x21, starting transfers between devices: 34.7 us -> 35.9 us  [swap(): return lax.ppermute(block, axis, [(at, at ^ mask) for at in range(count)])]
    pallas_call x27 -> x26, Pallas kernels: 20.4 us -> 20.2 us  [run(): pl.pallas_call(functools.partial(kernel, body=body, first=len(token), ins...]
  transfers between devices with their start and end apart: 22 -> 21, of which waited for: 8 -> 10; matrix products, arithmetic and copies ran while one was open for 0% -> 0% of each run, Pallas kernels for 18% -> 18%
where the time goes in v5:
time: 89.5 us; the launch traced here: 87.8 us
  starting transfers between devices  35.9 us (40%)
  waiting for transfers between devices  31.4 us (35%)
  Pallas kernels  20.2 us (23%)
    ppermute x21, starting transfers between devices, swap(): return lax.ppermute(block, axis, [(at, at ^ mask) for at in range(count)])  35.9 us
    ppermute x21, waiting for transfers between devices, swap(): return lax.ppermute(block, axis, [(at, at ^ mask) for at in range(count)])  31.4 us
    pallas_call x26, Pallas kernels, run(): pl.pallas_call(functools.partial(kernel, body=body, first=len(token), ins...  20.2 us
  transfers between devices with their start and end apart: 21, of which 10 were waited for; matrix products, arithmetic and copies ran while one was open for 0% of the time, Pallas kernels for 18%

profile of v5, /device:TPU:8, one launch (start us, length us, event | category | flops | bytes accessed | tf_op | source)
XLA Modules:
  0.0 87.8 jit_solution(1813476888705895407)
XLA Ops:
  0.0 1.8 %first.1 = (f32[8,64,128]{2,1,0:T(8,128)S(1)}, f32[8,64,128]{2,1,0:T(8,128)S(1)}) custom-call(bf16[4,64,64,256]{3,2,1,0:T(8,128)(2,1)} %bitcast.3, bf16[16,4,128,128]{3,2,1,0:T(8,128)(2,1)} %bitcast.7, bf16[16,4,64,256]{3,2,1,0:T(8,128)(2,1)} %bitcast.9), custom_call_target="tpu_custom_call" | custom-call | flops 8589934592 | bytes 1048576 | tf_op jit(solution)/shard_map/first/pallas_call | solution.py:255
  1.9 1.6 %tables.1 = (s32[4,64,128]{2,1,0:T(8,128)S(1)}, bf16[64,64,256]{2,1,0:T(8,128)(2,1)S(1)}) custom-call(f32[8,64,128]{2,1,0:T(8,128)S(1)} %get-tuple-element.39.refs_0_.refs_3_, bf16[4,64,64,256]{3,2,1,0:T(8,128)(2,1)} %bitcast.4, s32[4,1,1,64]{3,2,1,0:T(1,128)} %refs_2_.1), custom_call_target="tpu_custom_call" | custom-call | flops 8589934592 | bytes 1048576 | tf_op jit(solution)/shard_map/tables/pallas_call | solution.py:255
  4.1 2.0 %collective-permute-start.2 = (f32[8,64,128]{2,1,0:T(8,128)S(1)}, f32[8,64,128]{2,1,0:T(8,128)S(1)}, u32[]{:S(2)}, u32[]{:S(2)}) collective-permute-start(f32[8,64,128]{2,1,0:T(8,128)S(1)} %get-tuple-element.49), channel_id=1, source_target_pairs={{0,16},{8,24},{16,0},{24,8},{32,48},{40,56},{48,32},{56,40},{64,80... | collective-permute-start | bytes 786440 | tf_op jit(solution)/shard_map/ppermute | solution.py:45
  6.1 2.9 %rest.1 = (f32[24,64,128]{2,1,0:T(8,128)S(1)}, f32[24,64,128]{2,1,0:T(8,128)S(1)}, bf16[64,64,256]{2,1,0:T(8,128)(2,1)S(1)}) custom-call(f32[8,64,128]{2,1,0:T(8,128)S(1)} %get-tuple-element.43.refs_0_.refs_3_, bf16[16,4,128,128]{3,2,1,0:T(8,128)(2,1)} %bitcast.8, bf16[16,4,64,256]{3,2,1,0:T(8,128)(2,1)} %bitcast.10, bf16[4,64,64,256]{3,2,1,0:T(8,128)(2,1)} %bitcast.5), custom_call_target="tpu_custom_call" | custom-call | flops 8589934592 | bytes 1048576 | tf_op jit(solution)/shard_map/rest/pallas_call | solution.py:255
  9.4 2.2 %load.1 = (bf16[64,64,256]{2,1,0:T(8,128)(2,1)S(1)}, bf16[64,64,256]{2,1,0:T(8,128)(2,1)S(1)}) custom-call(f32[24,64,128]{2,1,0:T(8,128)S(1)} %get-tuple-element.44.refs_0_.refs_3_, bf16[4,64,64,256]{3,2,1,0:T(8,128)(2,1)} %bitcast.6), custom_call_target="tpu_custom_call" | custom-call | flops 8589934592 | bytes 1048576 | tf_op jit(solution)/shard_map/load/pallas_call | solution.py:255
  13.7 3.4 %collective-permute-start.4 = (f32[8,64,128]{2,1,0:T(8,128)S(1)}, f32[8,64,128]{2,1,0:T(8,128)S(1)}, u32[]{:S(2)}, u32[]{:S(2)}) collective-permute-start(f32[8,64,128]{2,1,0:T(8,128)S(1)} %get-tuple-element.55), channel_id=1, source_target_pairs={{0,32},{8,40},{16,48},{24,56},{32,0},{40,8},{48,16},{56,24},{64,96... | collective-permute-start | bytes 786440 | tf_op jit(solution)/shard_map/ppermute | solution.py:45
  17.0 9.4 %collective-permute-done.3.refs_4_ = f32[8,64,128]{2,1,0:T(8,128)S(1)} collective-permute-done((f32[8,64,128]{2,1,0:T(8,128)S(1)}, f32[8,64,128]{2,1,0:T(8,128)S(1)}, u32[]{:S(2)}, u32[]{:S(2)}) %collective-permute-start.3) | collective-permute-done | bytes 262176 | tf_op jit(solution)/shard_map/ppermute | solution.py:45
  28.3 8.7 %collective-permute-start.7 = (f32[8,64,128]{2,1,0:T(8,128)S(1)}, f32[8,64,128]{2,1,0:T(8,128)S(1)}, u32[]{:S(2)}, u32[]{:S(2)}) collective-permute-start(f32[8,64,128]{2,1,0:T(8,128)S(1)} %get-tuple-element.62), channel_id=1, source_target_pairs={{0,64},{8,72},{16,80},{24,88},{32,96},{40,104},{48,112},{56,120},{... | collective-permute-start | bytes 786440 | tf_op jit(solution)/shard_map/ppermute | solution.py:45
  37.1 4.0 %collective-permute-done.5.refs_4_ = f32[8,64,128]{2,1,0:T(8,128)S(1)} collective-permute-done((f32[8,64,128]{2,1,0:T(8,128)S(1)}, f32[8,64,128]{2,1,0:T(8,128)S(1)}, u32[]{:S(2)}, u32[]{:S(2)}) %collective-permute-start.5) | collective-permute-done | bytes 262176 | tf_op jit(solution)/shard_map/ppermute | solution.py:45
  43.4 2.9 %collective-permute-start.9 = (f32[16,64,128]{2,1,0:T(8,128)S(1)}, f32[16,64,128]{2,1,0:T(8,128)S(1)}, u32[]{:S(2)}, u32[]{:S(2)}) collective-permute-start(f32[16,64,128]{2,1,0:T(8,128)S(1)} %mix_3_0.1.refs_0_), channel_id=1, source_target_pairs={{0,3},{1,2},{2,1},{3,0},{4,7},{5,6},{6,5},{7,4},{8,11},{9,10},{10,... | collective-permute-start | bytes 1572872 | tf_op jit(solution)/shard_map/ppermute | solution.py:45
  46.7 1.7 %collective-permute-start.10 = (f32[4,64,128]{2,1,0:T(8,128)S(1)}, f32[4,64,128]{2,1,0:T(8,128)S(1)}, u32[]{:S(2)}, u32[]{:S(2)}) collective-permute-start(f32[4,64,128]{2,1,0:T(8,128)S(1)} %get-tuple-element.65), channel_id=1, source_target_pairs={{0,32},{8,40},{16,48},{24,56},{32,0},{40,8},{48,16},{56,24},{64,96... | collective-permute-start | bytes 393224 | tf_op jit(solution)/shard_map/ppermute | solution.py:45
  48.4 1.2 %collective-permute-start.12 = (f32[4,64,128]{2,1,0:T(8,128)S(1)}, f32[4,64,128]{2,1,0:T(8,128)S(1)}, u32[]{:S(2)}, u32[]{:S(2)}) collective-permute-start(f32[4,64,128]{2,1,0:T(8,128)S(1)} %get-tuple-element.68), channel_id=1, source_target_pairs={{0,32},{8,40},{16,48},{24,56},{32,0},{40,8},{48,16},{56,24},{64,96... | collective-permute-start | bytes 393224 | tf_op jit(solution)/shard_map/ppermute | solution.py:45
  49.6 1.3 %collective-permute-start.11 = (f32[8,64,128]{2,1,0:T(8,128)S(1)}, f32[8,64,128]{2,1,0:T(8,128)S(1)}, u32[]{:S(2)}, u32[]{:S(2)}) collective-permute-start(f32[8,64,128]{2,1,0:T(8,128)S(1)} %get-tuple-element.66), channel_id=1, source_target_pairs={{0,16},{8,24},{16,0},{24,8},{32,48},{40,56},{48,32},{56,40},{64,80... | collective-permute-start | bytes 786440 | tf_op jit(solution)/shard_map/ppermute | solution.py:45
  50.9 1.7 %collective-permute-done.8.refs_4_ = f32[8,64,128]{2,1,0:T(8,128)S(1)} collective-permute-done((f32[8,64,128]{2,1,0:T(8,128)S(1)}, f32[8,64,128]{2,1,0:T(8,128)S(1)}, u32[]{:S(2)}, u32[]{:S(2)}) %collective-permute-start.8) | collective-permute-done | bytes 262176 | tf_op jit(solution)/shard_map/ppermute | solution.py:45
  52.6 4.1 %collective-permute-done.9.refs_5_ = f32[16,64,128]{2,1,0:T(8,128)S(1)} collective-permute-done((f32[16,64,128]{2,1,0:T(8,128)S(1)}, f32[16,64,128]{2,1,0:T(8,128)S(1)}, u32[]{:S(2)}, u32[]{:S(2)}) %collective-permute-start.9) | collective-permute-done | bytes 524320 | tf_op jit(solution)/shard_map/ppermute | solution.py:45
  57.7 1.7 %collective-permute-start.13 = (f32[8,64,128]{2,1,0:T(8,128)S(1)}, f32[8,64,128]{2,1,0:T(8,128)S(1)}, u32[]{:S(2)}, u32[]{:S(2)}) collective-permute-start(f32[8,64,128]{2,1,0:T(8,128)S(1)} %mix_2_2.2.refs_0_), channel_id=1, source_target_pairs={{0,64},{8,72},{16,80},{24,88},{32,96},{40,104},{48,112},{56,120},{... | collective-permute-start | bytes 786440 | tf_op jit(solution)/shard_map/ppermute | solution.py:45
  62.3 1.9 %collective-permute-done.13.refs_4_ = f32[8,64,128]{2,1,0:T(8,128)S(1)} collective-permute-done((f32[8,64,128]{2,1,0:T(8,128)S(1)}, f32[8,64,128]{2,1,0:T(8,128)S(1)}, u32[]{:S(2)}, u32[]{:S(2)}) %collective-permute-start.13) | collective-permute-done | bytes 262176 | tf_op jit(solution)/shard_map/ppermute | solution.py:45
  64.5 2.8 %collective-permute-start.17 = (f32[8,64,128]{2,1,0:T(8,128)S(1)}, f32[8,64,128]{2,1,0:T(8,128)S(1)}, u32[]{:S(2)}, u32[]{:S(2)}) collective-permute-start(f32[8,64,128]{2,1,0:T(8,128)S(1)} %mix_3_2.2.refs_0_), channel_id=1, source_target_pairs={{0,3},{1,2},{2,1},{3,0},{4,7},{5,6},{6,5},{7,4},{8,11},{9,10},{10,... | collective-permute-start | bytes 786440 | tf_op jit(solution)/shard_map/ppermute | solution.py:45
  67.4 3.8 %collective-permute-done.14.refs_4_ = f32[8,64,128]{2,1,0:T(8,128)S(1)} collective-permute-done((f32[8,64,128]{2,1,0:T(8,128)S(1)}, f32[8,64,128]{2,1,0:T(8,128)S(1)}, u32[]{:S(2)}, u32[]{:S(2)}) %collective-permute-start.14) | collective-permute-done | bytes 262176 | tf_op jit(solution)/shard_map/ppermute | solution.py:45
  71.7 1.8 %collective-permute-start.16 = (f32[8,64,128]{2,1,0:T(8,128)S(1)}, f32[8,64,128]{2,1,0:T(8,128)S(1)}, u32[]{:S(2)}, u32[]{:S(2)}) collective-permute-start(f32[8,64,128]{2,1,0:T(8,128)S(1)} %get-tuple-element.72), channel_id=1, source_target_pairs={{0,64},{8,72},{16,80},{24,88},{32,96},{40,104},{48,112},{56,120},{... | collective-permute-start | bytes 786440 | tf_op jit(solution)/shard_map/ppermute | solution.py:45
  73.5 4.9 %collective-permute-start.19 = (f32[8,64,128]{2,1,0:T(8,128)S(1)}, f32[8,64,128]{2,1,0:T(8,128)S(1)}, u32[]{:S(2)}, u32[]{:S(2)}) collective-permute-start(f32[8,64,128]{2,1,0:T(8,128)S(1)} %far.1.refs_0_), channel_id=1, source_target_pairs={{0,4},{1,5},{2,6},{3,7},{4,0},{5,1},{6,2},{7,3},{8,12},{9,13},{10,... | collective-permute-start | bytes 786440 | tf_op jit(solution)/shard_map/ppermute | solution.py:45
  78.8 1.1 %collective-permute-start.20 = (f32[8,64,128]{2,1,0:T(8,128)S(1)}, f32[8,64,128]{2,1,0:T(8,128)S(1)}, u32[]{:S(2)}, u32[]{:S(2)}) collective-permute-start(f32[8,64,128]{2,1,0:T(8,128)S(1)} %mix_3_2.3.refs_0_), channel_id=1, source_target_pairs={{0,3},{1,2},{2,1},{3,0},{4,7},{5,6},{6,5},{7,4},{8,11},{9,10},{10,... | collective-permute-start | bytes 786440 | tf_op jit(solution)/shard_map/ppermute | solution.py:45
  81.7 4.7 %collective-permute-done.20.refs_5_ = f32[8,64,128]{2,1,0:T(8,128)S(1)} collective-permute-done((f32[8,64,128]{2,1,0:T(8,128)S(1)}, f32[8,64,128]{2,1,0:T(8,128)S(1)}, u32[]{:S(2)}, u32[]{:S(2)}) %collective-permute-start.20) | collective-permute-done | bytes 262176 | tf_op jit(solution)/shard_map/ppermute | solution.py:45
  86.7 1.1 %end.1 = bf16[1024,128]{1,0:T(8,128)(2,1)} custom-call(bf16[8,128,128]{2,1,0:T(8,128)(2,1)S(1)} %targets.1.refs_0_.refs_1_, bf16[8,128,128]{2,1,0:T(8,128)(2,1)S(1)} %targets.1.refs_0_.refs_1_, f32[8,64,128]{2,1,0:T(8,128)S(1)} %mix_3_3.3.refs_0_.refs_2_, f32[8,64,128]{2,1,0:T(8,128)S(1)} %collective-permute-done.18.refs_3_, ...), custom_call_target="tpu_custom_call" | custom-call | flops 8589934592 | bytes 1048576 | tf_op jit(solution)/shard_map/end/pallas_call | solution.py:255
  (44 shorter events, 14.9 us)
Async XLA Ops:
  1.8 1.7 %collective-permute-start = (f32[8,64,128]{2,1,0:T(8,128)S(1)}, f32[8,64,128]{2,1,0:T(8,128)S(1)}, u32[]{:S(2)}, u32[]{:S(2)}) collective-permute-start(f32[8,64,128]{2,1,0:T(8,128)S(1)} %get-tuple-element.42), channel_id=1, source_target_pairs={{0,8},{8,0},{16,24},{24,16},{32,40},{40,32},{48,56},{56,48},{64,72... | collective-permute-start | bytes 786440 | tf_op jit(solution)/shard_map/ppermute | solution.py:45
  4.1 9.0 %collective-permute-start.2 = (f32[8,64,128]{2,1,0:T(8,128)S(1)}, f32[8,64,128]{2,1,0:T(8,128)S(1)}, u32[]{:S(2)}, u32[]{:S(2)}) collective-permute-start(f32[8,64,128]{2,1,0:T(8,128)S(1)} %get-tuple-element.49), channel_id=1, source_target_pairs={{0,16},{8,24},{16,0},{24,8},{32,48},{40,56},{48,32},{56,40},{64,80... | collective-permute-start | bytes 786440 | tf_op jit(solution)/shard_map/ppermute | solution.py:45
  9.1 2.5 %collective-permute-start.1 = (f32[24,64,128]{2,1,0:T(8,128)S(1)}, f32[24,64,128]{2,1,0:T(8,128)S(1)}, u32[]{:S(2)}, u32[]{:S(2)}) collective-permute-start(f32[24,64,128]{2,1,0:T(8,128)S(1)} %get-tuple-element.46), channel_id=1, source_target_pairs={{0,8},{8,0},{16,24},{24,16},{32,40},{40,32},{48,56},{56,48},{64,72... | collective-permute-start | bytes 2359304 | tf_op jit(solution)/shard_map/ppermute | solution.py:45
  12.2 14.2 %collective-permute-start.3 = (f32[8,64,128]{2,1,0:T(8,128)S(1)}, f32[8,64,128]{2,1,0:T(8,128)S(1)}, u32[]{:S(2)}, u32[]{:S(2)}) collective-permute-start(f32[8,64,128]{2,1,0:T(8,128)S(1)} %get-tuple-element.51), channel_id=1, source_target_pairs={{0,16},{8,24},{16,0},{24,8},{32,48},{40,56},{48,32},{56,40},{64,80... | collective-permute-start | bytes 786440 | tf_op jit(solution)/shard_map/ppermute | solution.py:45
  13.7 14.1 %collective-permute-start.4 = (f32[8,64,128]{2,1,0:T(8,128)S(1)}, f32[8,64,128]{2,1,0:T(8,128)S(1)}, u32[]{:S(2)}, u32[]{:S(2)}) collective-permute-start(f32[8,64,128]{2,1,0:T(8,128)S(1)} %get-tuple-element.55), channel_id=1, source_target_pairs={{0,32},{8,40},{16,48},{24,56},{32,0},{40,8},{48,16},{56,24},{64,96... | collective-permute-start | bytes 786440 | tf_op jit(solution)/shard_map/ppermute | solution.py:45
  27.0 15.2 %collective-permute-start.6 = (f32[8,64,128]{2,1,0:T(8,128)S(1)}, f32[8,64,128]{2,1,0:T(8,128)S(1)}, u32[]{:S(2)}, u32[]{:S(2)}) collective-permute-start(f32[8,64,128]{2,1,0:T(8,128)S(1)} %get-tuple-element.60), channel_id=1, source_target_pairs={{0,32},{8,40},{16,48},{24,56},{32,0},{40,8},{48,16},{56,24},{64,96... | collective-permute-start | bytes 786440 | tf_op jit(solution)/shard_map/ppermute | solution.py:45
  27.7 13.4 %collective-permute-start.5 = (f32[8,64,128]{2,1,0:T(8,128)S(1)}, f32[8,64,128]{2,1,0:T(8,128)S(1)}, u32[]{:S(2)}, u32[]{:S(2)}) collective-permute-start(f32[8,64,128]{2,1,0:T(8,128)S(1)} %get-tuple-element.57), channel_id=1, source_target_pairs={{0,16},{8,24},{16,0},{24,8},{32,48},{40,56},{48,32},{56,40},{64,80... | collective-permute-start | bytes 786440 | tf_op jit(solution)/shard_map/ppermute | solution.py:45
  28.3 14.4 %collective-permute-start.7 = (f32[8,64,128]{2,1,0:T(8,128)S(1)}, f32[8,64,128]{2,1,0:T(8,128)S(1)}, u32[]{:S(2)}, u32[]{:S(2)}) collective-permute-start(f32[8,64,128]{2,1,0:T(8,128)S(1)} %get-tuple-element.62), channel_id=1, source_target_pairs={{0,64},{8,72},{16,80},{24,88},{32,96},{40,104},{48,112},{56,120},{... | collective-permute-start | bytes 786440 | tf_op jit(solution)/shard_map/ppermute | solution.py:45
  43.4 13.3 %collective-permute-start.9 = (f32[16,64,128]{2,1,0:T(8,128)S(1)}, f32[16,64,128]{2,1,0:T(8,128)S(1)}, u32[]{:S(2)}, u32[]{:S(2)}) collective-permute-start(f32[16,64,128]{2,1,0:T(8,128)S(1)} %mix_3_0.1.refs_0_), channel_id=1, source_target_pairs={{0,3},{1,2},{2,1},{3,0},{4,7},{5,6},{6,5},{7,4},{8,11},{9,10},{10,... | collective-permute-start | bytes 1572872 | tf_op jit(solution)/shard_map/ppermute | solution.py:45
  46.2 6.4 %collective-permute-start.8 = (f32[8,64,128]{2,1,0:T(8,128)S(1)}, f32[8,64,128]{2,1,0:T(8,128)S(1)}, u32[]{:S(2)}, u32[]{:S(2)}) collective-permute-start(f32[8,64,128]{2,1,0:T(8,128)S(1)} %get-tuple-element.63), channel_id=1, source_target_pairs={{0,64},{8,72},{16,80},{24,88},{32,96},{40,104},{48,112},{56,120},{... | collective-permute-start | bytes 786440 | tf_op jit(solution)/shard_map/ppermute | solution.py:45
  46.7 10.6 %collective-permute-start.10 = (f32[4,64,128]{2,1,0:T(8,128)S(1)}, f32[4,64,128]{2,1,0:T(8,128)S(1)}, u32[]{:S(2)}, u32[]{:S(2)}) collective-permute-start(f32[4,64,128]{2,1,0:T(8,128)S(1)} %get-tuple-element.65), channel_id=1, source_target_pairs={{0,32},{8,40},{16,48},{24,56},{32,0},{40,8},{48,16},{56,24},{64,96... | collective-permute-start | bytes 393224 | tf_op jit(solution)/shard_map/ppermute | solution.py:45
  48.4 13.5 %collective-permute-start.12 = (f32[4,64,128]{2,1,0:T(8,128)S(1)}, f32[4,64,128]{2,1,0:T(8,128)S(1)}, u32[]{:S(2)}, u32[]{:S(2)}) collective-permute-start(f32[4,64,128]{2,1,0:T(8,128)S(1)} %get-tuple-element.68), channel_id=1, source_target_pairs={{0,32},{8,40},{16,48},{24,56},{32,0},{40,8},{48,16},{56,24},{64,96... | collective-permute-start | bytes 393224 | tf_op jit(solution)/shard_map/ppermute | solution.py:45
  49.6 10.7 %collective-permute-start.11 = (f32[8,64,128]{2,1,0:T(8,128)S(1)}, f32[8,64,128]{2,1,0:T(8,128)S(1)}, u32[]{:S(2)}, u32[]{:S(2)}) collective-permute-start(f32[8,64,128]{2,1,0:T(8,128)S(1)} %get-tuple-element.66), channel_id=1, source_target_pairs={{0,16},{8,24},{16,0},{24,8},{32,48},{40,56},{48,32},{56,40},{64,80... | collective-permute-start | bytes 786440 | tf_op jit(solution)/shard_map/ppermute | solution.py:45
  57.7 6.5 %collective-permute-start.13 = (f32[8,64,128]{2,1,0:T(8,128)S(1)}, f32[8,64,128]{2,1,0:T(8,128)S(1)}, u32[]{:S(2)}, u32[]{:S(2)}) collective-permute-start(f32[8,64,128]{2,1,0:T(8,128)S(1)} %mix_2_2.2.refs_0_), channel_id=1, source_target_pairs={{0,64},{8,72},{16,80},{24,88},{32,96},{40,104},{48,112},{56,120},{... | collective-permute-start | bytes 786440 | tf_op jit(solution)/shard_map/ppermute | solution.py:45
  60.9 10.3 %collective-permute-start.14 = (f32[8,64,128]{2,1,0:T(8,128)S(1)}, f32[8,64,128]{2,1,0:T(8,128)S(1)}, u32[]{:S(2)}, u32[]{:S(2)}) collective-permute-start(f32[8,64,128]{2,1,0:T(8,128)S(1)} %get-tuple-element.69), channel_id=1, source_target_pairs={{0,32},{8,40},{16,48},{24,56},{32,0},{40,8},{48,16},{56,24},{64,96... | collective-permute-start | bytes 786440 | tf_op jit(solution)/shard_map/ppermute | solution.py:45
  61.6 11.8 %collective-permute-start.15 = (f32[8,64,128]{2,1,0:T(8,128)S(1)}, f32[8,64,128]{2,1,0:T(8,128)S(1)}, u32[]{:S(2)}, u32[]{:S(2)}) collective-permute-start(f32[8,64,128]{2,1,0:T(8,128)S(1)} %get-tuple-element.71), channel_id=1, source_target_pairs={{0,1},{1,0},{2,3},{3,2},{4,5},{5,4},{6,7},{7,6},{8,9},{9,8},{10,11... | collective-permute-start | bytes 786440 | tf_op jit(solution)/shard_map/ppermute | solution.py:45
  64.5 15.3 %collective-permute-start.17 = (f32[8,64,128]{2,1,0:T(8,128)S(1)}, f32[8,64,128]{2,1,0:T(8,128)S(1)}, u32[]{:S(2)}, u32[]{:S(2)}) collective-permute-start(f32[8,64,128]{2,1,0:T(8,128)S(1)} %mix_3_2.2.refs_0_), channel_id=1, source_target_pairs={{0,3},{1,2},{2,1},{3,0},{4,7},{5,6},{6,5},{7,4},{8,11},{9,10},{10,... | collective-permute-start | bytes 786440 | tf_op jit(solution)/shard_map/ppermute | solution.py:45
  71.7 8.2 %collective-permute-start.16 = (f32[8,64,128]{2,1,0:T(8,128)S(1)}, f32[8,64,128]{2,1,0:T(8,128)S(1)}, u32[]{:S(2)}, u32[]{:S(2)}) collective-permute-start(f32[8,64,128]{2,1,0:T(8,128)S(1)} %get-tuple-element.72), channel_id=1, source_target_pairs={{0,64},{8,72},{16,80},{24,88},{32,96},{40,104},{48,112},{56,120},{... | collective-permute-start | bytes 786440 | tf_op jit(solution)/shard_map/ppermute | solution.py:45
  73.5 13.2 %collective-permute-start.19 = (f32[8,64,128]{2,1,0:T(8,128)S(1)}, f32[8,64,128]{2,1,0:T(8,128)S(1)}, u32[]{:S(2)}, u32[]{:S(2)}) collective-permute-start(f32[8,64,128]{2,1,0:T(8,128)S(1)} %far.1.refs_0_), channel_id=1, source_target_pairs={{0,4},{1,5},{2,6},{3,7},{4,0},{5,1},{6,2},{7,3},{8,12},{9,13},{10,... | collective-permute-start | bytes 786440 | tf_op jit(solution)/shard_map/ppermute | solution.py:45
  78.8 7.7 %collective-permute-start.20 = (f32[8,64,128]{2,1,0:T(8,128)S(1)}, f32[8,64,128]{2,1,0:T(8,128)S(1)}, u32[]{:S(2)}, u32[]{:S(2)}) collective-permute-start(f32[8,64,128]{2,1,0:T(8,128)S(1)} %mix_3_2.3.refs_0_), channel_id=1, source_target_pairs={{0,3},{1,2},{2,1},{3,0},{4,7},{5,6},{6,5},{7,4},{8,11},{9,10},{10,... | collective-permute-start | bytes 786440 | tf_op jit(solution)/shard_map/ppermute | solution.py:45
  80.2 6.5 %collective-permute-start.18 = (f32[8,64,128]{2,1,0:T(8,128)S(1)}, f32[8,64,128]{2,1,0:T(8,128)S(1)}, u32[]{:S(2)}, u32[]{:S(2)}) collective-permute-start(f32[8,64,128]{2,1,0:T(8,128)S(1)} %mix_3_3.2.refs_0_), channel_id=1, source_target_pairs={{0,1},{1,0},{2,3},{3,2},{4,5},{5,4},{6,7},{7,6},{8,9},{9,8},{10,11... | collective-permute-start | bytes 786440 | tf_op jit(solution)/shard_map/ppermute | solution.py:45

commit v6 on v5

--- a/solution.py
+++ b/solution.py
@@ -29,13 +29,11 @@
     ('mix', 2, 2, ('sent',)),
     ('mix', 1, 3, ('sent', 'kept')),
     ('mix', 2, 2, ('kept',)),
-    ('mix', 3, 2, ('kept',)),
+    ('mix', 3, 2, ('kept_sent',)),
     ('mix', 2, 3, ('sent', 'kept')),
     ('far',),
-    ('mix', 3, 2, ('sent',)),
-    ('mix', 3, 3, ('sent',)),
-    ('mix', 3, 3, ('kept',)),
     ('targets',),
+    ('mix', 3, 3, ('sent', 'kept')),
     ('end',),
 ]
 

time: 89.5 us -> 89.5 us (level)
  waiting for transfers between devices: 31.4 us -> 32.6 us
    ppermute x21 -> x20, waiting for transfers between devices: 31.4 us -> 32.6 us  [swap(): return lax.ppermute(block, axis, [(at, at ^ mask) for at in range(count)])]
    ppermute x21 -> x20, starting transfers between devices: 35.9 us -> 35.1 us  [swap(): return lax.ppermute(block, axis, [(at, at ^ mask) for at in range(count)])]
    pallas_call x26 -> x24, Pallas kernels: 20.2 us -> 19.8 us  [run(): pl.pallas_call(functools.partial(kernel, body=body, first=len(token), ins...]
  transfers between devices with their start and end apart: 21 -> 20, of which waited for: 10 -> 9; matrix products, arithmetic and copies ran while one was open for 0% -> 0% of each run, Pallas kernels for 18% -> 18%
where the time goes in v6:
time: 89.5 us; the launch traced here: 87.8 us
  starting transfers between devices  35.1 us (39%)
  waiting for transfers between devices  32.6 us (36%)
  Pallas kernels  19.8 us (22%)
    ppermute x20, starting transfers between devices, swap(): return lax.ppermute(block, axis, [(at, at ^ mask) for at in range(count)])  35.1 us
    ppermute x20, waiting for transfers between devices, swap(): return lax.ppermute(block, axis, [(at, at ^ mask) for at in range(count)])  32.6 us
    pallas_call x24, Pallas kernels, run(): pl.pallas_call(functools.partial(kernel, body=body, first=len(token), ins...  19.8 us
  transfers between devices with their start and end apart: 20, of which 9 were waited for; matrix products, arithmetic and copies ran while one was open for 0% of the time, Pallas kernels for 18%

profile of v6, /device:TPU:8, one launch (start us, length us, event | category | flops | bytes accessed | tf_op | source)
XLA Modules:
  0.0 87.8 jit_solution(12357915001366405633)
XLA Ops:
  0.0 1.8 %first.1 = (f32[8,64,128]{2,1,0:T(8,128)S(1)}, f32[8,64,128]{2,1,0:T(8,128)S(1)}) custom-call(bf16[4,64,64,256]{3,2,1,0:T(8,128)(2,1)} %bitcast.3, bf16[16,4,128,128]{3,2,1,0:T(8,128)(2,1)} %bitcast.7, bf16[16,4,64,256]{3,2,1,0:T(8,128)(2,1)} %bitcast.9), custom_call_target="tpu_custom_call" | custom-call | flops 8589934592 | bytes 1048576 | tf_op jit(solution)/shard_map/first/pallas_call | solution.py:253
  1.9 1.6 %tables.1 = (s32[4,64,128]{2,1,0:T(8,128)S(1)}, bf16[64,64,256]{2,1,0:T(8,128)(2,1)S(1)}) custom-call(f32[8,64,128]{2,1,0:T(8,128)S(1)} %get-tuple-element.41.refs_0_.refs_3_, bf16[4,64,64,256]{3,2,1,0:T(8,128)(2,1)} %bitcast.4, s32[4,1,1,64]{3,2,1,0:T(1,128)} %refs_2_.1), custom_call_target="tpu_custom_call" | custom-call | flops 8589934592 | bytes 1048576 | tf_op jit(solution)/shard_map/tables/pallas_call | solution.py:253
  4.1 2.0 %collective-permute-start.2 = (f32[8,64,128]{2,1,0:T(8,128)S(1)}, f32[8,64,128]{2,1,0:T(8,128)S(1)}, u32[]{:S(2)}, u32[]{:S(2)}) collective-permute-start(f32[8,64,128]{2,1,0:T(8,128)S(1)} %get-tuple-element.51), channel_id=1, source_target_pairs={{0,16},{8,24},{16,0},{24,8},{32,48},{40,56},{48,32},{56,40},{64,80... | collective-permute-start | bytes 786440 | tf_op jit(solution)/shard_map/ppermute | solution.py:43
  6.1 2.9 %rest.1 = (f32[24,64,128]{2,1,0:T(8,128)S(1)}, f32[24,64,128]{2,1,0:T(8,128)S(1)}, bf16[64,64,256]{2,1,0:T(8,128)(2,1)S(1)}) custom-call(f32[8,64,128]{2,1,0:T(8,128)S(1)} %get-tuple-element.45.refs_0_.refs_3_, bf16[16,4,128,128]{3,2,1,0:T(8,128)(2,1)} %bitcast.8, bf16[16,4,64,256]{3,2,1,0:T(8,128)(2,1)} %bitcast.10, bf16[4,64,64,256]{3,2,1,0:T(8,128)(2,1)} %bitcast.5), custom_call_target="tpu_custom_call" | custom-call | flops 8589934592 | bytes 1048576 | tf_op jit(solution)/shard_map/rest/pallas_call | solution.py:253
  9.4 2.2 %load.1 = (bf16[64,64,256]{2,1,0:T(8,128)(2,1)S(1)}, bf16[64,64,256]{2,1,0:T(8,128)(2,1)S(1)}) custom-call(f32[24,64,128]{2,1,0:T(8,128)S(1)} %get-tuple-element.46.refs_0_.refs_3_, bf16[4,64,64,256]{3,2,1,0:T(8,128)(2,1)} %bitcast.6), custom_call_target="tpu_custom_call" | custom-call | flops 8589934592 | bytes 1048576 | tf_op jit(solution)/shard_map/load/pallas_call | solution.py:253
  13.7 3.4 %collective-permute-start.4 = (f32[8,64,128]{2,1,0:T(8,128)S(1)}, f32[8,64,128]{2,1,0:T(8,128)S(1)}, u32[]{:S(2)}, u32[]{:S(2)}) collective-permute-start(f32[8,64,128]{2,1,0:T(8,128)S(1)} %get-tuple-element.57), channel_id=1, source_target_pairs={{0,32},{8,40},{16,48},{24,56},{32,0},{40,8},{48,16},{56,24},{64,96... | collective-permute-start | bytes 786440 | tf_op jit(solution)/shard_map/ppermute | solution.py:43
  17.0 9.4 %collective-permute-done.3.refs_4_ = f32[8,64,128]{2,1,0:T(8,128)S(1)} collective-permute-done((f32[8,64,128]{2,1,0:T(8,128)S(1)}, f32[8,64,128]{2,1,0:T(8,128)S(1)}, u32[]{:S(2)}, u32[]{:S(2)}) %collective-permute-start.3) | collective-permute-done | bytes 262176 | tf_op jit(solution)/shard_map/ppermute | solution.py:43
  28.3 8.7 %collective-permute-start.7 = (f32[8,64,128]{2,1,0:T(8,128)S(1)}, f32[8,64,128]{2,1,0:T(8,128)S(1)}, u32[]{:S(2)}, u32[]{:S(2)}) collective-permute-start(f32[8,64,128]{2,1,0:T(8,128)S(1)} %get-tuple-element.64), channel_id=1, source_target_pairs={{0,64},{8,72},{16,80},{24,88},{32,96},{40,104},{48,112},{56,120},{... | collective-permute-start | bytes 786440 | tf_op jit(solution)/shard_map/ppermute | solution.py:43
  37.1 4.0 %collective-permute-done.5.refs_4_ = f32[8,64,128]{2,1,0:T(8,128)S(1)} collective-permute-done((f32[8,64,128]{2,1,0:T(8,128)S(1)}, f32[8,64,128]{2,1,0:T(8,128)S(1)}, u32[]{:S(2)}, u32[]{:S(2)}) %collective-permute-start.5) | collective-permute-done | bytes 262176 | tf_op jit(solution)/shard_map/ppermute | solution.py:43
  43.4 2.9 %collective-permute-start.9 = (f32[16,64,128]{2,1,0:T(8,128)S(1)}, f32[16,64,128]{2,1,0:T(8,128)S(1)}, u32[]{:S(2)}, u32[]{:S(2)}) collective-permute-start(f32[16,64,128]{2,1,0:T(8,128)S(1)} %mix_3_0.1.refs_0_), channel_id=1, source_target_pairs={{0,3},{1,2},{2,1},{3,0},{4,7},{5,6},{6,5},{7,4},{8,11},{9,10},{10,... | collective-permute-start | bytes 1572872 | tf_op jit(solution)/shard_map/ppermute | solution.py:43
  46.7 1.7 %collective-permute-start.10 = (f32[4,64,128]{2,1,0:T(8,128)S(1)}, f32[4,64,128]{2,1,0:T(8,128)S(1)}, u32[]{:S(2)}, u32[]{:S(2)}) collective-permute-start(f32[4,64,128]{2,1,0:T(8,128)S(1)} %get-tuple-element.67), channel_id=1, source_target_pairs={{0,32},{8,40},{16,48},{24,56},{32,0},{40,8},{48,16},{56,24},{64,96... | collective-permute-start | bytes 393224 | tf_op jit(solution)/shard_map/ppermute | solution.py:43
  48.4 1.2 %collective-permute-start.12 = (f32[4,64,128]{2,1,0:T(8,128)S(1)}, f32[4,64,128]{2,1,0:T(8,128)S(1)}, u32[]{:S(2)}, u32[]{:S(2)}) collective-permute-start(f32[4,64,128]{2,1,0:T(8,128)S(1)} %get-tuple-element.70), channel_id=1, source_target_pairs={{0,32},{8,40},{16,48},{24,56},{32,0},{40,8},{48,16},{56,24},{64,96... | collective-permute-start | bytes 393224 | tf_op jit(solution)/shard_map/ppermute | solution.py:43
  49.6 1.3 %collective-permute-start.11 = (f32[8,64,128]{2,1,0:T(8,128)S(1)}, f32[8,64,128]{2,1,0:T(8,128)S(1)}, u32[]{:S(2)}, u32[]{:S(2)}) collective-permute-start(f32[8,64,128]{2,1,0:T(8,128)S(1)} %get-tuple-element.68), channel_id=1, source_target_pairs={{0,16},{8,24},{16,0},{24,8},{32,48},{40,56},{48,32},{56,40},{64,80... | collective-permute-start | bytes 786440 | tf_op jit(solution)/shard_map/ppermute | solution.py:43
  50.9 1.7 %collective-permute-done.8.refs_4_ = f32[8,64,128]{2,1,0:T(8,128)S(1)} collective-permute-done((f32[8,64,128]{2,1,0:T(8,128)S(1)}, f32[8,64,128]{2,1,0:T(8,128)S(1)}, u32[]{:S(2)}, u32[]{:S(2)}) %collective-permute-start.8) | collective-permute-done | bytes 262176 | tf_op jit(solution)/shard_map/ppermute | solution.py:43
  52.6 4.1 %collective-permute-done.9.refs_5_ = f32[16,64,128]{2,1,0:T(8,128)S(1)} collective-permute-done((f32[16,64,128]{2,1,0:T(8,128)S(1)}, f32[16,64,128]{2,1,0:T(8,128)S(1)}, u32[]{:S(2)}, u32[]{:S(2)}) %collective-permute-start.9) | collective-permute-done | bytes 524320 | tf_op jit(solution)/shard_map/ppermute | solution.py:43
  57.7 1.7 %collective-permute-start.13 = (f32[8,64,128]{2,1,0:T(8,128)S(1)}, f32[8,64,128]{2,1,0:T(8,128)S(1)}, u32[]{:S(2)}, u32[]{:S(2)}) collective-permute-start(f32[8,64,128]{2,1,0:T(8,128)S(1)} %mix_2_2.2.refs_0_), channel_id=1, source_target_pairs={{0,64},{8,72},{16,80},{24,88},{32,96},{40,104},{48,112},{56,120},{... | collective-permute-start | bytes 786440 | tf_op jit(solution)/shard_map/ppermute | solution.py:43
  62.3 1.9 %collective-permute-done.13.refs_4_ = f32[8,64,128]{2,1,0:T(8,128)S(1)} collective-permute-done((f32[8,64,128]{2,1,0:T(8,128)S(1)}, f32[8,64,128]{2,1,0:T(8,128)S(1)}, u32[]{:S(2)}, u32[]{:S(2)}) %collective-permute-start.13) | collective-permute-done | bytes 262176 | tf_op jit(solution)/shard_map/ppermute | solution.py:43
  64.7 2.8 %collective-permute-start.17 = (f32[16,64,128]{2,1,0:T(8,128)S(1)}, f32[16,64,128]{2,1,0:T(8,128)S(1)}, u32[]{:S(2)}, u32[]{:S(2)}) collective-permute-start(f32[16,64,128]{2,1,0:T(8,128)S(1)} %mix_3_2.1.refs_0_), channel_id=1, source_target_pairs={{0,3},{1,2},{2,1},{3,0},{4,7},{5,6},{6,5},{7,4},{8,11},{9,10},{10,... | collective-permute-start | bytes 1572872 | tf_op jit(solution)/shard_map/ppermute | solution.py:43
  67.5 3.6 %collective-permute-done.14.refs_4_ = f32[8,64,128]{2,1,0:T(8,128)S(1)} collective-permute-done((f32[8,64,128]{2,1,0:T(8,128)S(1)}, f32[8,64,128]{2,1,0:T(8,128)S(1)}, u32[]{:S(2)}, u32[]{:S(2)}) %collective-permute-start.14) | collective-permute-done | bytes 262176 | tf_op jit(solution)/shard_map/ppermute | solution.py:43
  71.7 1.8 %collective-permute-start.16 = (f32[8,64,128]{2,1,0:T(8,128)S(1)}, f32[8,64,128]{2,1,0:T(8,128)S(1)}, u32[]{:S(2)}, u32[]{:S(2)}) collective-permute-start(f32[8,64,128]{2,1,0:T(8,128)S(1)} %get-tuple-element.74), channel_id=1, source_target_pairs={{0,64},{8,72},{16,80},{24,88},{32,96},{40,104},{48,112},{56,120},{... | collective-permute-start | bytes 786440 | tf_op jit(solution)/shard_map/ppermute | solution.py:43
  73.5 4.9 %collective-permute-start.19 = (f32[8,64,128]{2,1,0:T(8,128)S(1)}, f32[8,64,128]{2,1,0:T(8,128)S(1)}, u32[]{:S(2)}, u32[]{:S(2)}) collective-permute-start(f32[8,64,128]{2,1,0:T(8,128)S(1)} %far.1.refs_0_), channel_id=1, source_target_pairs={{0,4},{1,5},{2,6},{3,7},{4,0},{5,1},{6,2},{7,3},{8,12},{9,13},{10,... | collective-permute-start | bytes 786440 | tf_op jit(solution)/shard_map/ppermute | solution.py:43
  78.4 1.0 %targets.1.refs_0_.refs_1_ = bf16[8,128,128]{2,1,0:T(8,128)(2,1)S(1)} custom-call(f32[8,64,128]{2,1,0:T(8,128)S(1)} %far.1.refs_0_, bf16[1,64,128,128]{3,2,1,0:T(8,128)(2,1)} %refs_1_.1), custom_call_target="tpu_custom_call" | custom-call | flops 8589934592 | bytes 1048576 | tf_op jit(solution)/shard_map/targets/pallas_call | solution.py:253
  80.3 6.4 %collective-permute-done.19.refs_4_ = f32[8,64,128]{2,1,0:T(8,128)S(1)} collective-permute-done((f32[8,64,128]{2,1,0:T(8,128)S(1)}, f32[8,64,128]{2,1,0:T(8,128)S(1)}, u32[]{:S(2)}, u32[]{:S(2)}) %collective-permute-start.19) | collective-permute-done | bytes 262176 | tf_op jit(solution)/shard_map/ppermute | solution.py:43
  86.7 1.1 %end.1 = bf16[1024,128]{1,0:T(8,128)(2,1)} custom-call(f32[8,64,128]{2,1,0:T(8,128)S(1)} %get-tuple-element.75.refs_0_.refs_2_, bf16[8,128,128]{2,1,0:T(8,128)(2,1)S(1)} %targets.1.refs_0_.refs_1_, f32[8,64,128]{2,1,0:T(8,128)S(1)} %get-tuple-element.75.refs_0_.refs_2_, f32[8,64,128]{2,1,0:T(8,128)S(1)} %collective-permute-done.18.refs_3_, ...), custom_call_target="tpu_custom_call" | custom-call | flops 8589934592 | bytes 1048576 | tf_op jit(solution)/shard_map/end/pallas_call | solution.py:253
  (40 shorter events, 13.4 us)
Async XLA Ops:
  1.8 1.7 %collective-permute-start = (f32[8,64,128]{2,1,0:T(8,128)S(1)}, f32[8,64,128]{2,1,0:T(8,128)S(1)}, u32[]{:S(2)}, u32[]{:S(2)}) collective-permute-start(f32[8,64,128]{2,1,0:T(8,128)S(1)} %get-tuple-element.44), channel_id=1, source_target_pairs={{0,8},{8,0},{16,24},{24,16},{32,40},{40,32},{48,56},{56,48},{64,72... | collective-permute-start | bytes 786440 | tf_op jit(solution)/shard_map/ppermute | solution.py:43
  4.1 9.0 %collective-permute-start.2 = (f32[8,64,128]{2,1,0:T(8,128)S(1)}, f32[8,64,128]{2,1,0:T(8,128)S(1)}, u32[]{:S(2)}, u32[]{:S(2)}) collective-permute-start(f32[8,64,128]{2,1,0:T(8,128)S(1)} %get-tuple-element.51), channel_id=1, source_target_pairs={{0,16},{8,24},{16,0},{24,8},{32,48},{40,56},{48,32},{56,40},{64,80... | collective-permute-start | bytes 786440 | tf_op jit(solution)/shard_map/ppermute | solution.py:43
  9.1 2.5 %collective-permute-start.1 = (f32[24,64,128]{2,1,0:T(8,128)S(1)}, f32[24,64,128]{2,1,0:T(8,128)S(1)}, u32[]{:S(2)}, u32[]{:S(2)}) collective-permute-start(f32[24,64,128]{2,1,0:T(8,128)S(1)} %get-tuple-element.48), channel_id=1, source_target_pairs={{0,8},{8,0},{16,24},{24,16},{32,40},{40,32},{48,56},{56,48},{64,72... | collective-permute-start | bytes 2359304 | tf_op jit(solution)/shard_map/ppermute | solution.py:43
  12.2 14.2 %collective-permute-start.3 = (f32[8,64,128]{2,1,0:T(8,128)S(1)}, f32[8,64,128]{2,1,0:T(8,128)S(1)}, u32[]{:S(2)}, u32[]{:S(2)}) collective-permute-start(f32[8,64,128]{2,1,0:T(8,128)S(1)} %get-tuple-element.53), channel_id=1, source_target_pairs={{0,16},{8,24},{16,0},{24,8},{32,48},{40,56},{48,32},{56,40},{64,80... | collective-permute-start | bytes 786440 | tf_op jit(solution)/shard_map/ppermute | solution.py:43
  13.7 14.1 %collective-permute-start.4 = (f32[8,64,128]{2,1,0:T(8,128)S(1)}, f32[8,64,128]{2,1,0:T(8,128)S(1)}, u32[]{:S(2)}, u32[]{:S(2)}) collective-permute-start(f32[8,64,128]{2,1,0:T(8,128)S(1)} %get-tuple-element.57), channel_id=1, source_target_pairs={{0,32},{8,40},{16,48},{24,56},{32,0},{40,8},{48,16},{56,24},{64,96... | collective-permute-start | bytes 786440 | tf_op jit(solution)/shard_map/ppermute | solution.py:43
  27.0 15.2 %collective-permute-start.6 = (f32[8,64,128]{2,1,0:T(8,128)S(1)}, f32[8,64,128]{2,1,0:T(8,128)S(1)}, u32[]{:S(2)}, u32[]{:S(2)}) collective-permute-start(f32[8,64,128]{2,1,0:T(8,128)S(1)} %get-tuple-element.62), channel_id=1, source_target_pairs={{0,32},{8,40},{16,48},{24,56},{32,0},{40,8},{48,16},{56,24},{64,96... | collective-permute-start | bytes 786440 | tf_op jit(solution)/shard_map/ppermute | solution.py:43
  27.7 13.4 %collective-permute-start.5 = (f32[8,64,128]{2,1,0:T(8,128)S(1)}, f32[8,64,128]{2,1,0:T(8,128)S(1)}, u32[]{:S(2)}, u32[]{:S(2)}) collective-permute-start(f32[8,64,128]{2,1,0:T(8,128)S(1)} %get-tuple-element.59), channel_id=1, source_target_pairs={{0,16},{8,24},{16,0},{24,8},{32,48},{40,56},{48,32},{56,40},{64,80... | collective-permute-start | bytes 786440 | tf_op jit(solution)/shard_map/ppermute | solution.py:43
  28.3 14.4 %collective-permute-start.7 = (f32[8,64,128]{2,1,0:T(8,128)S(1)}, f32[8,64,128]{2,1,0:T(8,128)S(1)}, u32[]{:S(2)}, u32[]{:S(2)}) collective-permute-start(f32[8,64,128]{2,1,0:T(8,128)S(1)} %get-tuple-element.64), channel_id=1, source_target_pairs={{0,64},{8,72},{16,80},{24,88},{32,96},{40,104},{48,112},{56,120},{... | collective-permute-start | bytes 786440 | tf_op jit(solution)/shard_map/ppermute | solution.py:43
  43.4 13.3 %collective-permute-start.9 = (f32[16,64,128]{2,1,0:T(8,128)S(1)}, f32[16,64,128]{2,1,0:T(8,128)S(1)}, u32[]{:S(2)}, u32[]{:S(2)}) collective-permute-start(f32[16,64,128]{2,1,0:T(8,128)S(1)} %mix_3_0.1.refs_0_), channel_id=1, source_target_pairs={{0,3},{1,2},{2,1},{3,0},{4,7},{5,6},{6,5},{7,4},{8,11},{9,10},{10,... | collective-permute-start | bytes 1572872 | tf_op jit(solution)/shard_map/ppermute | solution.py:43
  46.2 6.4 %collective-permute-start.8 = (f32[8,64,128]{2,1,0:T(8,128)S(1)}, f32[8,64,128]{2,1,0:T(8,128)S(1)}, u32[]{:S(2)}, u32[]{:S(2)}) collective-permute-start(f32[8,64,128]{2,1,0:T(8,128)S(1)} %get-tuple-element.65), channel_id=1, source_target_pairs={{0,64},{8,72},{16,80},{24,88},{32,96},{40,104},{48,112},{56,120},{... | collective-permute-start | bytes 786440 | tf_op jit(solution)/shard_map/ppermute | solution.py:43
  46.7 10.6 %collective-permute-start.10 = (f32[4,64,128]{2,1,0:T(8,128)S(1)}, f32[4,64,128]{2,1,0:T(8,128)S(1)}, u32[]{:S(2)}, u32[]{:S(2)}) collective-permute-start(f32[4,64,128]{2,1,0:T(8,128)S(1)} %get-tuple-element.67), channel_id=1, source_target_pairs={{0,32},{8,40},{16,48},{24,56},{32,0},{40,8},{48,16},{56,24},{64,96... | collective-permute-start | bytes 393224 | tf_op jit(solution)/shard_map/ppermute | solution.py:43
  48.4 13.5 %collective-permute-start.12 = (f32[4,64,128]{2,1,0:T(8,128)S(1)}, f32[4,64,128]{2,1,0:T(8,128)S(1)}, u32[]{:S(2)}, u32[]{:S(2)}) collective-permute-start(f32[4,64,128]{2,1,0:T(8,128)S(1)} %get-tuple-element.70), channel_id=1, source_target_pairs={{0,32},{8,40},{16,48},{24,56},{32,0},{40,8},{48,16},{56,24},{64,96... | collective-permute-start | bytes 393224 | tf_op jit(solution)/shard_map/ppermute | solution.py:43
  49.6 10.7 %collective-permute-start.11 = (f32[8,64,128]{2,1,0:T(8,128)S(1)}, f32[8,64,128]{2,1,0:T(8,128)S(1)}, u32[]{:S(2)}, u32[]{:S(2)}) collective-permute-start(f32[8,64,128]{2,1,0:T(8,128)S(1)} %get-tuple-element.68), channel_id=1, source_target_pairs={{0,16},{8,24},{16,0},{24,8},{32,48},{40,56},{48,32},{56,40},{64,80... | collective-permute-start | bytes 786440 | tf_op jit(solution)/shard_map/ppermute | solution.py:43
  57.7 6.5 %collective-permute-start.13 = (f32[8,64,128]{2,1,0:T(8,128)S(1)}, f32[8,64,128]{2,1,0:T(8,128)S(1)}, u32[]{:S(2)}, u32[]{:S(2)}) collective-permute-start(f32[8,64,128]{2,1,0:T(8,128)S(1)} %mix_2_2.2.refs_0_), channel_id=1, source_target_pairs={{0,64},{8,72},{16,80},{24,88},{32,96},{40,104},{48,112},{56,120},{... | collective-permute-start | bytes 786440 | tf_op jit(solution)/shard_map/ppermute | solution.py:43
  60.9 10.3 %collective-permute-start.14 = (f32[8,64,128]{2,1,0:T(8,128)S(1)}, f32[8,64,128]{2,1,0:T(8,128)S(1)}, u32[]{:S(2)}, u32[]{:S(2)}) collective-permute-start(f32[8,64,128]{2,1,0:T(8,128)S(1)} %get-tuple-element.71), channel_id=1, source_target_pairs={{0,32},{8,40},{16,48},{24,56},{32,0},{40,8},{48,16},{56,24},{64,96... | collective-permute-start | bytes 786440 | tf_op jit(solution)/shard_map/ppermute | solution.py:43
  61.6 11.8 %collective-permute-start.15 = (f32[8,64,128]{2,1,0:T(8,128)S(1)}, f32[8,64,128]{2,1,0:T(8,128)S(1)}, u32[]{:S(2)}, u32[]{:S(2)}) collective-permute-start(f32[8,64,128]{2,1,0:T(8,128)S(1)} %get-tuple-element.73), channel_id=1, source_target_pairs={{0,1},{1,0},{2,3},{3,2},{4,5},{5,4},{6,7},{7,6},{8,9},{9,8},{10,11... | collective-permute-start | bytes 786440 | tf_op jit(solution)/shard_map/ppermute | solution.py:43
  64.7 14.7 %collective-permute-start.17 = (f32[16,64,128]{2,1,0:T(8,128)S(1)}, f32[16,64,128]{2,1,0:T(8,128)S(1)}, u32[]{:S(2)}, u32[]{:S(2)}) collective-permute-start(f32[16,64,128]{2,1,0:T(8,128)S(1)} %mix_3_2.1.refs_0_), channel_id=1, source_target_pairs={{0,3},{1,2},{2,1},{3,0},{4,7},{5,6},{6,5},{7,4},{8,11},{9,10},{10,... | collective-permute-start | bytes 1572872 | tf_op jit(solution)/shard_map/ppermute | solution.py:43
  71.7 7.7 %collective-permute-start.16 = (f32[8,64,128]{2,1,0:T(8,128)S(1)}, f32[8,64,128]{2,1,0:T(8,128)S(1)}, u32[]{:S(2)}, u32[]{:S(2)}) collective-permute-start(f32[8,64,128]{2,1,0:T(8,128)S(1)} %get-tuple-element.74), channel_id=1, source_target_pairs={{0,64},{8,72},{16,80},{24,88},{32,96},{40,104},{48,112},{56,120},{... | collective-permute-start | bytes 786440 | tf_op jit(solution)/shard_map/ppermute | solution.py:43
  73.5 13.2 %collective-permute-start.19 = (f32[8,64,128]{2,1,0:T(8,128)S(1)}, f32[8,64,128]{2,1,0:T(8,128)S(1)}, u32[]{:S(2)}, u32[]{:S(2)}) collective-permute-start(f32[8,64,128]{2,1,0:T(8,128)S(1)} %far.1.refs_0_), channel_id=1, source_target_pairs={{0,4},{1,5},{2,6},{3,7},{4,0},{5,1},{6,2},{7,3},{8,12},{9,13},{10,... | collective-permute-start | bytes 786440 | tf_op jit(solution)/shard_map/ppermute | solution.py:43
  80.0 6.8 %collective-permute-start.18 = (f32[8,64,128]{2,1,0:T(8,128)S(1)}, f32[8,64,128]{2,1,0:T(8,128)S(1)}, u32[]{:S(2)}, u32[]{:S(2)}) collective-permute-start(f32[8,64,128]{2,1,0:T(8,128)S(1)} %get-tuple-element.76), channel_id=1, source_target_pairs={{0,1},{1,0},{2,3},{3,2},{4,5},{5,4},{6,7},{7,6},{8,9},{9,8},{10,11... | collective-permute-start | bytes 786440 | tf_op jit(solution)/shard_map/ppermute | solution.py:43
